TPU v7x, 32 devices: a whole 2x2x4 slice. The times are simulated.
32 devices in a mesh: dp: 2 (over x), seq: 16 (over z, y, core).
Axes of the slice: x: 2, y: 2, z: 4, core: 2. Of those that a mesh axis runs over, the one named last changes fastest.
Arguments:
- inputs: bfloat16 [15360, 1152], P(('dp', 'seq')), may hold values from -6 to 6
- image_ids: int32 [15360], P(('dp', 'seq')), may hold values from 0 to 19, as said below
- token_mask: int32 [15360], P(('dp', 'seq')), may hold values from 0 to 1, as said below
- cotangent: bfloat16 [15360, 1152], P(('dp', 'seq')), may hold values from -6 to 6
- w_qkv: bfloat16 [2, 1152, 3456], P(None, ('dp', 'seq')), may hold values from -0.1875 to 0.1875
- w_out: bfloat16 [2, 1152, 1152], P(None, ('dp', 'seq')), may hold values from -1.5 to 1.5
- w_up: bfloat16 [2, 1152, 4304], P(None, ('dp', 'seq')), may hold values from -0.1875 to 0.1875
- w_down: bfloat16 [2, 4304, 1152], P(None, None, ('dp', 'seq')), may hold values from -0.09375 to 0.09375
- norm_gains: bfloat16 [2, 2, 1152], P(None, None, ('dp', 'seq')), may hold values from 0.5 to 1.5
- bias_rows: bfloat16 [2, 6, 1152], P(None, None, ('dp', 'seq')), may hold values from -1.1953125 to 1.1953125
- up_bias: bfloat16 [2, 4304], replicated, may hold values from -1.1953125 to 1.1953125
- first_qkv: float32 [2, 1152, 3456], P(None, ('dp', 'seq')), may hold values from -160 to 160
- first_out: float32 [2, 1152, 1152], P(None, ('dp', 'seq')), may hold values from -160 to 160
- first_up: float32 [2, 1152, 4304], P(None, ('dp', 'seq')), may hold values from -160 to 160
- first_down: float32 [2, 4304, 1152], P(None, None, ('dp', 'seq')), may hold values from -160 to 160
- first_gains: float32 [2, 2, 1152], P(None, None, ('dp', 'seq')), may hold values from -160 to 160
- first_bias: float32 [2, 6, 1152], P(None, None, ('dp', 'seq')), may hold values from -160 to 160
- first_upbias: float32 [2, 4304], replicated, may hold values from -160 to 160
- second_qkv: float32 [2, 1152, 3456], P(None, ('dp', 'seq')), may hold values from 1000 to 10000
- second_out: float32 [2, 1152, 1152], P(None, ('dp', 'seq')), may hold values from 1000 to 10000
- second_up: float32 [2, 1152, 4304], P(None, ('dp', 'seq')), may hold values from 1000 to 10000
- second_down: float32 [2, 4304, 1152], P(None, None, ('dp', 'seq')), may hold values from 1000 to 10000
- second_gains: float32 [2, 2, 1152], P(None, None, ('dp', 'seq')), may hold values from 1000 to 10000
- second_bias: float32 [2, 6, 1152], P(None, None, ('dp', 'seq')), may hold values from 245760 to 3932160
- second_upbias: float32 [2, 4304], replicated, may hold values from 1000 to 10000
Outputs:
- block_out: float32 [15360, 1152], P(('dp', 'seq'))
- input_grad: float32 [15360, 1152], P(('dp', 'seq'))
- grad_qkv: float32 [2, 1152, 3456], P(None, ('dp', 'seq'))
- grad_out: float32 [2, 1152, 1152], P(None, ('dp', 'seq'))
- grad_up: float32 [2, 1152, 4304], P(None, ('dp', 'seq'))
- grad_down: float32 [2, 4304, 1152], P(None, None, ('dp', 'seq'))
- grad_gains: float32 [2, 2, 1152], P(None, None, ('dp', 'seq'))
- grad_bias: float32 [2, 6, 1152], P(None, None, ('dp', 'seq'))
- grad_upbias: float32 [2, 4304], replicated
- new_first_qkv: float32 [2, 1152, 3456], P(None, ('dp', 'seq'))
- new_first_out: float32 [2, 1152, 1152], P(None, ('dp', 'seq'))
- new_first_up: float32 [2, 1152, 4304], P(None, ('dp', 'seq'))
- new_first_down: float32 [2, 4304, 1152], P(None, None, ('dp', 'seq'))
- new_first_gains: float32 [2, 2, 1152], P(None, None, ('dp', 'seq'))
- new_first_bias: float32 [2, 6, 1152], P(None, None, ('dp', 'seq'))
- new_first_upbias: float32 [2, 4304], replicated
- new_second_qkv: float32 [2, 1152, 3456], P(None, ('dp', 'seq'))
- new_second_out: float32 [2, 1152, 1152], P(None, ('dp', 'seq'))
- new_second_up: float32 [2, 1152, 4304], P(None, ('dp', 'seq'))
- new_second_down: float32 [2, 4304, 1152], P(None, None, ('dp', 'seq'))
- new_second_gains: float32 [2, 2, 1152], P(None, None, ('dp', 'seq'))
- new_second_bias: float32 [2, 6, 1152], P(None, None, ('dp', 'seq'))
- new_second_upbias: float32 [2, 4304], replicated
- step_qkv: float32 [2, 1152, 3456], P(None, ('dp', 'seq'))
- step_out: float32 [2, 1152, 1152], P(None, ('dp', 'seq'))
- step_up: float32 [2, 1152, 4304], P(None, ('dp', 'seq'))
- step_down: float32 [2, 4304, 1152], P(None, None, ('dp', 'seq'))
- step_gains: float32 [2, 2, 1152], P(None, None, ('dp', 'seq'))
- step_bias: float32 [2, 6, 1152], P(None, None, ('dp', 'seq'))
- step_upbias: float32 [2, 4304], replicated
Inputs may be any that keep to these rules, and one draw needn't show every extreme that they name: `image_ids`: group g (tokens g * 7680 to (g + 1) * 7680 - 1) holds images g * 10 to (g + 1) * 10 - 1 in rising order; the valid tokens of each image are one run of 729 consecutive positions, starting with the group's first token for its first image; padding tokens follow an image and carry its id. `token_mask`: each group has 390 padding tokens.
All inputs are finite; a program needn't handle non-finite values.
Results may differ from a plain program's by a relative error of at most 0.012.
Values may be sent and summed in bfloat16 or wider, within the bound.
A program may use at most 448 MiB of HBM per device.

v0:
```python
import math

import jax
import jax.numpy as jnp
from jax import lax
from jax.sharding import PartitionSpec as P

HEADS = 16
IMG = 729
STEP = 8


eps_norm = 1e-06
beta_first = 0.9
beta_second = 0.95
learn_rate = 0.025
weight_decay = 0.1
eps_adam = 1e-08
masked_score = -1e30


def from_behind(array, axis, by):
    devices = lax.axis_size(axis)
    pairs = [(i, i + by) for i in range(devices) if 0 <= i + by < devices]
    return lax.ppermute(array, axis, pairs)


def matmul(left_op, right_op):
    return jnp.dot(left_op, right_op, preferred_element_type=jnp.float32)


def inner_rows(left_op, right_op):
    return lax.dot_general(
        left_op, right_op, (((0,), (0,)), ((), ())), preferred_element_type=jnp.float32
    )


def inner_cols(left_op, right_op):
    return lax.dot_general(
        left_op, right_op, (((1,), (1,)), ((), ())), preferred_element_type=jnp.float32
    )


def column_sum(source):
    return jnp.sum(source.astype(jnp.float32), axis=0)


def norm_forward(source, gain_row, shift_row):
    row_mean = jnp.mean(source, axis=-1, keepdims=True)
    centred = source - row_mean
    variance = jnp.mean(centred * centred, axis=-1, keepdims=True)
    inv_scale = lax.rsqrt(variance + eps_norm)
    unit_rows = centred * inv_scale
    return (unit_rows * gain_row + shift_row, unit_rows, inv_scale)


def norm_backward(gradient, unit_rows, inv_scale, gain_row):
    scaled = gradient * gain_row
    grad_in = inv_scale * (
        scaled
        - jnp.mean(scaled, axis=-1, keepdims=True)
        - unit_rows * jnp.mean(scaled * unit_rows, axis=-1, keepdims=True)
    )
    return (grad_in, jnp.sum(gradient * unit_rows, axis=0), jnp.sum(gradient, axis=0))


def gelu_tanh(source):
    return jax.nn.gelu(source, approximate=True)


def adam_step(weight_now, gradient, first_old, second_old):
    first_new = beta_first * first_old + (1.0 - beta_first) * gradient
    second_new = beta_second * second_old + (1.0 - beta_second) * gradient * gradient
    first_hat = first_new / (1.0 - beta_first**STEP)
    second_hat = second_new / (1.0 - beta_second**STEP)
    update = -learn_rate * (
        first_hat / (jnp.sqrt(second_hat) + eps_adam)
        + weight_decay * weight_now.astype(jnp.float32)
    )
    return (first_new, second_new, update)


def per_device(
    inputs,
    image_ids,
    token_mask,
    cotangent,
    w_qkv,
    w_out,
    w_up,
    w_down,
    norm_gains,
    bias_rows,
    up_bias,
    first_qkv,
    first_out,
    first_up,
    first_down,
    first_gains,
    first_bias,
    first_upbias,
    second_qkv,
    second_out,
    second_up,
    second_down,
    second_gains,
    second_bias,
    second_upbias,
):
    tok_rows = inputs.shape[0]
    model_width = inputs.shape[1]
    head_count = HEADS
    head_size = model_width // head_count
    group_tok = tok_rows * lax.axis_size("seq")
    spare_count = group_tok - group_tok // IMG * IMG
    margin = IMG - 1 + spare_count
    reach_hops = (margin + tok_rows - 1) // tok_rows
    window_len = tok_rows + 2 * margin
    window_start = reach_hops * tok_rows - margin
    padded_len = (2 * reach_hops + 1) * tok_rows
    score_scale = 1.0 / math.sqrt(head_size)
    layer_count = w_qkv.shape[0]
    key_code = jnp.where(token_mask > 0, image_ids + 1, 0)
    code_blocks = []
    for offset in range(-reach_hops, reach_hops + 1):
        if offset == 0:
            code_blocks.append(key_code)
        else:
            code_blocks.append(from_behind(key_code, "seq", -offset))
    window_code = jnp.concatenate(code_blocks)[window_start : window_start + window_len]
    diagonal = jnp.arange(tok_rows)[:, None] + margin == jnp.arange(window_len)[None, :]
    allowed = ((image_ids + 1)[:, None] == window_code[None, :]) | diagonal

    def fetch_forward(key_value, offset):
        return from_behind(key_value, "seq", -offset)

    def fetch_again(key_value, offset):
        return from_behind(key_value, "seq", -offset)

    def neighbour_window(key_value, fetcher):
        blocks = []
        for offset in range(-reach_hops, reach_hops + 1):
            blocks.append(key_value if offset == 0 else fetcher(key_value, offset))
        return jnp.concatenate(blocks, axis=1)[:, window_start : window_start + window_len]

    def split_heads(source):
        return source.reshape(source.shape[0], head_count, head_size).transpose(1, 0, 2)

    def merge_heads(source):
        return source.transpose(1, 0, 2).reshape(source.shape[1], model_width)

    def head_forward(packed):
        query_head, key_head, value_head = packed
        scores = jnp.where(allowed, inner_cols(query_head, key_head) * score_scale, masked_score)
        row_top = jnp.max(scores, axis=1, keepdims=True)
        powers = jnp.exp(scores - row_top)
        row_total = jnp.sum(powers, axis=1, keepdims=True)
        prob_low = (powers / row_total).astype(jnp.bfloat16)
        return (matmul(prob_low, value_head), (row_top + jnp.log(row_total))[:, 0])

    def head_backward(packed):
        query_head, key_head, value_head, grad_head, lse_head = packed
        scores = jnp.where(allowed, inner_cols(query_head, key_head) * score_scale, masked_score)
        attn_prob = jnp.exp(scores - lse_head[:, None])
        prob_low = attn_prob.astype(jnp.bfloat16)
        grad_prob = inner_cols(grad_head, value_head)
        row_inner = jnp.sum(attn_prob * grad_prob, axis=1, keepdims=True)
        grad_scores = (attn_prob * (grad_prob - row_inner)).astype(jnp.bfloat16)
        grad_query = matmul(grad_scores, key_head) * score_scale
        grad_key = inner_rows(grad_scores, query_head) * score_scale
        grad_value = inner_rows(prob_low, grad_head)
        return (grad_query, grad_key, grad_value)

    residual = inputs.astype(jnp.float32)
    kept_layers = []
    for layer_index in range(layer_count):
        weights = (
            lax.all_gather(w_qkv[layer_index], ("dp", "seq"), axis=0, tiled=True),
            lax.all_gather(w_out[layer_index], ("dp", "seq"), axis=0, tiled=True),
            lax.all_gather(w_up[layer_index], ("dp", "seq"), axis=0, tiled=True),
            lax.all_gather(w_down[layer_index], ("dp", "seq"), axis=1, tiled=True),
            lax.all_gather(norm_gains[layer_index], ("dp", "seq"), axis=1, tiled=True),
            lax.all_gather(bias_rows[layer_index], ("dp", "seq"), axis=1, tiled=True),
        )
        qkv_weight, out_weight, up_weight, down_weight = (
            weights[0],
            weights[1],
            weights[2],
            weights[3],
        )
        gain_rows = weights[4].astype(jnp.float32)
        shift_rows = weights[5].astype(jnp.float32)
        normed, unit_one, inv_one = norm_forward(residual, gain_rows[0], shift_rows[0])
        normed_low = normed.astype(jnp.bfloat16)
        projected = matmul(normed_low, qkv_weight)
        queries = (projected[:, :model_width] + shift_rows[2]).astype(jnp.bfloat16)
        key_value = jnp.stack(
            [
                projected[:, model_width : 2 * model_width],
                projected[:, 2 * model_width :] + shift_rows[3],
            ]
        ).astype(jnp.bfloat16)
        window = neighbour_window(key_value, fetch_forward)
        head_out, log_total = lax.map(
            head_forward, (split_heads(queries), split_heads(window[0]), split_heads(window[1]))
        )
        attended = merge_heads(head_out).astype(jnp.bfloat16)
        middle = residual + matmul(attended, out_weight) + shift_rows[4]
        hidden, unit_two, inv_two = norm_forward(middle, gain_rows[1], shift_rows[1])
        hidden_low = hidden.astype(jnp.bfloat16)
        pre_act = matmul(hidden_low, up_weight) + up_bias[layer_index].astype(jnp.float32)
        active = gelu_tanh(pre_act).astype(jnp.bfloat16)
        residual = middle + matmul(active, down_weight) + shift_rows[5]
        kept_layers.append(
            (
                weights,
                window,
                key_value,
                unit_one,
                inv_one,
                normed_low,
                queries,
                log_total,
                attended,
                unit_two,
                inv_two,
                hidden_low,
                pre_act,
                active,
            )
        )
    grad_res = cotangent.astype(jnp.float32)
    layer_grads = [None] * layer_count
    upbias_grads = [None] * layer_count
    for layer_index in reversed(range(layer_count)):
        (
            weights,
            window,
            key_value,
            unit_one,
            inv_one,
            normed_low,
            queries,
            log_total,
            attended,
            unit_two,
            inv_two,
            hidden_low,
            pre_act,
            active,
        ) = kept_layers[layer_index]
        weights = (
            lax.all_gather(w_qkv[layer_index], ("dp", "seq"), axis=0, tiled=True),
            lax.all_gather(w_out[layer_index], ("dp", "seq"), axis=0, tiled=True),
            lax.all_gather(w_up[layer_index], ("dp", "seq"), axis=0, tiled=True),
            lax.all_gather(w_down[layer_index], ("dp", "seq"), axis=1, tiled=True),
            lax.all_gather(norm_gains[layer_index], ("dp", "seq"), axis=1, tiled=True),
            lax.all_gather(bias_rows[layer_index], ("dp", "seq"), axis=1, tiled=True),
        )
        window = neighbour_window(key_value, fetch_again)
        qkv_weight, out_weight, up_weight, down_weight = (
            weights[0],
            weights[1],
            weights[2],
            weights[3],
        )
        gain_rows = weights[4].astype(jnp.float32)
        grad_branch = grad_res.astype(jnp.bfloat16)
        grad_downw = inner_rows(active, grad_branch)
        grad_active = inner_cols(grad_branch, down_weight)
        gelu_value, gelu_pull = jax.vjp(gelu_tanh, pre_act)
        grad_pre_low = gelu_pull(grad_active)[0].astype(jnp.bfloat16)
        grad_upw = inner_rows(hidden_low, grad_pre_low)
        grad_hidden = inner_cols(grad_pre_low, up_weight)
        back_two, gain_two, shift_two = norm_backward(grad_hidden, unit_two, inv_two, gain_rows[1])
        grad_mid = grad_res + back_two
        grad_attn = grad_mid.astype(jnp.bfloat16)
        grad_outw = inner_rows(attended, grad_attn)
        grad_attended = inner_cols(grad_attn, out_weight).astype(jnp.bfloat16)
        grad_query, grad_key, grad_value = lax.map(
            head_backward,
            (
                split_heads(queries),
                split_heads(window[0]),
                split_heads(window[1]),
                split_heads(grad_attended),
                log_total,
            ),
        )
        grad_query_low = merge_heads(grad_query).astype(jnp.bfloat16)
        grad_window = jnp.stack([merge_heads(grad_key), merge_heads(grad_value)])
        grad_window = jnp.pad(
            grad_window, ((0, 0), (window_start, padded_len - window_start - window_len), (0, 0))
        )
        grad_pair = grad_window[:, reach_hops * tok_rows : (reach_hops + 1) * tok_rows]
        for offset in range(-reach_hops, reach_hops + 1):
            if offset != 0:
                piece = grad_window[
                    :, (offset + reach_hops) * tok_rows : (offset + reach_hops + 1) * tok_rows
                ]
                grad_pair = grad_pair + from_behind(
                    piece.astype(jnp.bfloat16), "seq", offset
                ).astype(piece.dtype)
        grad_pair_low = grad_pair.astype(jnp.bfloat16)
        grad_proj = jnp.concatenate([grad_query_low, grad_pair_low[0], grad_pair_low[1]], axis=1)
        grad_qkvw = inner_rows(normed_low, grad_proj)
        grad_normed = inner_cols(grad_proj, qkv_weight)
        back_one, gain_one, shift_one = norm_backward(grad_normed, unit_one, inv_one, gain_rows[0])
        grad_res = grad_mid + back_one
        grad_gain = jnp.stack([gain_one, gain_two])
        grad_shift = jnp.stack(
            [
                shift_one,
                shift_two,
                column_sum(grad_query_low),
                column_sum(grad_pair_low[1]),
                column_sum(grad_attn),
                column_sum(grad_branch),
            ]
        )
        upbias_grads[layer_index] = column_sum(grad_pre_low)
        layer_grads[layer_index] = (
            lax.psum_scatter(grad_qkvw, ("dp", "seq"), scatter_dimension=0, tiled=True),
            lax.psum_scatter(grad_outw, ("dp", "seq"), scatter_dimension=0, tiled=True),
            lax.psum_scatter(grad_upw, ("dp", "seq"), scatter_dimension=0, tiled=True),
            lax.psum_scatter(grad_downw, ("dp", "seq"), scatter_dimension=1, tiled=True),
            lax.psum_scatter(grad_gain, ("dp", "seq"), scatter_dimension=1, tiled=True),
            lax.psum_scatter(grad_shift, ("dp", "seq"), scatter_dimension=1, tiled=True),
        )

    def stack_member(member):
        return jnp.stack([layer_grads[layer_index][member] for layer_index in range(layer_count)])

    owned = (
        stack_member(0),
        stack_member(1),
        stack_member(2),
        stack_member(3),
        stack_member(4),
        stack_member(5),
    )
    grad_upbias = lax.psum(jnp.stack(upbias_grads), ("dp", "seq"))
    grads = (owned[0], owned[1], owned[2], owned[3], owned[4], owned[5], grad_upbias)
    params = (w_qkv, w_out, w_up, w_down, norm_gains, bias_rows, up_bias)
    firsts = (first_qkv, first_out, first_up, first_down, first_gains, first_bias, first_upbias)
    seconds = (
        second_qkv,
        second_out,
        second_up,
        second_down,
        second_gains,
        second_bias,
        second_upbias,
    )
    results = [
        adam_step(params[member], grads[member], firsts[member], seconds[member])
        for member in range(7)
    ]
    return (
        (residual, grad_res)
        + grads
        + tuple((results[member][0] for member in range(7)))
        + tuple((results[member][1] for member in range(7)))
        + tuple((results[member][2] for member in range(7)))
    )


def solution(mesh):
    in_specs = (
        P(("dp", "seq"), None),
        P(("dp", "seq")),
        P(("dp", "seq")),
        P(("dp", "seq"), None),
        P(None, ("dp", "seq"), None),
        P(None, ("dp", "seq"), None),
        P(None, ("dp", "seq"), None),
        P(None, None, ("dp", "seq")),
        P(None, None, ("dp", "seq")),
        P(None, None, ("dp", "seq")),
        P(),
        P(None, ("dp", "seq"), None),
        P(None, ("dp", "seq"), None),
        P(None, ("dp", "seq"), None),
        P(None, None, ("dp", "seq")),
        P(None, None, ("dp", "seq")),
        P(None, None, ("dp", "seq")),
        P(),
        P(None, ("dp", "seq"), None),
        P(None, ("dp", "seq"), None),
        P(None, ("dp", "seq"), None),
        P(None, None, ("dp", "seq")),
        P(None, None, ("dp", "seq")),
        P(None, None, ("dp", "seq")),
        P(),
    )
    out_specs = (
        P(("dp", "seq"), None),
        P(("dp", "seq"), None),
        P(None, ("dp", "seq"), None),
        P(None, ("dp", "seq"), None),
        P(None, ("dp", "seq"), None),
        P(None, None, ("dp", "seq")),
        P(None, None, ("dp", "seq")),
        P(None, None, ("dp", "seq")),
        P(),
        P(None, ("dp", "seq"), None),
        P(None, ("dp", "seq"), None),
        P(None, ("dp", "seq"), None),
        P(None, None, ("dp", "seq")),
        P(None, None, ("dp", "seq")),
        P(None, None, ("dp", "seq")),
        P(),
        P(None, ("dp", "seq"), None),
        P(None, ("dp", "seq"), None),
        P(None, ("dp", "seq"), None),
        P(None, None, ("dp", "seq")),
        P(None, None, ("dp", "seq")),
        P(None, None, ("dp", "seq")),
        P(),
        P(None, ("dp", "seq"), None),
        P(None, ("dp", "seq"), None),
        P(None, ("dp", "seq"), None),
        P(None, None, ("dp", "seq")),
        P(None, None, ("dp", "seq")),
        P(None, None, ("dp", "seq")),
        P(),
    )
    return jax.shard_map(
        per_device, mesh=mesh, in_specs=in_specs, out_specs=out_specs, check_vma=False
    )
```

profile of v0, /device:TPU:9, one launch (start us, length us, event | category | flops | bytes accessed | tf_op | source)
XLA Modules:
  0.0 4728.5 jit_solution(5821891330639877762)
XLA Ops:
  16.8 42.3 all-gather.1
  59.8 41.2 all-gather
  121.3 19.6 slice_reduce_fusion.9
  168.7 146.7 %collective-permute-done.6 = s32[480]{0:T(512)S(1)} collective-permute-done((s32[480]{0:T(512)S(1)}, s32[480]{0:T(512)S(1)}, u32[]{:S(2)}, u32[]{:S(2)}) %collective-permute-start.6) | collective-permute-done | bytes 1952 | tf_op jit(solution)/shard_map/ppermute | solution.py:25
  315.4 69.9 %collective-permute-start.8 = (s32[480]{0:T(512)S(1)}, s32[480]{0:T(512)S(1)}, u32[]{:S(2)}, u32[]{:S(2)}) collective-permute-start(s32[480]{0:T(512)S(1)} %get-tuple-element.866), channel_id=1, source_target_pairs={{0,1},{1,2},{2,3},{3,4},{4,5},{5,6},{6,7},{7,8},{8,9},{9,10},{10,1... | collective-permute-start | bytes 5768 | tf_op jit(solution)/shard_map/ppermute | solution.py:25
  398.8 43.3 all-gather.7
  447.7 20.0 slice_reduce_fusion.1
  474.8 220.0 %all-gather.6 = bf16[1,2,1152]{1,0,2:T(2,128)(2,1)S(1)} all-gather(bf16[1,2,36]{1,0,2:T(2,128)(2,1)S(1)} %copy.403), channel_id=8, replica_groups=mesh['dp'=2,'seq'=16] {'dp','seq'}, dimensions={2}, use_global_device_ids=true | all-gather | bytes 4752 | tf_op jit(solution)/shard_map/all_gather | solution.py:182
  785.4 97.9 %while.56 = (s32[]{:T(128)}, bf16[16,480,72]{1,2,0:T(8,128)(2,1)S(1)}, f32[16,480]{1,0:T(8,128)S(1)}, bf16[16,480,72]{2,1,0:T(8,128)(2,1)}, bf16[16,2716,72]{2,1...) while((s32[]{:T(128)}, ...), condition=%wide.region_5.6_spmd.clone, body=%wide.region_2.5_spmd.clone.sunk | while | flops 389799840 | bytes 17535464 | solution.py:204
  890.1 40.5 copy.325
  930.6 40.8 copy.324
  1022.2 39.9 collective-permute-done.12
  1069.5 40.2 copy.335
  1109.7 40.2 copy.334
  1157.4 49.4 %collective-permute-done.14 = bf16[2,480,1152]{2,1,0:T(8,128)(2,1)} collective-permute-done((bf16[2,480,1152]{2,1,0:T(8,128)(2,1)}, bf16[2,480,1152]{2,1,0:T(8,128)(2,1)}, u32[]{:S(2)}, u32[]{:S(2)}) %collective-permute-start.14) | collective-permute-done | bytes 2211872 | tf_op jit(solution)/shard_map/ppermute | solution.py:25
  1267.9 97.4 %while.57 = (s32[]{:T(128)}, bf16[16,480,72]{1,2,0:T(8,128)(2,1)S(1)}, f32[16,480]{1,0:T(8,128)S(1)}, bf16[16,480,72]{2,1,0:T(8,128)(2,1)}, bf16[16,2716,72]{2,1...) while((s32[]{:T(128)}, ...), condition=%wide.region_13.14_spmd.clone, body=%wide.region_10.13_spmd.clone.sunk | while | flops 389799840 | bytes 17535464 | solution.py:204
  1429.1 213.7 %while.58 = (s32[]{:T(128)}, bf16[16,480,72]{1,2,0:T(8,128)(2,1)S(1)}, f32[16,2716,72]{1,2,0:T(8,128)}, f32[16,2716,72]{1,2,0:T(8,128)}, bf16[16,480,72]{2,1,0:T...) while((s32[]{:T(128)}, ...), condition=%wide.region_20.21_spmd.clone, body=%wide.region_18.20_spmd.clone.sunk | while | flops 954523392 | bytes 43487608 | solution.py:280
  1688.0 37.4 collective-permute-start.23
  1791.9 94.1 %collective-permute-done.22 = bf16[2,480,1152]{2,1,0:T(8,128)(2,1)} collective-permute-done((bf16[2,480,1152]{2,1,0:T(8,128)(2,1)}, bf16[2,480,1152]{2,1,0:T(8,128)(2,1)}, u32[]{:S(2)}, u32[]{:S(2)}) %collective-permute-start.22) | collective-permute-done | bytes 2211872 | tf_op jit(solution)/shard_map/ppermute | solution.py:25
  1886.0 33.9 collective-permute-done.21
  1994.7 549.8 %fusion.245 = (f32[48,1152]{1,0:T(8,128)}, f32[40,4304]{1,0:T(8,128)}, f32[40,4304]{1,0:T(8,128)}) fusion(f32[1152,1152]{1,0:T(8,128)} %fusion.228, f32[1152,4304]{1,0:T(8,128)} %fusion.240, f32[1152,4304]{1,0:T(8,128)} %fusion.239), kind=kCustom, calls=%all-reduce-scatter.9 | all-reduce-scatter fusion | flops 12787714 | bytes 46572544
  2590.8 210.2 %while.59 = (s32[]{:T(128)}, bf16[16,480,72]{1,2,0:T(8,128)(2,1)S(1)}, f32[16,2716,72]{1,2,0:T(8,128)}, f32[16,2716,72]{1,2,0:T(8,128)}, bf16[16,480,72]{2,1,0:T...) while((s32[]{:T(128)}, ...), condition=%wide.region_27.28_spmd.clone, body=%wide.region_25.27_spmd.clone.sunk | while | flops 954523392 | bytes 43679608 | solution.py:280
  2857.2 474.7 %fusion.246 = (f32[4304,40]{0,1:T(8,128)}, f32[4304,40]{0,1:T(8,128)}) fusion(f32[4304,1152]{0,1:T(8,128)} %fusion.241, f32[4304,1152]{0,1:T(8,128)} %fusion.231), kind=kCustom, calls=%all-reduce-scatter.10 | all-reduce-scatter fusion | flops 11018241 | bytes 41042944
  3419.4 29.3 collective-permute-start.75
  3483.1 46.4 collective-permute-start.71
  3610.9 92.2 %collective-permute-done.28 = bf16[2,480,1152]{2,1,0:T(8,128)(2,1)} collective-permute-done((bf16[2,480,1152]{2,1,0:T(8,128)(2,1)}, bf16[2,480,1152]{2,1,0:T(8,128)(2,1)}, u32[]{:S(2)}, u32[]{:S(2)}) %collective-permute-start.28) | collective-permute-done | bytes 2211872 | tf_op jit(solution)/shard_map/ppermute | solution.py:25
  3703.2 23.7 collective-permute-done.27
  3744.5 527.4 %fusion.244 = (f32[48,3456]{1,0:T(8,128)}, f32[48,3456]{1,0:T(8,128)}, f32[48,1152]{1,0:T(8,128)S(1)}) fusion(f32[1152,3456]{1,0:T(8,128)} %fusion.205, f32[1152,3456]{1,0:T(8,128)} %fusion.204, f32[1152,1152]{1,0:T(8,128)} %fusion.234), kind=kCustom, calls=%all-reduce-scatter.8 | all-reduce-scatter fusion | flops 12386305 | bytes 38707200
  4362.7 161.2 %all-reduce.28.cloned.1.call-done = (f32[2,1152]{1,0:T(2,128)}, f32[2,1152]{1,0:T(2,128)}, f32[6,1152]{1,0:T(8,128)}, f32[6,1152]{1,0:T(8,128)}, f32[2,4304]{1,0:T(2,128)}) async-done(((f32[2,1152]{1,0:T(2,128)}, f32[2,1152]{1,0:T(2,128)}, f32[6,1152]{1,0:T(8,128)}, f32[6,1152]{1,0:T(8,128)}, f32[2,4304]{1,0:T(2,128)}), (f32[2,1152]{1,0:T(2,128)}, f32[2,1152]{1,0:T(2,128)}, f32[6,1152]{1,0:T(8,128)}, ...) | async-done | bytes 108176
  4610.9 19.8 collective-permute-start.31
  4637.8 37.3 concatenate.23
  4676.3 35.4 concatenate.22
  (1041 shorter events, 1692.3 us)
Async XLA Ops:
  10.3 873.0 %all-gather.23.cloned.1.call-start = ((), (), s32[]{:S(2)}) async-start(), calls=%async_computation.1 | async-start | bytes 5474304 | tf_op jit(solution)/shard_map/all_gather | solution.py:179
  11.4 878.7 %all-gather.27.cloned.1.call-start = ((), (), s32[]{:S(2)}) async-start(), calls=%async_computation.3 | async-start | bytes 20680704 | tf_op jit(solution)/shard_map/all_gather | solution.py:181
  13.4 917.2 %all-gather.25.cloned.1.call-start = ((), (), s32[]{:S(2)}) async-start(), calls=%async_computation.2 | async-start | bytes 20680704 | tf_op jit(solution)/shard_map/all_gather | solution.py:180
  15.4 979.7 %all-gather.29.cloned.1.call-start = ((), (), s32[]{:S(2)}) async-start(), calls=%async_computation.4 | async-start | bytes 16422912 | tf_op jit(solution)/shard_map/all_gather | solution.py:178
  16.0 1053.5 %all-gather.35.cloned.1.call-start = ((), (), s32[]{:S(2)}) async-start(), calls=%async_computation.7 | async-start | bytes 20680704 | tf_op jit(solution)/shard_map/all_gather | solution.py:181
  16.6 1093.1 %all-gather.33.cloned.1.call-start = ((), (), s32[]{:S(2)}) async-start(), calls=%async_computation.6 | async-start | bytes 20680704 | tf_op jit(solution)/shard_map/all_gather | solution.py:180
  153.4 314.9 %collective-permute-start = (bf16[2,480,1152]{2,1,0:T(8,128)(2,1)}, bf16[2,480,1152]{2,1,0:T(8,128)(2,1)}, u32[]{:S(2)}, u32[]{:S(2)}) collective-permute-start(bf16[2,480,1152]{2,1,0:T(8,128)(2,1)} %pad_maximum_fusion.4), channel_id=1, source_target_pairs={{0,3},{1,4},{2,5},{3,6},{4,7},{5,8},{6,9},{7,10},{8,11},{9,12},{10... | collective-permute-start | bytes 6635528 | tf_op jit(solution)/shard_map/ppermute | solution.py:25
  155.7 566.3 %collective-permute-start.1 = (bf16[2,480,1152]{2,1,0:T(8,128)(2,1)}, bf16[2,480,1152]{2,1,0:T(8,128)(2,1)}, u32[]{:S(2)}, u32[]{:S(2)}) collective-permute-start(bf16[2,480,1152]{2,1,0:T(8,128)(2,1)} %pad_maximum_fusion.4), channel_id=1, source_target_pairs={{0,2},{1,3},{2,4},{3,5},{4,6},{5,7},{6,8},{7,9},{8,10},{9,11},{10,... | collective-permute-start | bytes 6635528 | tf_op jit(solution)/shard_map/ppermute | solution.py:25
  159.1 565.0 %collective-permute-start.2 = (bf16[2,480,1152]{2,1,0:T(8,128)(2,1)}, bf16[2,480,1152]{2,1,0:T(8,128)(2,1)}, u32[]{:S(2)}, u32[]{:S(2)}) collective-permute-start(bf16[2,480,1152]{2,1,0:T(8,128)(2,1)} %pad_maximum_fusion.4), channel_id=1, source_target_pairs={{0,1},{1,2},{2,3},{3,4},{4,5},{5,6},{6,7},{7,8},{8,9},{9,10},{10,1... | collective-permute-start | bytes 6635528 | tf_op jit(solution)/shard_map/ppermute | solution.py:25
  165.4 219.9 %collective-permute-start.7 = (s32[480]{0:T(512)S(1)}, s32[480]{0:T(512)S(1)}, u32[]{:S(2)}, u32[]{:S(2)}) collective-permute-start(s32[480]{0:T(512)S(1)} %get-tuple-element.866), channel_id=1, source_target_pairs={{0,2},{1,3},{2,4},{3,5},{4,6},{5,7},{6,8},{7,9},{8,10},{9,11},{10,... | collective-permute-start | bytes 5768 | tf_op jit(solution)/shard_map/ppermute | solution.py:25
  387.3 978.1 %all-gather.31.cloned.1.call-start = ((), (), s32[]{:S(2)}) async-start(), calls=%async_computation.5 | async-start | bytes 5474304 | tf_op jit(solution)/shard_map/all_gather | solution.py:179
  442.8 283.7 %collective-permute-start.3 = (bf16[2,480,1152]{2,1,0:T(8,128)(2,1)}, bf16[2,480,1152]{2,1,0:T(8,128)(2,1)}, u32[]{:S(2)}, u32[]{:S(2)}) collective-permute-start(bf16[2,480,1152]{2,1,0:T(8,128)(2,1)} %pad_maximum_fusion.4), channel_id=1, source_target_pairs={{1,0},{2,1},{3,2},{4,3},{5,4},{6,5},{7,6},{8,7},{9,8},{10,9},{11,1... | collective-permute-start | bytes 6635528 | tf_op jit(solution)/shard_map/ppermute | solution.py:25
  444.9 283.6 %collective-permute-start.4 = (bf16[2,480,1152]{2,1,0:T(8,128)(2,1)}, bf16[2,480,1152]{2,1,0:T(8,128)(2,1)}, u32[]{:S(2)}, u32[]{:S(2)}) collective-permute-start(bf16[2,480,1152]{2,1,0:T(8,128)(2,1)} %pad_maximum_fusion.4), channel_id=1, source_target_pairs={{2,0},{3,1},{4,2},{5,3},{6,4},{7,5},{8,6},{9,7},{10,8},{11,9},{12,... | collective-permute-start | bytes 6635528 | tf_op jit(solution)/shard_map/ppermute | solution.py:25
  468.4 262.1 %collective-permute-start.5 = (bf16[2,480,1152]{2,1,0:T(8,128)(2,1)}, bf16[2,480,1152]{2,1,0:T(8,128)(2,1)}, u32[]{:S(2)}, u32[]{:S(2)}) collective-permute-start(bf16[2,480,1152]{2,1,0:T(8,128)(2,1)} %pad_maximum_fusion.4), channel_id=1, source_target_pairs={{3,0},{4,1},{5,2},{6,3},{7,4},{8,5},{9,6},{10,7},{11,8},{12,9},{13... | collective-permute-start | bytes 6635528 | tf_op jit(solution)/shard_map/ppermute | solution.py:25
  1012.4 194.4 %collective-permute-start.14 = (bf16[2,480,1152]{2,1,0:T(8,128)(2,1)}, bf16[2,480,1152]{2,1,0:T(8,128)(2,1)}, u32[]{:S(2)}, u32[]{:S(2)}) collective-permute-start(bf16[2,480,1152]{2,1,0:T(8,128)(2,1)} %pad_maximum_fusion.5), channel_id=1, source_target_pairs={{0,1},{1,2},{2,3},{3,4},{4,5},{5,6},{6,7},{7,8},{8,9},{9,10},{10,1... | collective-permute-start | bytes 6635528 | tf_op jit(solution)/shard_map/ppermute | solution.py:25
  1015.7 193.5 %collective-permute-start.15 = (bf16[2,480,1152]{2,1,0:T(8,128)(2,1)}, bf16[2,480,1152]{2,1,0:T(8,128)(2,1)}, u32[]{:S(2)}, u32[]{:S(2)}) collective-permute-start(bf16[2,480,1152]{2,1,0:T(8,128)(2,1)} %pad_maximum_fusion.5), channel_id=1, source_target_pairs={{1,0},{2,1},{3,2},{4,3},{5,4},{6,5},{7,6},{8,7},{9,8},{10,9},{11,1... | collective-permute-start | bytes 6635528 | tf_op jit(solution)/shard_map/ppermute | solution.py:25
  1018.0 193.1 %collective-permute-start.16 = (bf16[2,480,1152]{2,1,0:T(8,128)(2,1)}, bf16[2,480,1152]{2,1,0:T(8,128)(2,1)}, u32[]{:S(2)}, u32[]{:S(2)}) collective-permute-start(bf16[2,480,1152]{2,1,0:T(8,128)(2,1)} %pad_maximum_fusion.5), channel_id=1, source_target_pairs={{2,0},{3,1},{4,2},{5,3},{6,4},{7,5},{8,6},{9,7},{10,8},{11,9},{12,... | collective-permute-start | bytes 6635528 | tf_op jit(solution)/shard_map/ppermute | solution.py:25
  1064.1 3459.7 %all-reduce.28.cloned.1.call-start = ((), (), s32[]{:S(2)}) async-start(), calls=%async_computation.8 | async-start | bytes 253952
  1742.9 176.9 %collective-permute-start.21 = (bf16[2,480,1152]{2,1,0:T(8,128)(2,1)}, bf16[2,480,1152]{2,1,0:T(8,128)(2,1)}, u32[]{:S(2)}, u32[]{:S(2)}) collective-permute-start(bf16[2,480,1152]{2,1,0:T(8,128)(2,1)} %get-tuple-element.839), channel_id=1, source_target_pairs={{0,1},{1,2},{2,3},{3,4},{4,5},{5,6},{6,7},{7,8},{8,9},{9,10},{10,1... | collective-permute-start | bytes 6635528 | tf_op jit(solution)/shard_map/ppermute | solution.py:25
  1745.8 174.1 %collective-permute-start.20 = (bf16[2,480,1152]{2,1,0:T(8,128)(2,1)}, bf16[2,480,1152]{2,1,0:T(8,128)(2,1)}, u32[]{:S(2)}, u32[]{:S(2)}) collective-permute-start(bf16[2,480,1152]{2,1,0:T(8,128)(2,1)} %get-tuple-element.840), channel_id=1, source_target_pairs={{1,0},{2,1},{3,2},{4,3},{5,4},{6,5},{7,6},{8,7},{9,8},{10,9},{11,1... | collective-permute-start | bytes 6635528 | tf_op jit(solution)/shard_map/ppermute | solution.py:25
  1748.1 171.8 %collective-permute-start.19 = (bf16[2,480,1152]{2,1,0:T(8,128)(2,1)}, bf16[2,480,1152]{2,1,0:T(8,128)(2,1)}, u32[]{:S(2)}, u32[]{:S(2)}) collective-permute-start(bf16[2,480,1152]{2,1,0:T(8,128)(2,1)} %get-tuple-element.837), channel_id=1, source_target_pairs={{2,0},{3,1},{4,2},{5,3},{6,4},{7,5},{8,6},{9,7},{10,8},{11,9},{12,... | collective-permute-start | bytes 6635528 | tf_op jit(solution)/shard_map/ppermute | solution.py:25
  2546.3 791.5 %collective-permute-start.52 = (f32[48,1152]{1,0:T(8,128)}, f32[48,1152]{1,0:T(8,128)}, u32[]{:S(2)}, u32[]{:S(2)}) collective-permute-start(f32[48,1152]{1,0:T(8,128)} %get-tuple-element.778), channel_id=1, source_target_pairs={{0,7},{1,8},{2,9},{3,10},{4,11},{5,12},{6,13},{7,14},{8,15},{9,16}... | collective-permute-start | bytes 663560
  2548.5 793.9 %collective-permute-start.51 = (f32[48,1152]{1,0:T(8,128)}, f32[48,1152]{1,0:T(8,128)}, u32[]{:S(2)}, u32[]{:S(2)}) collective-permute-start(f32[48,1152]{1,0:T(8,128)} %get-tuple-element.778), channel_id=1, source_target_pairs={{0,6},{1,7},{2,8},{3,9},{4,10},{5,11},{6,12},{7,13},{8,14},{9,15},... | collective-permute-start | bytes 663560
  2558.3 787.3 %collective-permute-start.50 = (f32[48,1152]{1,0:T(8,128)}, f32[48,1152]{1,0:T(8,128)}, u32[]{:S(2)}, u32[]{:S(2)}) collective-permute-start(f32[48,1152]{1,0:T(8,128)} %get-tuple-element.778), channel_id=1, source_target_pairs={{0,5},{1,6},{2,7},{3,8},{4,9},{5,10},{6,11},{7,12},{8,13},{9,14},{... | collective-permute-start | bytes 663560
  2846.5 489.4 %collective-permute-start.53 = (f32[36,1152]{1,0:T(8,128)}, f32[36,1152]{1,0:T(8,128)}, u32[]{:S(2)}, u32[]{:S(2)}) collective-permute-start(f32[36,1152]{1,0:T(8,128)} %slice.349), channel_id=1, source_target_pairs={{0,8},{1,9},{2,10},{3,11},{4,12},{5,13},{6,14},{7,15},{8,16},{9,17... | collective-permute-start | bytes 497672
  2854.7 479.4 %collective-permute-start.69 = (f32[4,4304]{1,0:T(4,128)S(1)}, f32[4,4304]{1,0:T(4,128)S(1)}, u32[]{:S(2)}, u32[]{:S(2)}) collective-permute-start(f32[4,4304]{1,0:T(4,128)S(1)} %slice.352), channel_id=1, source_target_pairs={{0,4},{1,5},{2,6},{3,7},{4,8},{5,9},{6,10},{7,11},{8,12},{9,13},{1... | collective-permute-start | bytes 206600
  3561.9 164.9 %collective-permute-start.27 = (bf16[2,480,1152]{2,1,0:T(8,128)(2,1)}, bf16[2,480,1152]{2,1,0:T(8,128)(2,1)}, u32[]{:S(2)}, u32[]{:S(2)}) collective-permute-start(bf16[2,480,1152]{2,1,0:T(8,128)(2,1)} %get-tuple-element.833), channel_id=1, source_target_pairs={{0,1},{1,2},{2,3},{3,4},{4,5},{5,6},{6,7},{7,8},{8,9},{9,10},{10,1... | collective-permute-start | bytes 6635528 | tf_op jit(solution)/shard_map/ppermute | solution.py:25
  4334.1 200.2 %collective-permute-start.44 = (f32[48,3456]{1,0:T(8,128)}, f32[48,3456]{1,0:T(8,128)S(1)}, u32[]{:S(2)}, u32[]{:S(2)}) collective-permute-start(f32[48,3456]{1,0:T(8,128)} %get-tuple-element.772), channel_id=1, source_target_pairs={{0,7},{1,8},{2,9},{3,10},{4,11},{5,12},{6,13},{7,14},{8,15},{9,16}... | collective-permute-start | bytes 1990664
  4335.4 202.0 %collective-permute-start.43 = (f32[48,3456]{1,0:T(8,128)}, f32[48,3456]{1,0:T(8,128)S(1)}, u32[]{:S(2)}, u32[]{:S(2)}) collective-permute-start(f32[48,3456]{1,0:T(8,128)} %get-tuple-element.772), channel_id=1, source_target_pairs={{0,6},{1,7},{2,8},{3,9},{4,10},{5,11},{6,12},{7,13},{8,14},{9,15},... | collective-permute-start | bytes 1990664
  4336.8 202.9 %collective-permute-start.42 = (f32[48,3456]{1,0:T(8,128)}, f32[48,3456]{1,0:T(8,128)}, u32[]{:S(2)}, u32[]{:S(2)}) collective-permute-start(f32[48,3456]{1,0:T(8,128)} %get-tuple-element.772), channel_id=1, source_target_pairs={{0,5},{1,6},{2,7},{3,8},{4,9},{5,10},{6,11},{7,12},{8,13},{9,14},{... | collective-permute-start | bytes 1990664
  4338.8 205.7 %collective-permute-start.41 = (f32[48,3456]{1,0:T(8,128)}, f32[48,3456]{1,0:T(8,128)}, u32[]{:S(2)}, u32[]{:S(2)}) collective-permute-start(f32[48,3456]{1,0:T(8,128)} %get-tuple-element.772), channel_id=1, source_target_pairs={{0,4},{1,5},{2,6},{3,7},{4,8},{5,9},{6,10},{7,11},{8,12},{9,13},{1... | collective-permute-start | bytes 1990664
  4357.9 172.3 %collective-permute-start.37 = (f32[36,3456]{1,0:T(8,128)}, f32[36,3456]{1,0:T(8,128)S(1)}, u32[]{:S(2)}, u32[]{:S(2)}) collective-permute-start(f32[36,3456]{1,0:T(8,128)} %slice.347), channel_id=1, source_target_pairs={{0,8},{1,9},{2,10},{3,11},{4,12},{5,13},{6,14},{7,15},{8,16},{9,17... | collective-permute-start | bytes 1493000
  (189 other events, 12035.1 us)
Sparse Core Ops, SparseCore 0:
  11.5 116.4 all-gather.20
  131.4 69.3 all-gather.22
  204.3 182.6 all-gather.26
  390.3 198.0 all-gather.24
  591.6 129.0 all-gather.28
  724.0 128.6 all-gather.34
  856.2 128.2 all-gather.32
  1064.2 164.0 all-gather.30
  4305.5 218.2 all-reduce.27
where the time goes:
time: 4820 us; the launch traced here: 4730 us
  blocking collectives  1900 us (39%)
  matrix products  772 us (16%)
  local copies, waits for them, and re-layouts  730 us (15%)
  waiting for transfers between devices  712 us (15%)
  starting transfers between devices  461 us (10%)
  other arithmetic  135 us (3%)
    unnamed x3, blocking collectives  1550 us
    ppermute x30, waiting for transfers between devices, from_behind(): return lax.ppermute(array, axis, pairs)  491 us
    dot_general x104, matrix products, inner_cols(): lax.dot_general(left_op, right_op, (((1,), (1,)), ((), ())), preferred_el...  344 us
    unnamed x325, local copies, waits for them, and re-layouts  286 us
    unnamed x49, starting transfers between devices  267 us
    all_gather x2, blocking collectives, per_device(): lax.all_gather(norm_gains[layer_index], ('dp', 'seq'), axis=1, tiled=True)  261 us
    unnamed x58, waiting for transfers between devices  221 us
    dot_general x72, matrix products, matmul(): return jnp.dot(left_op, right_op, preferred_element_type=jnp.float32)  217 us
  transfers between devices with their start and end apart: 87, of which 16 were waited for; matrix products, arithmetic and copies ran while one was open for 35% of the time, Pallas kernels for 0%

commit v1 on v0

v1 whole, which is shorter than its diff:
```python
import functools
import math

import jax
import jax.numpy as jnp
from jax import lax
from jax.experimental import pallas as pl
from jax.experimental.pallas import tpu as pltpu
from jax.sharding import PartitionSpec as P

HEADS = 16
IMG = 729
STEP = 8

eps_norm = 1e-06
beta_first = 0.9
beta_second = 0.95
learn_rate = 0.025
weight_decay = 0.1
eps_adam = 1e-08
span_len = 768
lane_pair = 256
masked_score = -1e30
mib = 2**20


def head_lanes(head, head_size, width):
    low = head * head_size
    first = jnp.minimum(low // 128 * 128, width - lane_pair)
    lanes = lax.broadcasted_iota(jnp.int32, (1, lane_pair), 1)
    inside = (lanes >= low - first) & (lanes < low - first + head_size)
    keys = pl.ds(pl.multiple_of(first, 128), lane_pair)
    values = pl.ds(pl.multiple_of(first + width, 128), lane_pair)
    return keys, values, inside


def dot_nn(left, right):
    return lax.dot_general(left, right, (((1,), (0,)), ((), ())), preferred_element_type=jnp.float32)


def dot_nt(left, right):
    return lax.dot_general(left, right, (((1,), (1,)), ((), ())), preferred_element_type=jnp.float32)


def dot_tn(left, right):
    return lax.dot_general(left, right, (((0,), (0,)), ((), ())), preferred_element_type=jnp.float32)


def attention_forward_kernel(
    tile, left, exp_scale, plan, query, window, own_code, span_code, out, lse_out, bias, mix
):
    tok, width = query.shape
    head_size = width // HEADS

    def one_span(tile_index, which):
        offset = pl.multiple_of(plan[4 * tile_index + which], 16)
        image = plan[4 * tile_index + 2 + which]
        rows = pl.ds(pl.multiple_of(tile_index * tile, 16), tile)
        own_rows = pl.ds(pl.multiple_of(left + tile_index * tile, 16), tile)
        span = pl.ds(offset, span_len)
        code = own_code[rows, :]
        row_image = jnp.maximum(code, -code)
        mine = row_image == image
        bias[...] = jnp.where(row_image == span_code[2 * tile_index + which], 0.0, masked_score)
        self_bias = jnp.where(code < 0, 0.0, masked_score)
        lse_lane = lax.broadcasted_iota(jnp.int32, (tile, lse_out.shape[1]), 1)

        def one_head(head, carry):
            lanes, value_lanes, inside = head_lanes(head, head_size, width)
            queries = jnp.where(inside, query[rows, lanes], 0)
            scores = dot_nt(queries, window[span, lanes]) * exp_scale + bias[...]
            own_key = window[own_rows, lanes].astype(jnp.float32)
            own_value = window[own_rows, value_lanes].astype(jnp.float32)
            self_score = (
                jnp.sum(queries.astype(jnp.float32) * own_key, axis=1, keepdims=True) * exp_scale
                + self_bias
            )
            top = jnp.maximum(jnp.max(scores, axis=1, keepdims=True), self_score)
            powers = jnp.exp2(scores - top)
            self_power = jnp.exp2(self_score - top)
            total = jnp.sum(powers, axis=1, keepdims=True) + self_power
            mixed = dot_nn(powers.astype(jnp.bfloat16), window[span, value_lanes])
            mixed = (mixed + self_power * own_value) / total
            mix[rows, lanes] = jnp.where(inside & mine, mixed, mix[rows, lanes])
            lse_out[rows, :] = jnp.where(
                (lse_lane == head) & mine, top + jnp.log2(total), lse_out[rows, :]
            )
            return carry

        lax.fori_loop(0, HEADS, one_head, 0)

    def one_tile(tile_index, carry):
        one_span(tile_index, 0)

        @pl.when(plan[4 * tile_index + 2] != plan[4 * tile_index + 3])
        def _():
            one_span(tile_index, 1)

        return carry

    lax.fori_loop(0, tok // tile, one_tile, 0)
    out[...] = mix[...].astype(out.dtype)


def attention_backward_kernel(
    tile, left, exp_scale, plan, query, window, grad, lse_in, own_code, span_code,
    grad_query, grad_window, bias, acc_query, acc_window,
):
    tok, width = query.shape
    head_size = width // HEADS
    scale = 1.0 / math.sqrt(head_size)
    acc_query[...] = jnp.zeros_like(acc_query)
    acc_window[...] = jnp.zeros_like(acc_window)

    def one_span(tile_index, which):
        offset = pl.multiple_of(plan[4 * tile_index + which], 16)
        image = plan[4 * tile_index + 2 + which]
        rows = pl.ds(pl.multiple_of(tile_index * tile, 16), tile)
        own_rows = pl.ds(pl.multiple_of(left + tile_index * tile, 16), tile)
        span = pl.ds(offset, span_len)
        code = own_code[rows, :]
        row_image = jnp.maximum(code, -code)
        mine = row_image == image
        bias[...] = jnp.where(
            mine & (span_code[2 * tile_index + which] == image), 0.0, masked_score
        )
        self_bias = jnp.where((code < 0) & mine, 0.0, masked_score)
        lse_lane = lax.broadcasted_iota(jnp.int32, (tile, lse_in.shape[1]), 1)

        def one_head(head, carry):
            lanes, value_lanes, inside = head_lanes(head, head_size, width)
            queries = jnp.where(inside, query[rows, lanes], 0)
            grads = jnp.where(inside, grad[rows, lanes], 0)
            lse = jnp.sum(jnp.where(lse_lane == head, lse_in[rows, :], 0.0), axis=1, keepdims=True)
            keys = window[span, lanes]
            own_key = window[own_rows, lanes].astype(jnp.float32)
            own_value = window[own_rows, value_lanes].astype(jnp.float32)
            queries_wide = queries.astype(jnp.float32)
            grads_wide = grads.astype(jnp.float32)
            prob = jnp.exp2(dot_nt(queries, keys) * exp_scale + bias[...] - lse)
            self_score = jnp.sum(queries_wide * own_key, axis=1, keepdims=True) * exp_scale
            self_prob = jnp.exp2(self_score + self_bias - lse)
            grad_prob = dot_nt(grads, window[span, value_lanes])
            self_grad = jnp.sum(grads_wide * own_value, axis=1, keepdims=True)
            inner = jnp.sum(prob * grad_prob, axis=1, keepdims=True) + self_prob * self_grad
            grad_scores = (prob * (grad_prob - inner)).astype(jnp.bfloat16)
            self_grad_score = self_prob * (self_grad - inner)
            part = dot_nn(grad_scores, keys) + self_grad_score * own_key
            acc_query[rows, lanes] += jnp.where(inside, part, 0.0)
            acc_window[span, lanes] += dot_tn(grad_scores, queries)
            acc_window[span, value_lanes] += dot_tn(prob.astype(jnp.bfloat16), grads)
            acc_window[own_rows, lanes] += self_grad_score * queries_wide
            acc_window[own_rows, value_lanes] += self_prob * grads_wide
            return carry

        lax.fori_loop(0, HEADS, one_head, 0)

    def one_tile(tile_index, carry):
        one_span(tile_index, 0)

        @pl.when(plan[4 * tile_index + 2] != plan[4 * tile_index + 3])
        def _():
            one_span(tile_index, 1)

        return carry

    lax.fori_loop(0, tok // tile, one_tile, 0)
    grad_query[...] = (acc_query[...] * scale).astype(grad_query.dtype)
    step = 16

    def narrow(index, carry):
        rows = pl.ds(pl.multiple_of(index * step, step), step)
        grad_window[rows, :width] = (acc_window[rows, :width] * scale).astype(grad_window.dtype)
        grad_window[rows, width:] = acc_window[rows, width:].astype(grad_window.dtype)
        return carry

    lax.fori_loop(0, acc_window.shape[0] // step, narrow, 0)


def in_vmem():
    return pl.BlockSpec(memory_space=pltpu.VMEM)


def attention_forward(tile, left, plan, query, window, own_code, span_code):
    tok, width = query.shape
    exp_scale = math.log2(math.e) / math.sqrt(width // HEADS)
    return pl.pallas_call(
        functools.partial(attention_forward_kernel, tile, left, exp_scale),
        name="attention_forward",
        out_shape=[
            jax.ShapeDtypeStruct((tok, width), jnp.bfloat16),
            jax.ShapeDtypeStruct((tok, 128), jnp.float32),
        ],
        in_specs=[pl.BlockSpec(memory_space=pltpu.SMEM)] + [in_vmem()] * 4,
        out_specs=[in_vmem()] * 2,
        scratch_shapes=[
            pltpu.VMEM((tile, span_len), jnp.float32),
            pltpu.VMEM((tok, width), jnp.float32),
        ],
        compiler_params=pltpu.CompilerParams(vmem_limit_bytes=60 * mib),
    )(plan, query, window, own_code, span_code)


def attention_backward(tile, left, plan, query, window, grad, lse, own_code, span_code):
    tok, width = query.shape
    exp_scale = math.log2(math.e) / math.sqrt(width // HEADS)
    return pl.pallas_call(
        functools.partial(attention_backward_kernel, tile, left, exp_scale),
        name="attention_backward",
        out_shape=[
            jax.ShapeDtypeStruct((tok, width), jnp.bfloat16),
            jax.ShapeDtypeStruct(window.shape, jnp.bfloat16),
        ],
        in_specs=[pl.BlockSpec(memory_space=pltpu.SMEM)] + [in_vmem()] * 6,
        out_specs=[in_vmem()] * 2,
        scratch_shapes=[
            pltpu.VMEM((tile, span_len), jnp.float32),
            pltpu.VMEM((tok, width), jnp.float32),
            pltpu.VMEM(window.shape, jnp.float32),
        ],
        compiler_params=pltpu.CompilerParams(vmem_limit_bytes=62 * mib),
    )(plan, query, window, grad, lse, own_code, span_code)


def attention_plan(tile, left, right, own_ids, own_mask, window_ids, window_mask, place, places):
    tok = own_ids.shape[0]
    window_len = left + tok + right
    room = jnp.minimum(window_len, left + (places - place) * tok) - span_len
    position = jnp.arange(window_len)
    present = (position >= left - place * tok) & (position < left + (places - place) * tok)
    floor_ids = jnp.where(position < left, -1, window_ids + 0)
    ids = jnp.where(present, window_ids, floor_ids)
    codes = jnp.where((window_mask > 0) & present, window_ids + 1, 0)
    plans, spans = [], []
    for index in range(tok // tile):
        images = (own_ids[index * tile], own_ids[(index + 1) * tile - 1])
        offsets = []
        for image in images:
            start = jnp.sum((ids < image) & (position < left + tok)).astype(jnp.int32)
            offset = jnp.minimum(start // 16 * 16, room)
            offsets.append(offset)
            spans.append(lax.dynamic_slice(codes, (offset,), (span_len,)))
        plans += offsets + [image + 1 for image in images]
    plan = jnp.stack(plans).astype(jnp.int32)
    own_code = jnp.where(own_mask > 0, own_ids + 1, -(own_ids + 1)).astype(jnp.int32)[:, None]
    return plan, own_code, jnp.stack(spans)[:, None, :].astype(jnp.int32)


class Layout:
    def __init__(self, groups, seats, model_width):
        self.rows = model_width // (groups * seats)
        self.members = 2
        while self.members * self.rows % 16:
            self.members *= 2
        self.sides = self.members // 2
        self.lines = seats // self.members
        self.slab = self.members * self.rows
        self.padded = -(-self.rows // 16) * 16
        self.near = model_width // groups
        self.model_width = model_width

    def width(self, columns, shared):
        blocks = 2 if shared else 2 * self.sides
        return -(-columns // (128 * blocks)) * 128

    def columns(self, columns, shared):
        return self.width(columns, shared) * (2 if shared else 2 * self.sides)


class Mail:
    def __init__(self, layout, send, recv, slots):
        self.layout, self.send_sems, self.recv_sems, self.slots = layout, send, recv, slots
        self.group = lax.axis_index("dp")
        seat = lax.axis_index("seq")
        self.line = seat // layout.members
        self.member = seat % layout.members
        self.side = self.member // 2
        self.core = self.member % 2
        self.started = []

    def at(self, group=None, line=None, side=None, core=None):
        group = self.group if group is None else group
        line = self.line if line is None else line
        side = self.side if side is None else side
        core = self.core if core is None else core
        return (group, line * self.layout.members + side * 2 + core)

    def copy(self, slot, source, target, device, shift=0):
        index = self.slots[slot] + shift
        return pltpu.make_async_remote_copy(
            src_ref=source,
            dst_ref=target,
            send_sem=self.send_sems.at[index],
            recv_sem=self.recv_sems.at[index],
            device_id=device,
            device_id_type=pl.DeviceIdType.MESH,
        )

    def send(self, slot, source, target, device, when=None):
        copy = self.copy(slot, source, target, device)
        self.started.append((copy, when))
        guarded(when, copy.start)

    def wait(self, slot, target, shift=0):
        self.copy(slot, target, target, self.at(core=1 - self.core), shift).wait_recv()

    def finish(self):
        for copy, when in self.started:
            guarded(when, copy.wait_send)


def guarded(when, action):
    if when is None:
        action()
    else:
        pl.when(when)(action)


def all_of(*conditions):
    kept = [condition for condition in conditions if condition is not None]
    return functools.reduce(jnp.logical_and, kept) if kept else None


def run_steps(works, lag):
    waiting = [(index, work) for index, work in enumerate(works)]
    for _, work in waiting:
        next(work)
    clock = 0
    while waiting:
        for entry in list(waiting):
            if clock >= lag * entry[0]:
                try:
                    next(entry[1])
                except StopIteration:
                    waiting.remove(entry)
        clock += 1


def number(names):
    return {name: index for index, name in enumerate(names)}


def gather_slots(layout, shared):
    names = []
    steps = range(1, layout.lines)
    sources = ["own"] + [f"{way}{t}" for t in steps for way in ("below", "above")]
    for index, one_block in enumerate(shared):
        names += [(index, "mix", j) for j in range(1, layout.members)]
        names += [(index, way, t) for way in ("up", "down") for t in range(layout.lines)]
        names += [(index, "cross", source) for source in sources]
        if not one_block:
            for j in range(1, layout.sides):
                names += [
                    (index, "side", half, source, j) for half in (0, 1) for source in sources
                ]
        names += [(index, "core", j) for j in range(layout.sides)]
    return number(names)


def gather_kernel(layout, shared, widths, lag, *refs):
    count = len(shared)
    shards, outs = refs[:count], refs[count : 2 * count]
    landings, slabs = refs[2 * count : 3 * count], refs[3 * count : 4 * count]
    wide, send, recv, local = refs[4 * count :]
    mail = Mail(layout, send, recv, gather_slots(layout, shared))
    group, line, member, side, core = mail.group, mail.line, mail.member, mail.side, mail.core
    lines, members, sides = layout.lines, layout.members, layout.sides
    has_up, has_down = line < lines - 1, line > 0

    def work(index):
        shard, out, landing, slab = shards[index], outs[index], landings[index], slabs[index]
        width, one_block = widths[index], shared[index]

        def columns(side_of, core_of):
            block = core_of if one_block else core_of * sides + side_of
            return pl.ds(pl.multiple_of(block * width, 128), width)

        own = columns(side, core)

        def place(group_of, line_of):
            first = (group_of * lines + line_of) * layout.slab
            return out.at[pl.ds(pl.multiple_of(first, 16), layout.slab), own]

        for j in range(1, members):
            other = (member + j) % members
            mail.send(
                (index, "mix", j),
                shard.at[:, columns(other // 2, other % 2)],
                landing.at[member],
                mail.at(side=other // 2, core=other % 2),
            )
        mine = pltpu.make_async_copy(shard.at[:, own], landing.at[member], local.at[index, 0])
        mine.start()
        yield
        for j in range(1, members):
            mail.wait((index, "mix", j), landing.at[(member + members - j) % members])
        mine.wait()
        for m in range(members):
            rows = slice(m * layout.rows, (m + 1) * layout.rows)
            wide[rows, :width] = landing[m, : layout.rows, :].astype(jnp.float32)
        slab[...] = wide[:, :width].astype(slab.dtype)
        keep = pltpu.make_async_copy(slab, place(group, line), local.at[index, 1])
        keep.start()

        def pass_on(source, what, half, where, when=None):
            if half == 0:
                mail.send(
                    (index, "cross", source), what, where, mail.at(group=1 - group), when
                )
            if not one_block:
                for j in range(1, sides):
                    mail.send(
                        (index, "side", half, source, j),
                        what,
                        where,
                        mail.at(side=(side + j) % sides),
                        when,
                    )

        home = place(group, line)
        mail.send((index, "up", 0), slab, home, mail.at(line=line + 1), has_up)
        mail.send((index, "down", 0), slab, home, mail.at(line=line - 1), has_down)
        pass_on("own", slab, 0, home)
        yield
        for t in range(1, lines):
            below, above = line >= t, line < lines - t

            @pl.when(below)
            def _():
                mail.wait((index, "up", t - 1), place(group, line - t))

            where = place(group, line - t)
            mail.send(
                (index, "up", t), where, where, mail.at(line=line + 1), all_of(below, has_up)
            )
            pass_on(f"below{t}", where, 0, where, below)

            @pl.when(above)
            def _():
                mail.wait((index, "down", t - 1), place(group, line + t))

            where = place(group, line + t)
            mail.send(
                (index, "down", t), where, where, mail.at(line=line - 1), all_of(above, has_down)
            )
            pass_on(f"above{t}", where, 0, where, above)
            if t == 1:
                where = place(1 - group, line)
                mail.wait((index, "cross", "own"), where)
                pass_on("own", where, 1, where)
            yield
        for t in range(1, lines):
            for way, step, when in (("below", -t, line >= t), ("above", t, line < lines - t)):
                where = place(1 - group, line + step)

                @pl.when(when)
                def _():
                    mail.wait((index, "cross", f"{way}{t}"), where)

                pass_on(f"{way}{t}", where, 1, where, when)
            yield
        keep.wait()
        partner = mail.at(core=1 - core)
        mail.send((index, "core", 0), out.at[:, own], out.at[:, own], partner)
        if not one_block:
            yield
            for j in range(1, sides):
                source_side = (side + sides - j) % sides
                theirs = columns(source_side, core)
                for half, group_of in ((0, group), (1, 1 - group)):
                    for source, step, when in [("own", 0, None)] + [
                        (f"{way}{t}", sign * t, line >= t if sign < 0 else line < lines - t)
                        for t in range(1, lines)
                        for way, sign in (("below", -1), ("above", 1))
                    ]:
                        first = (group_of * lines + line + step) * layout.slab
                        where = out.at[pl.ds(pl.multiple_of(first, 16), layout.slab), theirs]
                        slot = (index, "side", half, source, j)
                        guarded(when, functools.partial(mail.wait, slot, where))
                mail.send((index, "core", j), out.at[:, theirs], out.at[:, theirs], partner)
        yield
        mail.wait((index, "core", 0), out.at[:, columns(side, 1 - core)])
        if not one_block:
            for j in range(1, sides):
                source_side = (side + sides - j) % sides
                mail.wait((index, "core", j), out.at[:, columns(source_side, 1 - core)])

    run_steps([work(index) for index in range(count)], lag)
    mail.finish()


def gather_parameters(layout, shards, shared, lag=2):
    widths = [
        shard.shape[1] // (2 if one_block else 2 * layout.sides)
        for shard, one_block in zip(shards, shared)
    ]
    slots = len(gather_slots(layout, shared))
    anywhere = pl.BlockSpec(memory_space=pl.ANY)
    return pl.pallas_call(
        functools.partial(gather_kernel, layout, shared, widths, lag),
        name="gather_parameters",
        out_shape=[
            jax.ShapeDtypeStruct((layout.model_width, shard.shape[1]), shard.dtype)
            for shard in shards
        ],
        in_specs=[anywhere] * len(shards),
        out_specs=[anywhere] * len(shards),
        scratch_shapes=[
            pltpu.VMEM((layout.members, layout.padded, width), jnp.bfloat16) for width in widths
        ]
        + [pltpu.VMEM((layout.slab, width), jnp.bfloat16) for width in widths]
        + [
            pltpu.VMEM((layout.slab, max(widths)), jnp.float32),
            pltpu.SemaphoreType.DMA((slots,)),
            pltpu.SemaphoreType.DMA((slots,)),
            pltpu.SemaphoreType.DMA((len(shards), 2)),
        ],
        compiler_params=pltpu.CompilerParams(
            has_side_effects=True, vmem_limit_bytes=40 * mib
        ),
    )(*shards)


def reduce_slots(layout, shared):
    names = []
    for index, one_block in enumerate(shared):
        names += [(index, "core", half) for half in (0, 1)]
        if not one_block:
            names += [(index, "side", half, j) for half in (0, 1) for j in range(1, layout.sides)]
        names += [(index, "cross")]
        names += [(index, way, t) for way in ("up", "down") for t in range(layout.lines)]
        names += [(index, "mix", j) for j in range(1, layout.members)]
    return number(names)


def add_rows(target, first, target_columns, source, source_columns, count, source_first=0):
    step = 48

    def one(index, carry):
        rows = pl.ds(pl.multiple_of(first + index * step, 16), step)
        theirs = pl.ds(pl.multiple_of(source_first + index * step, 16), step)
        total = target[rows, target_columns].astype(jnp.float32)
        total += source[theirs, source_columns].astype(jnp.float32)
        target[rows, target_columns] = total.astype(target.dtype)
        return carry

    lax.fori_loop(0, count // step, one, 0)


def reduce_kernel(layout, shared, widths, lag, *refs):
    count = len(shared)
    take = iter(range(0, len(refs), count))
    grads, outs, cores, sums, crosses, ups, downs, pieces, landings = (
        refs[first : first + count] for first in [next(take) for _ in range(9)]
    )
    rest = list(refs[9 * count :])
    sides_in = [None if one_block else rest.pop(0) for one_block in shared]
    wide, spare, send, recv, local = rest
    mail = Mail(layout, send, recv, reduce_slots(layout, shared))
    group, line, member, side, core = mail.group, mail.line, mail.member, mail.side, mail.core
    lines, members, sides = layout.lines, layout.members, layout.sides
    near_rows, slab_rows = layout.near, layout.slab
    far_first = pl.multiple_of((1 - group) * near_rows, 16)
    near_first = pl.multiple_of(group * near_rows, 16)

    def work(index):
        grad, out, from_core, total = grads[index], outs[index], cores[index], sums[index]
        cross, up, down = crosses[index], ups[index], downs[index]
        piece, landing, from_side = pieces[index], landings[index], sides_in[index]
        width, one_block = widths[index], shared[index]
        half = width if one_block else width * sides
        first_own = 0 if one_block else pl.multiple_of(side * width, 128)
        own = pl.ds(first_own, width)
        halves = ((0, far_first), (1, near_first))
        loads = []
        for tag, first in halves:
            rows = pl.ds(first, near_rows)
            away = pl.ds(pl.multiple_of((1 - core) * half, 128), half)
            stay = pl.ds(pl.multiple_of(core * half, 128), half)
            mail.send(
                (index, "core", tag), grad.at[rows, away], from_core.at[rows], mail.at(core=1 - core)
            )
            load = pltpu.make_async_copy(grad.at[rows, stay], total.at[rows], local.at[index, tag])
            load.start()
            loads.append(load)
        yield
        for tag, first in halves:
            rows = pl.ds(first, near_rows)
            mail.wait((index, "core", tag), from_core.at[rows])
            fetch = pltpu.make_async_copy(
                from_core.at[rows], spare.at[:, pl.ds(0, half)], local.at[index, 2]
            )
            fetch.start()
            loads[tag].wait()
            fetch.wait()
            add_rows(total, first, pl.ds(0, half), spare, pl.ds(0, half), near_rows)
            if not one_block:
                for j in range(1, sides):
                    other = (side + j) % sides
                    theirs = pl.ds(pl.multiple_of(other * width, 128), width)
                    mail.send(
                        (index, "side", tag, j),
                        total.at[rows, theirs],
                        from_side.at[j - 1, rows],
                        mail.at(side=other),
                    )
            elif tag == 0:
                mail.send((index, "cross"), total.at[rows, own], cross, mail.at(group=1 - group))
            yield
        if not one_block:
            for tag, first in halves:
                rows = pl.ds(first, near_rows)
                for j in range(1, sides):
                    mail.wait((index, "side", tag, j), from_side.at[j - 1, rows])
                    add_rows(
                        total, first, own, from_side.at[j - 1], pl.ds(0, width), near_rows, first
                    )
                if tag == 0:
                    mail.send(
                        (index, "cross"), total.at[rows, own], cross, mail.at(group=1 - group)
                    )
                yield
        mail.wait((index, "cross"), cross)
        add_rows(total, near_first, own, cross, pl.ds(0, width), near_rows)

        def slab_first(line_of):
            return pl.multiple_of(near_first + line_of * slab_rows, 16)

        for t in range(lines - 1):
            for way, buffer, goal, going, fed, to in (
                ("up", up, lines - 1 - t, line < lines - 1 - t, line > 0, line + 1),
                ("down", down, t, line > t, line < lines - 1, line - 1),
            ):
                slot = (index, way, goal)
                first = slab_first(goal)

                @pl.when(all_of(going, fed))
                def _():
                    mail.wait(slot, buffer.at[goal])
                    add_rows(total, first, own, buffer.at[goal], pl.ds(0, width), slab_rows)

                mail.send(
                    slot,
                    total.at[pl.ds(first, slab_rows), own],
                    buffer.at[goal],
                    mail.at(line=to),
                    going,
                )
            yield
        first = slab_first(line)
        wide[:, :width] = total[pl.ds(first, slab_rows), own].astype(jnp.float32)
        for way, buffer, fed in (("up", up, line > 0), ("down", down, line < lines - 1)):

            @pl.when(fed)
            def _():
                mail.wait((index, way, 0), buffer.at[line], line)
                wide[:, :width] += buffer[line].astype(jnp.float32)

        for m in range(members):
            rows = slice(m * layout.rows, (m + 1) * layout.rows)
            piece[m] = jnp.zeros(piece.shape[1:], piece.dtype)
            piece[m, : layout.rows, :] = wide[rows, :width].astype(piece.dtype)
        seat = core * sides + side
        for j in range(1, members):
            other = (member + j) % members
            mail.send(
                (index, "mix", j),
                piece.at[other],
                landing.at[seat],
                mail.at(side=other // 2, core=other % 2),
            )
        landing[seat] = piece[member]
        yield
        for j in range(1, members):
            other = (member + members - j) % members
            mail.wait((index, "mix", j), landing.at[other % 2 * sides + other // 2])
        if one_block:
            for c in range(2):
                block = landing[c * sides].astype(jnp.float32)
                for s in range(1, sides):
                    block += landing[c * sides + s].astype(jnp.float32)
                out[:, c * width : (c + 1) * width] = block
        else:
            for b in range(2 * sides):
                out[:, b * width : (b + 1) * width] = landing[b].astype(jnp.float32)

    run_steps([work(index) for index in range(count)], lag)
    mail.finish()


def reduce_gradients(layout, grads, shared, lag=1):
    blocks = [2 if one_block else 2 * layout.sides for one_block in shared]
    widths = [grad.shape[1] // block for grad, block in zip(grads, blocks)]
    slots = len(reduce_slots(layout, shared))
    anywhere = pl.BlockSpec(memory_space=pl.ANY)
    count, rows, slab = len(grads), layout.model_width, layout.slab
    low = jnp.bfloat16
    members, padded, lines = layout.members, layout.padded, layout.lines
    halves = [grad.shape[1] // 2 for grad in grads]
    results = pl.pallas_call(
        functools.partial(reduce_kernel, layout, shared, widths, lag),
        name="reduce_gradients",
        out_shape=[jax.ShapeDtypeStruct((padded, grad.shape[1]), jnp.float32) for grad in grads]
        + [jax.ShapeDtypeStruct((rows, half), low) for half in halves],
        in_specs=[anywhere] * count,
        out_specs=[in_vmem()] * count + [anywhere] * count,
        scratch_shapes=[pltpu.VMEM((rows, half), low) for half in halves]
        + [pltpu.VMEM((layout.near, width), low) for width in widths]
        + [pltpu.VMEM((lines, slab, width), low) for _ in range(2) for width in widths]
        + [pltpu.VMEM((members, padded, width), low) for _ in range(2) for width in widths]
        + [
            pltpu.VMEM((layout.sides - 1, rows, width), low)
            for width, one_block in zip(widths, shared)
            if not one_block
        ]
        + [
            pltpu.VMEM((slab, max(widths)), jnp.float32),
            pltpu.VMEM((layout.near, max(halves)), low),
            pltpu.SemaphoreType.DMA((slots,)),
            pltpu.SemaphoreType.DMA((slots,)),
            pltpu.SemaphoreType.DMA((count, 3)),
        ],
        compiler_params=pltpu.CompilerParams(
            has_side_effects=True, vmem_limit_bytes=60 * mib
        ),
    )(*grads)
    return results[:count]


def shifted(array, by):
    devices = lax.axis_size("seq")
    pairs = [(i, i + by) for i in range(devices) if 0 <= i + by < devices]
    return lax.ppermute(array, "seq", pairs)


def column_sum(source):
    return jnp.sum(source.astype(jnp.float32), axis=0)


def norm_forward(source, gain_row, shift_row):
    row_mean = jnp.mean(source, axis=-1, keepdims=True)
    centred = source - row_mean
    variance = jnp.mean(centred * centred, axis=-1, keepdims=True)
    inv_scale = lax.rsqrt(variance + eps_norm)
    unit_rows = centred * inv_scale
    return (unit_rows * gain_row + shift_row, unit_rows, inv_scale)


def norm_backward(gradient, unit_rows, inv_scale, gain_row):
    scaled = gradient * gain_row
    grad_in = inv_scale * (
        scaled
        - jnp.mean(scaled, axis=-1, keepdims=True)
        - unit_rows * jnp.mean(scaled * unit_rows, axis=-1, keepdims=True)
    )
    return (grad_in, jnp.sum(gradient * unit_rows, axis=0), jnp.sum(gradient, axis=0))


def gelu_tanh(source):
    return jax.nn.gelu(source, approximate=True)


def adam_step(weight_now, gradient, first_old, second_old):
    first_new = beta_first * first_old + (1.0 - beta_first) * gradient
    second_new = beta_second * second_old + (1.0 - beta_second) * gradient * gradient
    first_hat = first_new / (1.0 - beta_first**STEP)
    second_hat = second_new / (1.0 - beta_second**STEP)
    update = -learn_rate * (
        first_hat / (jnp.sqrt(second_hat) + eps_adam)
        + weight_decay * weight_now.astype(jnp.float32)
    )
    return (first_new, second_new, update)


def round_up(count, unit):
    return -(-count // unit) * unit


def per_device(
    inputs, image_ids, token_mask, cotangent,
    w_qkv, w_out, w_up, w_down, norm_gains, bias_rows, up_bias,
    first_qkv, first_out, first_up, first_down, first_gains, first_bias, first_upbias,
    second_qkv, second_out, second_up, second_down, second_gains, second_bias, second_upbias,
):
    tok, width = inputs.shape
    layers, _, hidden_width = w_up.shape
    places = lax.axis_size("seq")
    place = lax.axis_index("seq")
    layout = Layout(lax.axis_size("dp"), places, width)
    group_tok = tok * places
    spare_count = group_tok - group_tok // IMG * IMG
    left = round_up(IMG - 1 + spare_count, 16)
    right = round_up(IMG - 1, 16)
    tile = tok // 2

    reach_left = [min(tok, left - first) for first in range(0, left, tok)]
    reach_right = [min(tok, right - first) for first in range(0, right, tok)]

    def window_of(array):
        parts = [shifted(array[tok - rows :], by + 1) for by, rows in enumerate(reach_left)][::-1]
        parts += [array]
        parts += [shifted(array[:rows], -by - 1) for by, rows in enumerate(reach_right)]
        return jnp.concatenate(parts)

    def owned_of(window):
        total = window[left : left + tok].astype(jnp.float32)
        for by, rows in enumerate(reach_left):
            first = left - by * tok - rows
            part = shifted(window[first : first + rows], -by - 1).astype(jnp.float32)
            total = total + jnp.pad(part, ((tok - rows, 0), (0, 0)))
        for by, rows in enumerate(reach_right):
            first = left + (by + 1) * tok
            part = shifted(window[first : first + rows], by + 1).astype(jnp.float32)
            total = total + jnp.pad(part, ((0, tok - rows), (0, 0)))
        return total.astype(jnp.bfloat16)

    half = hidden_width // 2
    half_pad = round_up(half + 8 * layers, 128)
    wide_columns = 2 * half_pad

    def spread(array):
        pad = [(0, 0)] * (array.ndim - 1) + [(0, half_pad - half)]
        return jnp.concatenate([jnp.pad(array[..., :half], pad), jnp.pad(array[..., half:], pad)], -1)

    def unspread(array):
        return jnp.concatenate(
            [array[..., :half], array[..., half_pad : half_pad + half]], axis=-1
        )

    def filled(array, rows, columns):
        return jnp.pad(array, ((0, rows - array.shape[0]), (0, columns - array.shape[1])))

    shared = (False, True, False)
    attn_columns = layout.columns(4 * width, False)
    up_columns = layout.columns(wide_columns, True)
    down_columns = layout.columns(wide_columns, False)
    rows_of = jnp.concatenate([norm_gains.reshape(-1, layout.rows), bias_rows.reshape(-1, layout.rows)])
    row_count = rows_of.shape[0]
    shards = []
    for layer in range(layers):
        attn_shard = jnp.concatenate([w_qkv[layer], w_out[layer]], axis=1)
        up_shard = spread(w_up[layer])
        if layer == 0:
            up_shard = up_shard.at[:, half : half + row_count].set(rows_of.T)
        down_shard = spread(w_down[layer].T)
        shards += [
            filled(attn_shard, layout.padded, attn_columns),
            filled(up_shard, layout.padded, up_columns),
            filled(down_shard, layout.padded, down_columns),
        ]
    gathered = gather_parameters(layout, shards, shared * layers)
    all_rows = gathered[1][:, half : half + row_count].T.astype(jnp.float32)
    gains = all_rows[: 2 * layers].reshape(layers, 2, width)
    shifts = all_rows[2 * layers :].reshape(layers, 6, width)
    up_shift = spread(up_bias.astype(jnp.float32))

    window_word = window_of(image_ids * 2 + (token_mask > 0).astype(jnp.int32))
    plan, own_code, span_code = attention_plan(
        tile, left, right, image_ids, token_mask, window_word // 2, window_word % 2, place, places
    )

    residual = inputs.astype(jnp.float32)
    kept_layers = []
    for layer in range(layers):
        attn_weight, up_weight, down_weight = gathered[3 * layer : 3 * layer + 3]
        down_weight = down_weight[:, :wide_columns]
        normed, unit_one, inv_one = norm_forward(residual, gains[layer, 0], shifts[layer, 0])
        normed_low = normed.astype(jnp.bfloat16)
        projected = dot_nn(normed_low, attn_weight[:, : 3 * width])
        queries = (projected[:, :width] + shifts[layer, 2]).astype(jnp.bfloat16)
        value_shift = jnp.concatenate([jnp.zeros_like(shifts[layer, 3]), shifts[layer, 3]])
        key_value = (projected[:, width:] + value_shift).astype(jnp.bfloat16)
        window = window_of(key_value)
        attended, lse = attention_forward(tile, left, plan, queries, window, own_code, span_code)
        middle = (
            residual
            + dot_nn(attended, attn_weight[:, 3 * width : 4 * width])
            + shifts[layer, 4]
        )
        hidden, unit_two, inv_two = norm_forward(middle, gains[layer, 1], shifts[layer, 1])
        hidden_low = hidden.astype(jnp.bfloat16)
        pre_act = dot_nn(hidden_low, up_weight[:, :wide_columns]) + up_shift[layer]
        active = gelu_tanh(pre_act).astype(jnp.bfloat16)
        residual = middle + dot_nt(active, down_weight) + shifts[layer, 5]
        kept_layers.append(
            (window, unit_one, inv_one, normed_low, queries, lse, attended,
             unit_two, inv_two, hidden_low, pre_act, active)
        )

    grad_res = cotangent.astype(jnp.float32)
    owned = [None] * layers
    upbias_grads = [None] * layers
    for layer in reversed(range(layers)):
        (window, unit_one, inv_one, normed_low, queries, lse, attended,
         unit_two, inv_two, hidden_low, pre_act, active) = kept_layers[layer]
        attn_weight, up_weight, down_weight = gathered[3 * layer : 3 * layer + 3]
        down_weight = down_weight[:, :wide_columns]
        grad_branch = grad_res.astype(jnp.bfloat16)
        grad_downw = dot_tn(grad_branch, active).astype(jnp.bfloat16)
        grad_active = dot_nn(grad_branch, down_weight)
        _, gelu_pull = jax.vjp(gelu_tanh, pre_act)
        grad_pre = gelu_pull(grad_active)[0].astype(jnp.bfloat16)
        grad_upw = dot_tn(hidden_low, grad_pre).astype(jnp.bfloat16)
        upbias_grads[layer] = lax.psum(unspread(column_sum(grad_pre)), ("dp", "seq"))
        grad_hidden = dot_nt(grad_pre, up_weight[:, :wide_columns])
        back_two, gain_two, shift_two = norm_backward(
            grad_hidden, unit_two, inv_two, gains[layer, 1]
        )
        grad_mid = grad_res + back_two
        grad_attn = grad_mid.astype(jnp.bfloat16)
        grad_outw = dot_tn(attended, grad_attn).astype(jnp.bfloat16)
        grad_attended = dot_nt(grad_attn, attn_weight[:, 3 * width : 4 * width]).astype(
            jnp.bfloat16
        )
        grad_query, grad_window = attention_backward(
            tile, left, plan, queries, window, grad_attended, lse, own_code, span_code
        )
        grad_key_value = owned_of(grad_window)
        grad_proj = jnp.concatenate([grad_query, grad_key_value], axis=1)
        grad_qkvw = dot_tn(normed_low, grad_proj).astype(jnp.bfloat16)
        grad_normed = dot_nt(grad_proj, attn_weight[:, : 3 * width])
        back_one, gain_one, shift_one = norm_backward(
            grad_normed, unit_one, inv_one, gains[layer, 0]
        )
        grad_res = grad_mid + back_one
        grad_rows = jnp.stack(
            [
                gain_one,
                gain_two,
                shift_one,
                shift_two,
                column_sum(grad_query),
                column_sum(grad_key_value[:, width:]),
                column_sum(grad_attn),
                column_sum(grad_branch),
            ]
        )
        grad_upw = grad_upw.at[:, half : half + 8].set(grad_rows.T.astype(jnp.bfloat16))
        owned[layer] = reduce_gradients(
            layout,
            [
                filled(jnp.concatenate([grad_qkvw, grad_outw], axis=1), width, attn_columns),
                filled(grad_upw, width, up_columns),
                filled(grad_downw, width, down_columns),
            ],
            shared,
        )

    def stacked(part):
        return jnp.stack([part(*owned[layer]) for layer in range(layers)])

    rows = layout.rows
    grads = (
        stacked(lambda attn, up, down: attn[:rows, : 3 * width]),
        stacked(lambda attn, up, down: attn[:rows, 3 * width : 4 * width]),
        stacked(lambda attn, up, down: unspread(up[:rows])),
        stacked(lambda attn, up, down: unspread(down[:rows]).T),
        stacked(lambda attn, up, down: up[:rows, half : half + 2].T),
        stacked(lambda attn, up, down: up[:rows, half + 2 : half + 8].T),
        jnp.stack(upbias_grads),
    )
    params = (w_qkv, w_out, w_up, w_down, norm_gains, bias_rows, up_bias)
    firsts = (first_qkv, first_out, first_up, first_down, first_gains, first_bias, first_upbias)
    seconds = (
        second_qkv, second_out, second_up, second_down, second_gains, second_bias, second_upbias,
    )
    results = [adam_step(*packed) for packed in zip(params, grads, firsts, seconds)]
    return (
        (residual, grad_res)
        + grads
        + tuple(result[0] for result in results)
        + tuple(result[1] for result in results)
        + tuple(result[2] for result in results)
    )


def solution(mesh):
    in_specs = (
        P(("dp", "seq"), None),
        P(("dp", "seq")),
        P(("dp", "seq")),
        P(("dp", "seq"), None),
        P(None, ("dp", "seq"), None),
        P(None, ("dp", "seq"), None),
        P(None, ("dp", "seq"), None),
        P(None, None, ("dp", "seq")),
        P(None, None, ("dp", "seq")),
        P(None, None, ("dp", "seq")),
        P(),
        P(None, ("dp", "seq"), None),
        P(None, ("dp", "seq"), None),
        P(None, ("dp", "seq"), None),
        P(None, None, ("dp", "seq")),
        P(None, None, ("dp", "seq")),
        P(None, None, ("dp", "seq")),
        P(),
        P(None, ("dp", "seq"), None),
        P(None, ("dp", "seq"), None),
        P(None, ("dp", "seq"), None),
        P(None, None, ("dp", "seq")),
        P(None, None, ("dp", "seq")),
        P(None, None, ("dp", "seq")),
        P(),
    )
    out_specs = (
        P(("dp", "seq"), None),
        P(("dp", "seq"), None),
        P(None, ("dp", "seq"), None),
        P(None, ("dp", "seq"), None),
        P(None, ("dp", "seq"), None),
        P(None, None, ("dp", "seq")),
        P(None, None, ("dp", "seq")),
        P(None, None, ("dp", "seq")),
        P(),
        P(None, ("dp", "seq"), None),
        P(None, ("dp", "seq"), None),
        P(None, ("dp", "seq"), None),
        P(None, None, ("dp", "seq")),
        P(None, None, ("dp", "seq")),
        P(None, None, ("dp", "seq")),
        P(),
        P(None, ("dp", "seq"), None),
        P(None, ("dp", "seq"), None),
        P(None, ("dp", "seq"), None),
        P(None, None, ("dp", "seq")),
        P(None, None, ("dp", "seq")),
        P(None, None, ("dp", "seq")),
        P(),
        P(None, ("dp", "seq"), None),
        P(None, ("dp", "seq"), None),
        P(None, ("dp", "seq"), None),
        P(None, None, ("dp", "seq")),
        P(None, None, ("dp", "seq")),
        P(None, None, ("dp", "seq")),
        P(),
    )
    return jax.shard_map(
        per_device, mesh=mesh, in_specs=in_specs, out_specs=out_specs, check_vma=False
    )
```

time: 4820 us -> 1810 us (0.38); the launches traced: 4730 us -> 1800 us
  blocking collectives: 1900 us -> 38.7 us
  Pallas kernels: 0 us -> 903 us
  local copies, waits for them, and re-layouts: 730 us -> 141 us
  matrix products: 772 us -> 225 us
  waiting for transfers between devices: 712 us -> 224 us
  starting transfers between devices: 461 us -> 182 us
  other arithmetic: 135 us -> 67.6 us
    unnamed x3 -> x0, blocking collectives: 1550 us -> none
    pallas_call x0 -> x7, Pallas kernels: none -> 903 us  [the longest x2 460 us: reduce_gradients(): pl.pallas_call(functools.partial(reduce_kernel, layout, shared, widths, l...]
    dot_general x248 -> x24, matrix products: 772 us -> 225 us  [the longest x8 83.2 us: dot_nn(): lax.dot_general(left, right, (((1,), (0,)), ((), ())), preferred_element_...]
    all_gather x4 -> x0, blocking collectives: 347 us -> none  [the longest x2 261 us: per_device(): lax.all_gather(norm_gains[layer_index], ('dp', 'seq'), axis=1, tiled=True)]
    ppermute x30 -> x25, waiting for transfers between devices: 491 us -> 224 us  [shifted(): return lax.ppermute(array, 'seq', pairs)]
    unnamed x49 -> x0, starting transfers between devices: 267 us -> none
    unnamed x325 -> x253, local copies, waits for them, and re-layouts: 286 us -> 50.2 us
    unnamed x58 -> x0, waiting for transfers between devices: 221 us -> none
  transfers between devices with their start and end apart: 87 -> 25, of which waited for: 16 -> 8; matrix products, arithmetic and copies ran while one was open for 35% -> 7% of each run, Pallas kernels for 0% -> 15%
where the time goes in v1:
time: 1810 us; the launch traced here: 1800 us
  Pallas kernels  903 us (50%)
  matrix products  225 us (12%)
  waiting for transfers between devices  224 us (12%)
  starting transfers between devices  182 us (10%)
  local copies, waits for them, and re-layouts  141 us (8%)
  other arithmetic  67.6 us (4%)
  blocking collectives  38.7 us (2%)
    pallas_call x2, Pallas kernels, reduce_gradients(): pl.pallas_call(functools.partial(reduce_kernel, layout, shared, widths, l...  460 us
    pallas_call x1, Pallas kernels, gather_parameters(): pl.pallas_call(functools.partial(gather_kernel, layout, shared, widths, l...  282 us
    ppermute x25, waiting for transfers between devices, shifted(): return lax.ppermute(array, 'seq', pairs)  224 us
    ppermute x25, starting transfers between devices, shifted(): return lax.ppermute(array, 'seq', pairs)  182 us
    pallas_call x2, Pallas kernels, attention_backward(): pl.pallas_call(functools.partial(attention_backward_kernel, tile, left, e...  101 us
    dot_general x8, matrix products, dot_nn(): lax.dot_general(left, right, (((1,), (0,)), ((), ())), preferred_element_...  83.2 us
    dot_general x8, matrix products, dot_nt(): lax.dot_general(left, right, (((1,), (1,)), ((), ())), preferred_element_...  76.4 us
    dot_general x8, matrix products, dot_tn(): lax.dot_general(left, right, (((0,), (0,)), ((), ())), preferred_element_...  65.6 us
  transfers between devices with their start and end apart: 25, of which 8 were waited for; matrix products, arithmetic and copies ran while one was open for 7% of the time, Pallas kernels for 15%

profile of v1, /device:TPU:9, one launch (start us, length us, event | category | flops | bytes accessed | tf_op | source)
XLA Modules:
  0.0 1797.6 jit_solution(1305700196010071304)
XLA Ops:
  5.9 281.8 %gather_parameters.1 = (bf16[1152,4608]{1,0:T(8,128)(2,1)}, bf16[1152,4352]{1,0:T(8,128)(2,1)S(1)}, bf16[1152,4608]{1,0:T(8,128)(2,1)}, bf16[1152,4608]{1,0:T(8,...) custom-call(bf16[48,4608]{1,0:T(8,128)(2,1)S(1)} %get-tuple-element.327.refs_0_, ...), custom_call_target="tpu_custom_call" | custom-call | tf_op jit(solution)/shard_map/gather_parameters/pallas_call | solution.py:499
  323.8 49.4 %collective-permute-done = s32[160]{0:T(256)S(1)} collective-permute-done((s32[160]{0:T(256)S(1)}, s32[160]{0:T(256)S(1)}, u32[]{:S(2)}, u32[]{:S(2)}) %collective-permute-start) | collective-permute-done | bytes 672 | tf_op jit(solution)/shard_map/ppermute | solution.py:733
  373.3 24.5 %collective-permute-start.4 = (s32[256]{0:T(256)S(1)}, s32[256]{0:T(256)S(1)}, u32[]{:S(2)}, u32[]{:S(2)}) collective-permute-start(s32[256]{0:T(256)S(1)} %slice.365), channel_id=1, source_target_pairs={{2,0},{3,1},{4,2},{5,3},{6,4},{7,5},{8,6},{9,7},{10,8},{11,9},{12,... | collective-permute-start | bytes 3080 | tf_op jit(solution)/shard_map/ppermute | solution.py:733
  463.0 30.2 %attention_forward.2 = (bf16[480,1152]{1,0:T(8,128)(2,1)}, f32[480,128]{1,0:T(8,128)}) custom-call(s32[8]{0:T(128)} %stack.185.plan, bf16[480,1152]{1,0:T(8,128)(2,1)} %fusion.73.query, bf16[2336,2304]{1,0:T(8,128)(2,1)} %constant_dynamic-update-slice_fusion.window, s32[480,1]{1,0:T(8,128)} %copy.196.own_code, s32[4,1,768]{2,1,0:T(1,128)} %broadcast_in_dim.9.span_code), custom_call_target="tpu_custom_call" | custom-call | tf_op jit(solution)/shard_map/attention_forward/pallas_call | solution.py:187
  498.0 11.9 convolution_add_fusion.1
  510.0 12.4 fusion.143
  523.1 17.0 fusion.32
  543.3 25.9 %collective-permute-start.12 = (bf16[480,2304]{1,0:T(8,128)(2,1)S(1)}, bf16[480,2304]{1,0:T(8,128)(2,1)S(1)}, u32[]{:S(2)}, u32[]{:S(2)}) collective-permute-start(bf16[480,2304]{1,0:T(8,128)(2,1)S(1)} %fusion.38), channel_id=1, source_target_pairs={{0,1},{1,2},{2,3},{3,4},{4,5},{5,6},{6,7},{7,8},{8,9},{9,10},{10,1... | collective-permute-start | bytes 6635528 | tf_op jit(solution)/shard_map/ppermute | solution.py:733
  579.6 52.5 %collective-permute-done.10 = bf16[160,2304]{1,0:T(8,128)(2,1)S(1)} collective-permute-done((bf16[160,2304]{1,0:T(8,128)(2,1)S(1)}, bf16[160,2304]{1,0:T(8,128)(2,1)S(1)}, u32[]{:S(2)}, u32[]{:S(2)}) %collective-permute-start.10) | collective-permute-done | bytes 737312 | tf_op jit(solution)/shard_map/ppermute | solution.py:733
  634.5 31.6 %collective-permute-done.12 = bf16[480,2304]{1,0:T(8,128)(2,1)S(1)} collective-permute-done((bf16[480,2304]{1,0:T(8,128)(2,1)S(1)}, bf16[480,2304]{1,0:T(8,128)(2,1)S(1)}, u32[]{:S(2)}, u32[]{:S(2)}) %collective-permute-start.12) | collective-permute-done | bytes 2211872 | tf_op jit(solution)/shard_map/ppermute | solution.py:733
  674.1 29.9 %attention_forward.3 = (bf16[480,1152]{1,0:T(8,128)(2,1)}, f32[480,128]{1,0:T(8,128)}) custom-call(s32[8]{0:T(128)} %stack.185.plan, bf16[480,1152]{1,0:T(8,128)(2,1)} %fusion.72.query, bf16[2336,2304]{1,0:T(8,128)(2,1)} %constant_dynamic-update-slice_fusion.6.window, s32[480,1]{1,0:T(8,128)} %copy.196.own_code, s32[4,1,768]{2,1,0:T(1,128)} %broadcast_in_dim.9.span_code), custom_call_target="tpu_custom_call" | custom-call | tf_op jit(solution)/shard_map/attention_forward/pallas_call | solution.py:187
  709.0 12.1 convolution_add_fusion
  721.1 12.8 convert_reduce_fusion
  733.9 11.0 multiply_reduce_fusion
  751.4 50.4 %attention_backward.2 = (bf16[480,1152]{1,0:T(8,128)(2,1)}, bf16[2336,2304]{1,0:T(8,128)(2,1)}) custom-call(s32[8]{0:T(128)} %stack.185.plan, bf16[480,1152]{1,0:T(8,128)(2,1)} %fusion.72.query, bf16[2336,2304]{1,0:T(8,128)(2,1)} %constant_dynamic-update-slice_fusion.6.window, bf16[480,1152]{1,0:T(8,128)(2,1)} %convolution_convert_fusion.9.grad, ...), custom_call_target="tpu_custom_call" | custom-call | tf_op jit(solution)/shard_map/attention_backward/pallas_call | solution.py:207
  812.0 11.2 fusion
  823.2 44.6 %collective-permute-start.15 = (bf16[480,2304]{1,0:T(8,128)(2,1)}, bf16[480,2304]{1,0:T(8,128)(2,1)}, u32[]{:S(2)}, u32[]{:S(2)}) collective-permute-start(bf16[480,2304]{1,0:T(8,128)(2,1)} %get-tuple-element.271), channel_id=1, source_target_pairs={{1,0},{2,1},{3,2},{4,3},{5,4},{6,5},{7,6},{8,7},{9,8},{10,9},{11,1... | collective-permute-start | bytes 6635528 | tf_op jit(solution)/shard_map/ppermute | solution.py:733
  882.3 13.7 fusion.46
  896.0 10.4 convolution_convert_fusion.1
  920.0 39.2 %collective-permute-done.17 = bf16[160,2304]{1,0:T(8,128)(2,1)} collective-permute-done((bf16[160,2304]{1,0:T(8,128)(2,1)}, bf16[160,2304]{1,0:T(8,128)(2,1)}, u32[]{:S(2)}, u32[]{:S(2)}) %collective-permute-start.17) | collective-permute-done | bytes 737312 | tf_op jit(solution)/shard_map/ppermute | solution.py:733
  959.3 40.3 %collective-permute-done.19 = bf16[256,2304]{1,0:T(8,128)(2,1)S(1)} collective-permute-done((bf16[256,2304]{1,0:T(8,128)(2,1)}, bf16[256,2304]{1,0:T(8,128)(2,1)S(1)}, u32[]{:S(2)}, u32[]{:S(2)}) %collective-permute-start.19) | collective-permute-done | bytes 1179680 | tf_op jit(solution)/shard_map/ppermute | solution.py:733
  1004.1 9.1 multiply_reduce_fusion.1
  1015.4 13.9 convert_reduce_fusion.1
  1029.3 11.9 convolution_convert_fusion.2
  1041.3 9.5 multiply_reduce_fusion.2
  1058.5 50.4 %attention_backward.3 = (bf16[480,1152]{1,0:T(8,128)(2,1)}, bf16[2336,2304]{1,0:T(8,128)(2,1)}) custom-call(s32[8]{0:T(128)} %stack.185.plan, bf16[480,1152]{1,0:T(8,128)(2,1)} %fusion.73.query, bf16[2336,2304]{1,0:T(8,128)(2,1)} %constant_dynamic-update-slice_fusion.window, bf16[480,1152]{1,0:T(8,128)(2,1)} %convolution_convert_fusion.8.grad, ...), custom_call_target="tpu_custom_call" | custom-call | tf_op jit(solution)/shard_map/attention_backward/pallas_call | solution.py:207
  1135.9 18.3 %collective-permute-start.20 = (bf16[480,2304]{1,0:T(8,128)(2,1)}, bf16[480,2304]{1,0:T(8,128)(2,1)}, u32[]{:S(2)}, u32[]{:S(2)}) collective-permute-start(bf16[480,2304]{1,0:T(8,128)(2,1)} %get-tuple-element.268), channel_id=1, source_target_pairs={{1,0},{2,1},{3,2},{4,3},{5,4},{6,5},{7,6},{8,7},{9,8},{10,9},{11,1... | collective-permute-start | bytes 6635528 | tf_op jit(solution)/shard_map/ppermute | solution.py:733
  1186.7 264.8 %reduce_gradients.3 = (f32[48,4608]{1,0:T(8,128)}, f32[48,4352]{1,0:T(8,128)}, f32[48,4608]{1,0:T(8,128)}, bf16[1152,2304]{1,0:T(8,128)(2,1)}, bf16[1152,2176]{1,0:T(8,128)(2,1)}, /*index=5*/bf16[1152,2304]{1,0:T(8,128)(2,1)}) custom-call(bf16[1152,4608]{1,0:T(8,128)(2,1)} %pad_maximum_fusion.1.refs_0_, bf16[1152,4352]{1,0:T(8,128)(2,1)} %scatter.14.refs_1_, ...), custom_call_target="tpu_custom_call" | custom-call | tf_op jit(solution)/shard_map/reduce_gradients/pallas_call | solution.py:700
  1454.7 38.7 %all-reduce.19 = (f32[1,4304]{1,0:T(1,128)S(1)}, f32[1,4304]{1,0:T(1,128)S(1)}) all-reduce(f32[1,4304]{1,0:T(1,128)S(1)} %stack.228, f32[1,4304]{1,0:T(1,128)S(1)} %stack.227), channel_id=1, replica_groups=mesh['dp'=2,'seq'=16] {'dp','seq'}, use_global_device_ids=true, to_apply=%region_41.42 | all-reduce | flops 8608 | bytes 68864 | tf_op jit(solution)/shard_map/psum | solution.py:904
  1522.5 10.0 fusion.70
  1551.1 9.9 pad_maximum_fusion.refs_0_
  1561.0 195.6 %reduce_gradients.2 = (f32[48,4608]{1,0:T(8,128)}, f32[48,4352]{1,0:T(8,128)}, f32[48,4608]{1,0:T(8,128)}, bf16[1152,2304]{1,0:T(8,128)(2,1)}, bf16[1152,2176]{1,0:T(8,128)(2,1)}, /*index=5*/bf16[1152,2304]{1,0:T(8,128)(2,1)}) custom-call(bf16[1152,4608]{1,0:T(8,128)(2,1)} %pad_maximum_fusion.refs_0_, bf16[1152,4352]{1,0:T(8,128)(2,1)} %scatter.11.refs_1_, ...), custom_call_target="tpu_custom_call" | custom-call | tf_op jit(solution)/shard_map/reduce_gradients/pallas_call | solution.py:700
  (471 shorter events, 337.0 us)
Async XLA Ops:
  303.9 136.7 %collective-permute-start.6 = (bf16[480,2304]{1,0:T(8,128)(2,1)}, bf16[480,2304]{1,0:T(8,128)(2,1)}, u32[]{:S(2)}, u32[]{:S(2)}) collective-permute-start(bf16[480,2304]{1,0:T(8,128)(2,1)} %fusion.39), channel_id=1, source_target_pairs={{0,2},{1,3},{2,4},{3,5},{4,6},{5,7},{6,8},{7,9},{8,10},{9,11},{10,... | collective-permute-start | bytes 6635528 | tf_op jit(solution)/shard_map/ppermute | solution.py:733
  306.1 137.9 %collective-permute-start.7 = (bf16[480,2304]{1,0:T(8,128)(2,1)}, bf16[480,2304]{1,0:T(8,128)(2,1)}, u32[]{:S(2)}, u32[]{:S(2)}) collective-permute-start(bf16[480,2304]{1,0:T(8,128)(2,1)} %fusion.39), channel_id=1, source_target_pairs={{0,1},{1,2},{2,3},{3,4},{4,5},{5,6},{6,7},{7,8},{8,9},{9,10},{10,1... | collective-permute-start | bytes 6635528 | tf_op jit(solution)/shard_map/ppermute | solution.py:733
  312.2 126.3 %collective-permute-start.5 = (bf16[160,2304]{1,0:T(8,128)(2,1)}, bf16[160,2304]{1,0:T(8,128)(2,1)}, u32[]{:S(2)}, u32[]{:S(2)}) collective-permute-start(bf16[160,2304]{1,0:T(8,128)(2,1)} %slice.485), channel_id=1, source_target_pairs={{0,3},{1,4},{2,5},{3,6},{4,7},{5,8},{6,9},{7,10},{8,11},{9,12},{10... | collective-permute-start | bytes 2211848 | tf_op jit(solution)/shard_map/ppermute | solution.py:733
  315.3 90.1 %collective-permute-start.1 = (s32[480]{0:T(512)}, s32[480]{0:T(512)S(1)}, u32[]{:S(2)}, u32[]{:S(2)}) collective-permute-start(s32[480]{0:T(512)} %convert_add_fusion.1), channel_id=1, source_target_pairs={{0,2},{1,3},{2,4},{3,5},{4,6},{5,7},{6,8},{7,9},{8,10},{9,11},{10,... | collective-permute-start | bytes 5768 | tf_op jit(solution)/shard_map/ppermute | solution.py:733
  319.5 53.7 %collective-permute-start = (s32[160]{0:T(256)S(1)}, s32[160]{0:T(256)S(1)}, u32[]{:S(2)}, u32[]{:S(2)}) collective-permute-start(s32[160]{0:T(256)S(1)} %slice.364), channel_id=1, source_target_pairs={{0,3},{1,4},{2,5},{3,6},{4,7},{5,8},{6,9},{7,10},{8,11},{9,12},{10... | collective-permute-start | bytes 1928 | tf_op jit(solution)/shard_map/ppermute | solution.py:733
  373.3 25.5 %collective-permute-start.4 = (s32[256]{0:T(256)S(1)}, s32[256]{0:T(256)S(1)}, u32[]{:S(2)}, u32[]{:S(2)}) collective-permute-start(s32[256]{0:T(256)S(1)} %slice.365), channel_id=1, source_target_pairs={{2,0},{3,1},{4,2},{5,3},{6,4},{7,5},{8,6},{9,7},{10,8},{11,9},{12,... | collective-permute-start | bytes 3080 | tf_op jit(solution)/shard_map/ppermute | solution.py:733
  398.8 17.2 collective-permute-start.2
  405.5 12.5 collective-permute-start.3
  416.0 41.5 %collective-permute-start.8 = (bf16[480,2304]{1,0:T(8,128)(2,1)}, bf16[480,2304]{1,0:T(8,128)(2,1)}, u32[]{:S(2)}, u32[]{:S(2)}) collective-permute-start(bf16[480,2304]{1,0:T(8,128)(2,1)} %fusion.39), channel_id=1, source_target_pairs={{1,0},{2,1},{3,2},{4,3},{5,4},{6,5},{7,6},{8,7},{9,8},{10,9},{11,1... | collective-permute-start | bytes 6635528 | tf_op jit(solution)/shard_map/ppermute | solution.py:733
  418.0 42.6 %collective-permute-start.9 = (bf16[256,2304]{1,0:T(8,128)(2,1)}, bf16[256,2304]{1,0:T(8,128)(2,1)}, u32[]{:S(2)}, u32[]{:S(2)}) collective-permute-start(bf16[256,2304]{1,0:T(8,128)(2,1)} %slice.486), channel_id=1, source_target_pairs={{2,0},{3,1},{4,2},{5,3},{6,4},{7,5},{8,6},{9,7},{10,8},{11,9},{12,... | collective-permute-start | bytes 3538952 | tf_op jit(solution)/shard_map/ppermute | solution.py:733
  522.4 181.7 %copy-start.9 = (f32[480,1152]{1,0:T(8,128)}, f32[480,1152]{1,0:T(8,128)S(1)}, u32[]{:S(2)}) copy-start(f32[480,1152]{1,0:T(8,128)S(1)} %get-tuple-element.316) | copy-start | bytes 6635524
  540.4 92.6 %collective-permute-start.11 = (bf16[480,2304]{1,0:T(8,128)(2,1)S(1)}, bf16[480,2304]{1,0:T(8,128)(2,1)S(1)}, u32[]{:S(2)}, u32[]{:S(2)}) collective-permute-start(bf16[480,2304]{1,0:T(8,128)(2,1)S(1)} %fusion.38), channel_id=1, source_target_pairs={{0,2},{1,3},{2,4},{3,5},{4,6},{5,7},{6,8},{7,9},{8,10},{9,11},{10,... | collective-permute-start | bytes 6635528 | tf_op jit(solution)/shard_map/ppermute | solution.py:733
  543.3 122.8 %collective-permute-start.12 = (bf16[480,2304]{1,0:T(8,128)(2,1)S(1)}, bf16[480,2304]{1,0:T(8,128)(2,1)S(1)}, u32[]{:S(2)}, u32[]{:S(2)}) collective-permute-start(bf16[480,2304]{1,0:T(8,128)(2,1)S(1)} %fusion.38), channel_id=1, source_target_pairs={{0,1},{1,2},{2,3},{3,4},{4,5},{5,6},{6,7},{7,8},{8,9},{9,10},{10,1... | collective-permute-start | bytes 6635528 | tf_op jit(solution)/shard_map/ppermute | solution.py:733
  569.2 62.9 %collective-permute-start.10 = (bf16[160,2304]{1,0:T(8,128)(2,1)S(1)}, bf16[160,2304]{1,0:T(8,128)(2,1)S(1)}, u32[]{:S(2)}, u32[]{:S(2)}) collective-permute-start(bf16[160,2304]{1,0:T(8,128)(2,1)S(1)} %slice.500), channel_id=1, source_target_pairs={{0,3},{1,4},{2,5},{3,6},{4,7},{5,8},{6,9},{7,10},{8,11},{9,12},{10... | collective-permute-start | bytes 2211848 | tf_op jit(solution)/shard_map/ppermute | solution.py:733
  571.8 99.6 %collective-permute-start.13 = (bf16[480,2304]{1,0:T(8,128)(2,1)S(1)}, bf16[480,2304]{1,0:T(8,128)(2,1)S(1)}, u32[]{:S(2)}, u32[]{:S(2)}) collective-permute-start(bf16[480,2304]{1,0:T(8,128)(2,1)S(1)} %fusion.38), channel_id=1, source_target_pairs={{1,0},{2,1},{3,2},{4,3},{5,4},{6,5},{7,6},{8,7},{9,8},{10,9},{11,1... | collective-permute-start | bytes 6635528 | tf_op jit(solution)/shard_map/ppermute | solution.py:733
  573.9 99.1 %collective-permute-start.14 = (bf16[256,2304]{1,0:T(8,128)(2,1)S(1)}, bf16[256,2304]{1,0:T(8,128)(2,1)S(1)}, u32[]{:S(2)}, u32[]{:S(2)}) collective-permute-start(bf16[256,2304]{1,0:T(8,128)(2,1)S(1)} %slice.501), channel_id=1, source_target_pairs={{2,0},{3,1},{4,2},{5,3},{6,4},{7,5},{8,6},{9,7},{10,8},{11,9},{12,... | collective-permute-start | bytes 3538952 | tf_op jit(solution)/shard_map/ppermute | solution.py:733
  812.0 70.3 %copy-start.15 = (f32[480,1152]{1,0:T(8,128)S(1)}, f32[480,1152]{1,0:T(8,128)}, u32[]{:S(2)}) copy-start(f32[480,1152]{1,0:T(8,128)} %copy-done.14) | copy-start | bytes 6635524
  812.0 70.3 %copy-start.84 = (f32[1152]{0:T(1024)S(1)}, f32[1152]{0:T(1024)}, u32[]{:S(2)}) copy-start(f32[1152]{0:T(1024)} %get-tuple-element.213) | copy-start | bytes 13828
  823.2 176.3 %collective-permute-start.15 = (bf16[480,2304]{1,0:T(8,128)(2,1)}, bf16[480,2304]{1,0:T(8,128)(2,1)}, u32[]{:S(2)}, u32[]{:S(2)}) collective-permute-start(bf16[480,2304]{1,0:T(8,128)(2,1)} %get-tuple-element.271), channel_id=1, source_target_pairs={{1,0},{2,1},{3,2},{4,3},{5,4},{6,5},{7,6},{8,7},{9,8},{10,9},{11,1... | collective-permute-start | bytes 6635528 | tf_op jit(solution)/shard_map/ppermute | solution.py:733
  867.9 131.7 %collective-permute-start.16 = (bf16[480,2304]{1,0:T(8,128)(2,1)}, bf16[480,2304]{1,0:T(8,128)(2,1)}, u32[]{:S(2)}, u32[]{:S(2)}) collective-permute-start(bf16[480,2304]{1,0:T(8,128)(2,1)} %get-tuple-element.273), channel_id=1, source_target_pairs={{2,0},{3,1},{4,2},{5,3},{6,4},{7,5},{8,6},{9,7},{10,8},{11,9},{12,... | collective-permute-start | bytes 6635528 | tf_op jit(solution)/shard_map/ppermute | solution.py:733
  869.8 129.8 %collective-permute-start.18 = (bf16[480,2304]{1,0:T(8,128)(2,1)}, bf16[480,2304]{1,0:T(8,128)(2,1)}, u32[]{:S(2)}, u32[]{:S(2)}) collective-permute-start(bf16[480,2304]{1,0:T(8,128)(2,1)} %get-tuple-element.272), channel_id=1, source_target_pairs={{0,1},{1,2},{2,3},{3,4},{4,5},{5,6},{6,7},{7,8},{8,9},{9,10},{10,1... | collective-permute-start | bytes 6635528 | tf_op jit(solution)/shard_map/ppermute | solution.py:733
  873.3 126.2 %collective-permute-start.19 = (bf16[256,2304]{1,0:T(8,128)(2,1)}, bf16[256,2304]{1,0:T(8,128)(2,1)S(1)}, u32[]{:S(2)}, u32[]{:S(2)}) collective-permute-start(bf16[256,2304]{1,0:T(8,128)(2,1)} %slice.429), channel_id=1, source_target_pairs={{0,2},{1,3},{2,4},{3,5},{4,6},{5,7},{6,8},{7,9},{8,10},{9,11},{10,... | collective-permute-start | bytes 3538952 | tf_op jit(solution)/shard_map/ppermute | solution.py:733
  877.7 81.5 %collective-permute-start.17 = (bf16[160,2304]{1,0:T(8,128)(2,1)}, bf16[160,2304]{1,0:T(8,128)(2,1)}, u32[]{:S(2)}, u32[]{:S(2)}) collective-permute-start(bf16[160,2304]{1,0:T(8,128)(2,1)} %slice.427), channel_id=1, source_target_pairs={{3,0},{4,1},{5,2},{6,3},{7,4},{8,5},{9,6},{10,7},{11,8},{12,9},{13... | collective-permute-start | bytes 2211848 | tf_op jit(solution)/shard_map/ppermute | solution.py:733
  920.0 84.0 %copy-start.10 = (f32[480,1152]{1,0:T(8,128)S(1)}, f32[480,1152]{1,0:T(8,128)}, u32[]{:S(2)}) copy-start(f32[480,1152]{1,0:T(8,128)} %copy-done.9) | copy-start | bytes 6635524
  920.0 84.0 %copy-start.38 = (bf16[480,1152]{1,0:T(8,128)(2,1)S(1)}, bf16[480,1152]{1,0:T(8,128)(2,1)}, u32[]{:S(2)}) copy-start(bf16[480,1152]{1,0:T(8,128)(2,1)} %get-tuple-element.95) | copy-start | bytes 3317764
  1128.5 49.5 %copy-start.22 = (bf16[1152,1152]{1,0:T(8,128)(2,1)S(1)}, bf16[1152,1152]{1,0:T(8,128)(2,1)}, u32[]{:S(2)}) copy-start(bf16[1152,1152]{1,0:T(8,128)(2,1)} %convolution_convert_fusion.6) | copy-start | bytes 7962628
  1135.9 381.6 %collective-permute-start.20 = (bf16[480,2304]{1,0:T(8,128)(2,1)}, bf16[480,2304]{1,0:T(8,128)(2,1)}, u32[]{:S(2)}, u32[]{:S(2)}) collective-permute-start(bf16[480,2304]{1,0:T(8,128)(2,1)} %get-tuple-element.268), channel_id=1, source_target_pairs={{1,0},{2,1},{3,2},{4,3},{5,4},{6,5},{7,6},{8,7},{9,8},{10,9},{11,1... | collective-permute-start | bytes 6635528 | tf_op jit(solution)/shard_map/ppermute | solution.py:733
  1154.3 363.3 %collective-permute-start.21 = (bf16[480,2304]{1,0:T(8,128)(2,1)}, bf16[480,2304]{1,0:T(8,128)(2,1)}, u32[]{:S(2)}, u32[]{:S(2)}) collective-permute-start(bf16[480,2304]{1,0:T(8,128)(2,1)} %get-tuple-element.270), channel_id=1, source_target_pairs={{2,0},{3,1},{4,2},{5,3},{6,4},{7,5},{8,6},{9,7},{10,8},{11,9},{12,... | collective-permute-start | bytes 6635528 | tf_op jit(solution)/shard_map/ppermute | solution.py:733
  1158.5 359.0 %collective-permute-start.23 = (bf16[480,2304]{1,0:T(8,128)(2,1)}, bf16[480,2304]{1,0:T(8,128)(2,1)}, u32[]{:S(2)}, u32[]{:S(2)}) collective-permute-start(bf16[480,2304]{1,0:T(8,128)(2,1)} %get-tuple-element.269), channel_id=1, source_target_pairs={{0,1},{1,2},{2,3},{3,4},{4,5},{5,6},{6,7},{7,8},{8,9},{9,10},{10,1... | collective-permute-start | bytes 6635528 | tf_op jit(solution)/shard_map/ppermute | solution.py:733
  1162.5 355.1 %collective-permute-start.24 = (bf16[256,2304]{1,0:T(8,128)(2,1)}, bf16[256,2304]{1,0:T(8,128)(2,1)}, u32[]{:S(2)}, u32[]{:S(2)}) collective-permute-start(bf16[256,2304]{1,0:T(8,128)(2,1)} %slice.435), channel_id=1, source_target_pairs={{0,2},{1,3},{2,4},{3,5},{4,6},{5,7},{6,8},{7,9},{8,10},{9,11},{10,... | collective-permute-start | bytes 3538952 | tf_op jit(solution)/shard_map/ppermute | solution.py:733
  1169.1 348.4 %collective-permute-start.22 = (bf16[160,2304]{1,0:T(8,128)(2,1)}, bf16[160,2304]{1,0:T(8,128)(2,1)}, u32[]{:S(2)}, u32[]{:S(2)}) collective-permute-start(bf16[160,2304]{1,0:T(8,128)(2,1)} %slice.433), channel_id=1, source_target_pairs={{3,0},{4,1},{5,2},{6,3},{7,4},{8,5},{9,6},{10,7},{11,8},{12,9},{13... | collective-permute-start | bytes 2211848 | tf_op jit(solution)/shard_map/ppermute | solution.py:733
  1451.5 43.0 %copy-start.50 = (bf16[2,4304]{1,0:T(2,128)(2,1)S(1)}, bf16[2,4304]{1,0:T(2,128)(2,1)}, u32[]{:S(2)}) copy-start(bf16[2,4304]{1,0:T(2,128)(2,1)} %param.41) | copy-start | bytes 51652
  (105 other events, 889.1 us)

commit v2 on v1

v2 whole, which is shorter than its diff:
```python
import functools
import math

import jax
import jax.numpy as jnp
from jax import lax
from jax.experimental import pallas as pl
from jax.experimental.pallas import tpu as pltpu
from jax.sharding import PartitionSpec as P

HEADS = 16
IMG = 729
STEP = 8

eps_norm = 1e-06
beta_first = 0.9
beta_second = 0.95
learn_rate = 0.025
weight_decay = 0.1
eps_adam = 1e-08
span_len = 768
lane_pair = 256
masked_score = -1e30
mib = 2**20


def head_lanes(head, head_size, width):
    low = head * head_size
    first = jnp.minimum(low // 128 * 128, width - lane_pair)
    lanes = lax.broadcasted_iota(jnp.int32, (1, lane_pair), 1)
    inside = (lanes >= low - first) & (lanes < low - first + head_size)
    keys = pl.ds(pl.multiple_of(first, 128), lane_pair)
    values = pl.ds(pl.multiple_of(first + width, 128), lane_pair)
    return keys, values, inside


def dot_nn(left, right):
    return lax.dot_general(left, right, (((1,), (0,)), ((), ())), preferred_element_type=jnp.float32)


def dot_nt(left, right):
    return lax.dot_general(left, right, (((1,), (1,)), ((), ())), preferred_element_type=jnp.float32)


def dot_tn(left, right):
    return lax.dot_general(left, right, (((0,), (0,)), ((), ())), preferred_element_type=jnp.float32)


def attention_forward_kernel(
    tile, left, exp_scale, plan, query, window, own_code, span_code, out, lse_out, bias, mix
):
    tok, width = query.shape
    head_size = width // HEADS

    def one_span(tile_index, which):
        offset = pl.multiple_of(plan[4 * tile_index + which], 16)
        image = plan[4 * tile_index + 2 + which]
        rows = pl.ds(pl.multiple_of(tile_index * tile, 16), tile)
        own_rows = pl.ds(pl.multiple_of(left + tile_index * tile, 16), tile)
        span = pl.ds(offset, span_len)
        code = own_code[rows, :]
        row_image = jnp.maximum(code, -code)
        mine = row_image == image
        bias[...] = jnp.where(row_image == span_code[2 * tile_index + which], 0.0, masked_score)
        self_bias = jnp.where(code < 0, 0.0, masked_score)
        lse_lane = lax.broadcasted_iota(jnp.int32, (tile, lse_out.shape[1]), 1)

        def one_head(head, carry):
            lanes, value_lanes, inside = head_lanes(head, head_size, width)
            queries = jnp.where(inside, query[rows, lanes], 0)
            scores = dot_nt(queries, window[span, lanes]) * exp_scale + bias[...]
            own_key = window[own_rows, lanes].astype(jnp.float32)
            own_value = window[own_rows, value_lanes].astype(jnp.float32)
            self_score = (
                jnp.sum(queries.astype(jnp.float32) * own_key, axis=1, keepdims=True) * exp_scale
                + self_bias
            )
            top = jnp.maximum(jnp.max(scores, axis=1, keepdims=True), self_score)
            powers = jnp.exp2(scores - top)
            self_power = jnp.exp2(self_score - top)
            total = jnp.sum(powers, axis=1, keepdims=True) + self_power
            mixed = dot_nn(powers.astype(jnp.bfloat16), window[span, value_lanes])
            mixed = (mixed + self_power * own_value) / total
            mix[rows, lanes] = jnp.where(inside & mine, mixed, mix[rows, lanes])
            lse_out[rows, :] = jnp.where(
                (lse_lane == head) & mine, top + jnp.log2(total), lse_out[rows, :]
            )
            return carry

        lax.fori_loop(0, HEADS, one_head, 0, unroll=2)

    def one_tile(tile_index, carry):
        one_span(tile_index, 0)

        @pl.when(plan[4 * tile_index + 2] != plan[4 * tile_index + 3])
        def _():
            one_span(tile_index, 1)

        return carry

    lax.fori_loop(0, tok // tile, one_tile, 0)
    out[...] = mix[...].astype(out.dtype)


def attention_backward_kernel(
    tile, left, exp_scale, plan, query, window, grad, lse_in, own_code, span_code,
    grad_query, grad_window, bias, acc_query, acc_window,
):
    tok, width = query.shape
    head_size = width // HEADS
    scale = 1.0 / math.sqrt(head_size)
    acc_query[...] = jnp.zeros_like(acc_query)
    acc_window[...] = jnp.zeros_like(acc_window)

    def one_span(tile_index, which):
        offset = pl.multiple_of(plan[4 * tile_index + which], 16)
        image = plan[4 * tile_index + 2 + which]
        rows = pl.ds(pl.multiple_of(tile_index * tile, 16), tile)
        own_rows = pl.ds(pl.multiple_of(left + tile_index * tile, 16), tile)
        span = pl.ds(offset, span_len)
        code = own_code[rows, :]
        row_image = jnp.maximum(code, -code)
        mine = row_image == image
        bias[...] = jnp.where(
            mine & (span_code[2 * tile_index + which] == image), 0.0, masked_score
        )
        self_bias = jnp.where((code < 0) & mine, 0.0, masked_score)
        lse_lane = lax.broadcasted_iota(jnp.int32, (tile, lse_in.shape[1]), 1)

        def one_head(head, carry):
            lanes, value_lanes, inside = head_lanes(head, head_size, width)
            queries = jnp.where(inside, query[rows, lanes], 0)
            grads = jnp.where(inside, grad[rows, lanes], 0)
            lse = jnp.sum(jnp.where(lse_lane == head, lse_in[rows, :], 0.0), axis=1, keepdims=True)
            keys = window[span, lanes]
            own_key = window[own_rows, lanes].astype(jnp.float32)
            own_value = window[own_rows, value_lanes].astype(jnp.float32)
            queries_wide = queries.astype(jnp.float32)
            grads_wide = grads.astype(jnp.float32)
            prob = jnp.exp2(dot_nt(queries, keys) * exp_scale + bias[...] - lse)
            self_score = jnp.sum(queries_wide * own_key, axis=1, keepdims=True) * exp_scale
            self_prob = jnp.exp2(self_score + self_bias - lse)
            grad_prob = dot_nt(grads, window[span, value_lanes])
            self_grad = jnp.sum(grads_wide * own_value, axis=1, keepdims=True)
            inner = jnp.sum(prob * grad_prob, axis=1, keepdims=True) + self_prob * self_grad
            grad_scores = (prob * (grad_prob - inner)).astype(jnp.bfloat16)
            self_grad_score = self_prob * (self_grad - inner)
            part = dot_nn(grad_scores, keys) + self_grad_score * own_key
            acc_query[rows, lanes] += jnp.where(inside, part, 0.0)
            acc_window[span, lanes] += dot_tn(grad_scores, queries)
            acc_window[span, value_lanes] += dot_tn(prob.astype(jnp.bfloat16), grads)
            acc_window[own_rows, lanes] += self_grad_score * queries_wide
            acc_window[own_rows, value_lanes] += self_prob * grads_wide
            return carry

        lax.fori_loop(0, HEADS, one_head, 0, unroll=2)

    def one_tile(tile_index, carry):
        one_span(tile_index, 0)

        @pl.when(plan[4 * tile_index + 2] != plan[4 * tile_index + 3])
        def _():
            one_span(tile_index, 1)

        return carry

    lax.fori_loop(0, tok // tile, one_tile, 0)
    grad_query[...] = (acc_query[...] * scale).astype(grad_query.dtype)
    step = 16

    def narrow(index, carry):
        rows = pl.ds(pl.multiple_of(index * step, step), step)
        grad_window[rows, :width] = (acc_window[rows, :width] * scale).astype(grad_window.dtype)
        grad_window[rows, width:] = acc_window[rows, width:].astype(grad_window.dtype)
        return carry

    lax.fori_loop(0, acc_window.shape[0] // step, narrow, 0)


def in_vmem():
    return pl.BlockSpec(memory_space=pltpu.VMEM)


def attention_forward(tile, left, plan, query, window, own_code, span_code):
    tok, width = query.shape
    exp_scale = math.log2(math.e) / math.sqrt(width // HEADS)
    return pl.pallas_call(
        functools.partial(attention_forward_kernel, tile, left, exp_scale),
        name="attention_forward",
        out_shape=[
            jax.ShapeDtypeStruct((tok, width), jnp.bfloat16),
            jax.ShapeDtypeStruct((tok, 128), jnp.float32),
        ],
        in_specs=[pl.BlockSpec(memory_space=pltpu.SMEM)] + [in_vmem()] * 4,
        out_specs=[in_vmem()] * 2,
        scratch_shapes=[
            pltpu.VMEM((tile, span_len), jnp.float32),
            pltpu.VMEM((tok, width), jnp.float32),
        ],
        compiler_params=pltpu.CompilerParams(vmem_limit_bytes=60 * mib),
    )(plan, query, window, own_code, span_code)


def attention_backward(tile, left, plan, query, window, grad, lse, own_code, span_code):
    tok, width = query.shape
    exp_scale = math.log2(math.e) / math.sqrt(width // HEADS)
    return pl.pallas_call(
        functools.partial(attention_backward_kernel, tile, left, exp_scale),
        name="attention_backward",
        out_shape=[
            jax.ShapeDtypeStruct((tok, width), jnp.bfloat16),
            jax.ShapeDtypeStruct(window.shape, jnp.bfloat16),
        ],
        in_specs=[pl.BlockSpec(memory_space=pltpu.SMEM)] + [in_vmem()] * 6,
        out_specs=[in_vmem()] * 2,
        scratch_shapes=[
            pltpu.VMEM((tile, span_len), jnp.float32),
            pltpu.VMEM((tok, width), jnp.float32),
            pltpu.VMEM(window.shape, jnp.float32),
        ],
        compiler_params=pltpu.CompilerParams(vmem_limit_bytes=62 * mib),
    )(plan, query, window, grad, lse, own_code, span_code)


def attention_plan(tile, left, right, own_ids, own_mask, window_ids, window_mask, place, places):
    tok = own_ids.shape[0]
    window_len = left + tok + right
    room = jnp.minimum(window_len, left + (places - place) * tok) - span_len
    position = jnp.arange(window_len)
    present = (position >= left - place * tok) & (position < left + (places - place) * tok)
    floor_ids = jnp.where(position < left, -1, window_ids + 0)
    ids = jnp.where(present, window_ids, floor_ids)
    codes = jnp.where((window_mask > 0) & present, window_ids + 1, 0)
    plans, spans = [], []
    for index in range(tok // tile):
        images = (own_ids[index * tile], own_ids[(index + 1) * tile - 1])
        offsets = []
        for image in images:
            start = jnp.sum((ids < image) & (position < left + tok)).astype(jnp.int32)
            offset = jnp.minimum(start // 16 * 16, room)
            offsets.append(offset)
            spans.append(lax.dynamic_slice(codes, (offset,), (span_len,)))
        plans += offsets + [image + 1 for image in images]
    plan = jnp.stack(plans).astype(jnp.int32)
    own_code = jnp.where(own_mask > 0, own_ids + 1, -(own_ids + 1)).astype(jnp.int32)[:, None]
    return plan, own_code, jnp.stack(spans)[:, None, :].astype(jnp.int32)


class Layout:
    def __init__(self, groups, seats, model_width):
        self.rows = model_width // (groups * seats)
        self.members = 2
        while self.members * self.rows % 16:
            self.members *= 2
        self.sides = self.members // 2
        self.lines = seats // self.members
        self.slab = self.members * self.rows
        self.padded = -(-self.rows // 16) * 16
        self.near = model_width // groups
        self.model_width = model_width

    def blocks(self, one_block):
        return 2 if one_block else 2 * self.sides

    def columns(self, columns, one_block):
        unit = 128 * self.blocks(one_block)
        return -(-columns // unit) * unit


class Mail:
    def __init__(self, layout, send, recv, slots):
        self.layout, self.send_sems, self.recv_sems, self.slots = layout, send, recv, slots
        self.group = lax.axis_index("dp")
        seat = lax.axis_index("seq")
        self.line = seat // layout.members
        self.member = seat % layout.members
        self.side = self.member // 2
        self.core = self.member % 2
        self.started = {}

    def at(self, group=None, line=None, side=None, core=None):
        group = self.group if group is None else group
        line = self.line if line is None else line
        side = self.side if side is None else side
        core = self.core if core is None else core
        return (group, line * self.layout.members + side * 2 + core)

    def copy(self, slot, source, target, device, shift=0):
        index = self.slots[slot] + shift
        return pltpu.make_async_remote_copy(
            src_ref=source,
            dst_ref=target,
            send_sem=self.send_sems.at[index],
            recv_sem=self.recv_sems.at[index],
            device_id=device,
            device_id_type=pl.DeviceIdType.MESH,
        )

    def send(self, slot, source, target, device, when=None):
        copy = self.copy(slot, source, target, device)
        self.started[slot] = (copy, when)
        guarded(when, copy.start)

    def wait(self, slot, target, shift=0):
        self.copy(slot, target, target, self.at(core=1 - self.core), shift).wait_recv()

    def settle(self, slot):
        copy, when = self.started.pop(slot)
        guarded(when, copy.wait_send)

    def finish(self):
        for slot in list(self.started):
            self.settle(slot)


class Desk:
    def __init__(self, mail, index, local):
        self.mail, self.index, self.local_sems = mail, index, local
        self.group, self.line, self.member = mail.group, mail.line, mail.member
        self.side, self.core, self.at = mail.side, mail.core, mail.at

    def send(self, slot, source, target, device, when=None):
        self.mail.send((self.index, slot), source, target, device, when)

    def wait(self, slot, target, shift=0):
        self.mail.wait((self.index, slot), target, shift)

    def settle(self, slot):
        self.mail.settle((self.index, slot))

    def local(self, number, source, target):
        return pltpu.make_async_copy(source, target, self.local_sems.at[number])


class Work:
    def __init__(self, steps, ins, outs, scratch, slots, local):
        self.steps, self.ins, self.outs, self.scratch = steps, ins, outs, scratch
        self.slots, self.local = slots, local


def guarded(when, action):
    if when is None:
        action()
    else:
        pl.when(when)(action)


def all_of(*conditions):
    kept = [condition for condition in conditions if condition is not None]
    return functools.reduce(jnp.logical_and, kept) if kept else None


def run_steps(works, turns):
    queue = []
    for index, (work, first) in enumerate(zip(works, turns)):
        next(work)
        queue.append((first[0], index, 0))
    while queue:
        turn, index, done = min(queue)
        queue.remove((turn, index, done))
        try:
            next(works[index])
        except StopIteration:
            continue
        done += 1
        listed = turns[index]
        queue.append((listed[done] if done < len(listed) else turn + 1, index, done))


def anywhere():
    return pl.BlockSpec(memory_space=pl.ANY)


def exchange(name, layout, works, starts, megabytes, common=()):
    slots = [(index, slot) for index, work in enumerate(works) for slot in work.slots]
    numbers = {slot: index for index, slot in enumerate(slots)}
    ins = [entry for work in works for entry in work.ins]
    outs = [entry for work in works for entry in work.outs]
    scratch = [entry for work in works for entry in work.scratch]

    def kernel(*refs):
        refs = list(refs)

        def take(count):
            taken = refs[:count]
            del refs[:count]
            return taken

        in_refs = [take(len(work.ins)) for work in works]
        out_refs = [take(len(work.outs)) for work in works]
        scratch_refs = [take(len(work.scratch)) for work in works]
        common_refs = take(len(common))
        locals_of = [take(1)[0] for work in works]
        send, recv = refs
        mail = Mail(layout, send, recv, numbers)
        run_steps(
            [
                work.steps(
                    Desk(mail, index, locals_of[index]),
                    in_refs[index],
                    out_refs[index],
                    scratch_refs[index],
                    common_refs,
                )
                for index, work in enumerate(works)
            ],
            starts,
        )
        mail.finish()

    results = pl.pallas_call(
        kernel,
        name=name,
        out_shape=[shape for shape, _ in outs],
        in_specs=[spec for _, spec in ins],
        out_specs=[spec for _, spec in outs],
        scratch_shapes=scratch
        + list(common)
        + [pltpu.SemaphoreType.DMA((work.local,)) for work in works]
        + [pltpu.SemaphoreType.DMA((len(slots),))] * 2,
        compiler_params=pltpu.CompilerParams(
            has_side_effects=True, vmem_limit_bytes=megabytes * mib
        ),
    )(*[array for array, _ in ins])
    results = list(results)
    grouped = []
    for work in works:
        grouped.append(results[: len(work.outs)])
        del results[: len(work.outs)]
    return grouped


def gather_work(layout, shard, one_block):
    lines, members, sides = layout.lines, layout.members, layout.sides
    width = shard.shape[1] // layout.blocks(one_block)
    spots = [("own", 0)]
    for t in range(1, lines):
        spots += [(f"below{t}", -t), (f"above{t}", t)]
    slots = [("mix", j) for j in range(1, members)]
    slots += [(way, t) for way in ("up", "down") for t in range(lines)]
    slots += [("cross", source) for source, _ in spots]
    slots += [("core", j) for j in range(1 if one_block else sides)]
    if not one_block:
        slots += [
            ("side", half, source, j)
            for half in (0, 1)
            for source, _ in spots
            for j in range(1, sides)
        ]

    def steps(desk, ins, outs, scratch, common):
        (shard,), (out,), (landing, slab, wide) = ins, outs, scratch
        group, line, member, side, core = desk.group, desk.line, desk.member, desk.side, desk.core
        has_up, has_down = line < lines - 1, line > 0

        def columns(side_of, core_of):
            block = core_of if one_block else core_of * sides + side_of
            return pl.ds(pl.multiple_of(block * width, 128), width)

        own = columns(side, core)

        def place(group_of, line_of, lanes=own):
            first = (group_of * lines + line_of) * layout.slab
            return out.at[pl.ds(pl.multiple_of(first, 16), layout.slab), lanes]

        def present(step):
            return None if step == 0 else line >= -step if step < 0 else line < lines - step

        for j in range(1, members):
            other = (member + j) % members
            desk.send(
                ("mix", j),
                shard.at[:, columns(other // 2, other % 2)],
                landing.at[member],
                desk.at(side=other // 2, core=other % 2),
            )
        mine = desk.local(0, shard.at[:, own], landing.at[member])
        mine.start()
        yield
        for j in range(1, members):
            desk.wait(("mix", j), landing.at[(member + members - j) % members])
        mine.wait()
        for m in range(members):
            rows = slice(m * layout.rows, (m + 1) * layout.rows)
            wide[rows, :] = landing[m, : layout.rows, :].astype(jnp.float32)
        slab[...] = wide[...].astype(slab.dtype)
        keep = desk.local(1, slab, place(group, line))
        keep.start()

        def pass_on(source, what, half, where, when):
            if half == 0:
                desk.send(("cross", source), what, where, desk.at(group=1 - group), when)
            if not one_block:
                for j in range(1, sides):
                    slot = ("side", half, source, j)
                    desk.send(slot, what, where, desk.at(side=(side + j) % sides), when)

        home = place(group, line)
        desk.send(("up", 0), slab, home, desk.at(line=line + 1), has_up)
        desk.send(("down", 0), slab, home, desk.at(line=line - 1), has_down)
        pass_on("own", slab, 0, home, None)
        yield
        for t in range(1, lines):
            for way, name, step, further, to in (
                ("up", "below", -t, has_up, line + 1),
                ("down", "above", t, has_down, line - 1),
            ):
                when, where = present(step), place(group, line + step)
                guarded(when, functools.partial(desk.wait, (way, t - 1), where))
                desk.send((way, t), where, where, desk.at(line=to), all_of(when, further))
                pass_on(f"{name}{t}", where, 0, where, when)
            if t == 1:
                where = place(1 - group, line)
                desk.wait(("cross", "own"), where)
                pass_on("own", where, 1, where, None)
            yield
        for t in range(1, lines):
            for name, step in ((f"below{t}", -t), (f"above{t}", t)):
                when, where = present(step), place(1 - group, line + step)
                guarded(when, functools.partial(desk.wait, ("cross", name), where))
                pass_on(name, where, 1, where, when)
            yield
        keep.wait()
        partner = desk.at(core=1 - core)
        desk.send(("core", 0), out.at[:, own], out.at[:, own], partner)
        if not one_block:
            yield
            for j in range(1, sides):
                theirs = columns((side + sides - j) % sides, core)
                for half, group_of in ((0, group), (1, 1 - group)):
                    for source, step in spots:
                        where = place(group_of, line + step, theirs)
                        slot = ("side", half, source, j)
                        guarded(present(step), functools.partial(desk.wait, slot, where))
                desk.send(("core", j), out.at[:, theirs], out.at[:, theirs], partner)
        yield
        desk.wait(("core", 0), out.at[:, columns(side, 1 - core)])
        if not one_block:
            for j in range(1, sides):
                theirs = columns((side + sides - j) % sides, 1 - core)
                desk.wait(("core", j), out.at[:, theirs])

    low = jnp.bfloat16
    return Work(
        steps,
        [(shard, anywhere())],
        [(jax.ShapeDtypeStruct((layout.model_width, shard.shape[1]), low), anywhere())],
        [
            pltpu.VMEM((members, layout.padded, width), low),
            pltpu.VMEM((layout.slab, width), low),
            pltpu.VMEM((layout.slab, width), jnp.float32),
        ],
        slots,
        2,
    )


def add_rows(target, first, target_columns, source, source_columns, count, source_first=0):
    step = math.gcd(count, 48)

    def one(index, carry):
        rows = pl.ds(pl.multiple_of(first + index * step, 16), step)
        theirs = pl.ds(pl.multiple_of(source_first + index * step, 16), step)
        total = target[rows, target_columns].astype(jnp.float32)
        total += source[theirs, source_columns].astype(jnp.float32)
        target[rows, target_columns] = total.astype(target.dtype)
        return carry

    lax.fori_loop(0, count // step, one, 0)


def reduce_work(layout, lefts, right, one_block, switch=0, split=3):
    lines, members, sides = layout.lines, layout.members, layout.sides
    tok, columns = right.shape
    blocks = layout.blocks(one_block)
    width, half = columns // blocks, columns // 2
    near_rows, slab_rows, low = layout.near, layout.slab, jnp.bfloat16
    count, depth = min(split, width // 128), min(4, lines)
    parts = []
    for index in range(count):
        first = width // 128 * index // count * 128
        parts.append((first, width // 128 * (index + 1) // count * 128 - first))
    order = []
    for t in range(lines):
        goal = lines - 1 - t // 2 if t % 2 == 0 else t // 2
        order.append(goal)
    slots = [("left", k) for k in range(len(lefts))] + ["right"]
    slots += [("cross", part, t) for part in parts for t in range(lines)]
    slots += [
        (way, part, t) for way in ("up", "down") for part in parts for t in range(1, lines)
    ]
    slots += [("mix", j) for j in range(1, members)]
    if not one_block:
        slots += [
            ("side", part, tag, t, j)
            for part in parts
            for tag in (0, 1)
            for t in range(lines)
            for j in range(1, sides)
        ]

    def steps(desk, ins, outs, scratch, common):
        left_in, right_in = ins[: len(lefts)], ins[len(lefts)]
        out, left_land, right_land = outs[0], outs[1 : 1 + len(lefts)], outs[1 + len(lefts)]
        total, cross, up, down, piece, landing, wide = scratch[:7]
        from_side = None if one_block else scratch[7]
        left_all, right_all = common
        group, line, member, side, core = desk.group, desk.line, desk.member, desk.side, desk.core
        partner = desk.at(core=1 - core)
        own = pl.ds(0 if one_block else pl.multiple_of(side * width, 128), width)
        stay = pl.ds(pl.multiple_of(core * half, 128), half)
        away = pl.ds(pl.multiple_of((1 - core) * half, 128), half)

        def first_of(tag, goal):
            return pl.multiple_of((group if tag else 1 - group) * near_rows + goal * slab_rows, 16)

        for k, left in enumerate(left_in):
            desk.send(("left", k), left, left_land[k], partner)
        desk.send("right", right_in.at[:, away], right_land, partner)
        yield
        loads = []

        def load(source, target):
            copy = desk.local(len(loads), source, target)
            copy.start()
            loads.append(copy)

        for k, left in enumerate(left_in):
            load(left, left_all.at[k, 0])
        load(right_in.at[:, stay], right_all.at[0, :, pl.ds(0, half)])
        for k in range(len(left_in)):
            desk.wait(("left", k), left_land[k])
            load(left_land[k], left_all.at[k, 1])
        desk.wait("right", right_land)
        load(right_land, right_all.at[1, :, pl.ds(0, half)])
        for copy in loads:
            copy.wait()

        def multiply(tag):
            rows = pl.ds(first_of(tag, 0), near_rows)

            def piece_of(first, lanes, which):
                theirs = pl.ds(first, lanes)
                product = dot_nn(left_all[which, 0, rows, :], right_all[0, :, theirs])
                product += dot_nn(left_all[which, 1, rows, :], right_all[1, :, theirs])
                total[rows, theirs] = product.astype(low)

            lanes = 256 if len(lefts) == 1 else math.gcd(switch, 384)

            def one(index, carry):
                first = pl.multiple_of(index * lanes, 128)
                which = 0
                if len(lefts) > 1:
                    which = jnp.where(core * half + index * lanes >= switch, 1, 0)
                piece_of(first, lanes, which)
                return carry

            lax.fori_loop(0, half // lanes, one, 0)
            if half % lanes:
                piece_of(half // lanes * lanes, half % lanes, 0)

        own_first = 0 if one_block else side * width
        pieces = [
            (part, tag, goal)
            for part in parts
            for tag in ((0,) if one_block else (0, 1))
            for goal in order
        ]

        def lanes_of(part, first):
            return pl.ds(pl.multiple_of(first + part[0], 128), part[1])

        def post(number):
            if number >= len(pieces):
                return
            part, tag, goal = pieces[number]
            if one_block:
                if number >= depth:
                    before = pieces[number - depth]
                    desk.settle(("cross", before[0], before[2]))
                send_across(part, goal)
                return
            rows = pl.ds(first_of(tag, goal), slab_rows)
            for j in range(1, sides):
                if number >= depth:
                    desk.settle(("side", *pieces[number - depth], j))
                other = (side + j) % sides
                desk.send(
                    ("side", part, tag, goal, j),
                    total.at[rows, lanes_of(part, other * width)],
                    from_side.at[j - 1, rows, lanes_of(part, 0)],
                    desk.at(side=other),
                )

        def send_across(part, goal):
            rows = pl.ds(first_of(0, goal), slab_rows)
            desk.send(
                ("cross", part, goal),
                total.at[rows, lanes_of(part, own_first)],
                cross.at[goal, :, lanes_of(part, 0)],
                desk.at(group=1 - group),
            )

        def take_side(part, tag, goal):
            first = first_of(tag, goal)
            rows, lanes = pl.ds(first, slab_rows), lanes_of(part, 0)
            for j in range(1, sides):
                desk.wait(("side", part, tag, goal, j), from_side.at[j - 1, rows, lanes])
            post(pieces.index((part, tag, goal)) + depth)
            for j in range(1, sides):
                add_rows(
                    total, first, lanes_of(part, own_first), from_side.at[j - 1], lanes,
                    slab_rows, first,
                )

        ends = lines - 1 - line

        def part_steps(part):
            lanes, mine = lanes_of(part, 0), lanes_of(part, own_first)
            if not one_block:
                for goal in order:
                    take_side(part, 0, goal)
                    send_across(part, goal)
                    yield
            for goal in order:
                if not one_block:
                    take_side(part, 1, goal)
                desk.wait(("cross", part, goal), cross.at[goal, :, lanes])
                if one_block:
                    post(pieces.index((part, 0, goal)) + depth)
                add_rows(total, first_of(1, goal), mine, cross.at[goal], lanes, slab_rows)
                yield
            for t in range(1, lines):
                for way, buffer, going, fed, goal, to in (
                    ("up", up, line < t, line > 0, lines - t + line, line + 1),
                    ("down", down, ends < t, ends > 0, t - lines + line, line - 1),
                ):
                    first = first_of(1, goal)

                    @pl.when(all_of(going, fed))
                    def _():
                        if t > 1:
                            desk.wait((way, part, t - 1), buffer.at[t - 2, :, lanes])
                            add_rows(total, first, mine, buffer.at[t - 2], lanes, slab_rows)

                    desk.send(
                        (way, part, t),
                        total.at[pl.ds(first, slab_rows), mine],
                        buffer.at[t - 1, :, lanes],
                        desk.at(line=to),
                        going,
                    )
                yield

        multiply(0)
        for number in range(depth):
            post(number)
        yield
        multiply(1)
        yield
        running = [part_steps(part) for part in parts]
        turn, lag = 0, len(pieces) // len(parts)
        while running:
            for index, steps_of in enumerate(running):
                if steps_of is not None and turn >= lag * index:
                    try:
                        next(steps_of)
                    except StopIteration:
                        running[index] = None
            if not any(running):
                break
            turn += 1
            yield
        first = first_of(1, line)
        wide[...] = total[pl.ds(first, slab_rows), own].astype(jnp.float32)
        for way, buffer, fed in (("up", up, line > 0), ("down", down, ends > 0)):

            @pl.when(fed)
            def _():
                for part in parts:
                    where = buffer.at[lines - 2, :, lanes_of(part, 0)]
                    desk.wait((way, part, lines - 1), where)
                wide[...] += buffer[lines - 2].astype(jnp.float32)

        for m in range(members):
            rows = slice(m * layout.rows, (m + 1) * layout.rows)
            piece[m] = jnp.zeros(piece.shape[1:], piece.dtype)
            piece[m, : layout.rows, :] = wide[rows, :].astype(piece.dtype)
        seat = core * sides + side
        for j in range(1, members):
            other = (member + j) % members
            desk.send(
                ("mix", j),
                piece.at[other],
                landing.at[seat],
                desk.at(side=other // 2, core=other % 2),
            )
        landing[seat] = piece[member]
        yield
        for j in range(1, members):
            other = (member + members - j) % members
            desk.wait(("mix", j), landing.at[other % 2 * sides + other // 2])
        if one_block:
            for c in range(2):
                block = landing[c * sides].astype(jnp.float32)
                for s in range(1, sides):
                    block += landing[c * sides + s].astype(jnp.float32)
                out[:, c * width : (c + 1) * width] = block
        else:
            for b in range(blocks):
                out[:, b * width : (b + 1) * width] = landing[b].astype(jnp.float32)

    scratch = [
        pltpu.VMEM((layout.model_width, half), low),
        pltpu.VMEM((lines, slab_rows, width), low),
        pltpu.VMEM((lines - 1, slab_rows, width), low),
        pltpu.VMEM((lines - 1, slab_rows, width), low),
        pltpu.VMEM((members, layout.padded, width), low),
        pltpu.VMEM((members, layout.padded, width), low),
        pltpu.VMEM((slab_rows, width), jnp.float32),
    ]
    if not one_block:
        scratch.append(pltpu.VMEM((sides - 1, layout.model_width, width), low))
    ins = [(array, anywhere()) for array in [*lefts, right]]
    return Work(
        steps,
        ins,
        [(jax.ShapeDtypeStruct((layout.padded, columns), jnp.float32), in_vmem())]
        + [(jax.ShapeDtypeStruct(left.shape, low), anywhere()) for left in lefts]
        + [(jax.ShapeDtypeStruct((tok, half), low), anywhere())],
        scratch,
        slots,
        2 * len(lefts) + 2,
    )


class Reach:
    def __init__(self, tok, left, right):
        self.tok, self.left, self.right = tok, left, right
        self.window = left + tok + right
        self.deltas = [d for d in range(-8, 9) if d != 0 and self.rows(d) > 0]

    def first(self, delta):
        return max(0, self.tok * delta - self.left)

    def rows(self, delta):
        last = min(self.tok, self.tok * delta - self.left + self.window)
        return last - self.first(delta)

    def spot(self, delta):
        return self.first(delta) - self.tok * delta + self.left


def parts_of(count, step=80):
    return [(first, min(step, count - first)) for first in range(0, count, step)]


def window_work(layout, reach, key_value):
    tok, width = key_value.shape
    left, lines, places = reach.left, layout.lines, layout.lines * layout.members
    routed = layout.sides == 2
    pieces, depth = parts_of(tok), 2
    near_below, far_below = reach.spot(2), reach.spot(3)
    tail = (reach.first(3), max(reach.rows(3), 0))
    head = max(reach.rows(-2), 0)
    if routed:
        slots = ["pair", "tail", "share", "wide", "thin", "last"]
        slots += [(name, k) for name in ("right", "left", "climb", "drop") for k in range(len(pieces))]
        slots += [("fall", k) for k in range(len(parts_of(head)))]
    else:
        slots = [("reach", delta) for delta in reach.deltas]

    def direct(desk, own, window):
        seat = desk.line * layout.members + desk.member
        for delta in reach.deltas:
            count = reach.rows(delta)
            desk.send(
                ("reach", delta),
                own.at[pl.ds(reach.first(delta), count)],
                window.at[pl.ds(reach.spot(delta), count)],
                (desk.group, seat + delta),
                (seat + delta >= 0) & (seat + delta < places),
            )
        yield
        for delta in reach.deltas:
            where = window.at[pl.ds(reach.spot(delta), reach.rows(delta))]
            when = (seat - delta >= 0) & (seat - delta < places)
            guarded(when, functools.partial(desk.wait, ("reach", delta), where))

    def by_way(desk, own, window, transit):
        line, core = desk.line, desk.core
        first_side, last_side = desk.side == 0, desk.side == 1
        low_core, high_core = core == 0, core == 1
        has_up, has_down = line < lines - 1, line > 0
        has_before = last_side | has_down
        partner = desk.at(core=1 - core)

        def part(ref, first, count):
            return ref.at[pl.ds(first, count)]

        def post(k):
            if k >= len(pieces):
                return
            if k >= depth:
                desk.settle(("right", k - depth))
                desk.settle(("left", k - depth))
            first, count = pieces[k]
            desk.send(
                ("right", k), part(own, first, count), part(window, near_below + first, count),
                desk.at(side=1), first_side,
            )
            desk.send(
                ("left", k), part(own, first, count), part(transit, first, count),
                desk.at(side=0), last_side,
            )

        for k in range(depth):
            post(k)
        desk.send(
            "tail", part(own, *tail), part(window, far_below, tail[1]),
            desk.at(line=line + 1, core=0), high_core & has_up,
        )
        mirrored = pl.multiple_of(left + (2 * core - 1) * tok, 16)
        desk.send("pair", own, part(window, mirrored, tok), partner)
        yield
        for k, (first, count) in enumerate(pieces):
            ahead = part(transit, first, count)
            guarded(first_side, functools.partial(desk.wait, ("left", k), ahead))
            desk.send(
                ("climb", k), ahead, part(window, near_below + first, count),
                desk.at(line=line + 1), first_side & has_up,
            )
            behind = part(window, near_below + first, count)
            guarded(last_side, functools.partial(desk.wait, ("right", k), behind))
            post(k + depth)
            desk.send(
                ("drop", k), behind, part(window, left + tok + first, count),
                desk.at(line=line - 1, core=1), last_side & has_down & low_core,
            )
            if first < head:
                count = min(count, head - first)
                desk.send(
                    ("fall", k), part(window, near_below + first, count),
                    part(window, left + 2 * tok + first, count),
                    desk.at(line=line - 1), last_side & has_down & high_core,
                )
            yield
        stay = desk.local(1, part(transit, 0, head), part(window, left + 2 * tok, head))
        guarded(first_side, stay.start)
        desk.send(
            "share", transit, part(window, left + tok, tok), partner, first_side & low_core
        )

        def share_before(when):
            desk.send(
                "wide", part(window, near_below, tok), part(window, left - tok, tok), partner,
                when & high_core,
            )
            desk.send(
                "thin", part(window, near_below + tail[0], tail[1]),
                part(window, far_below, tail[1]), partner, when & low_core,
            )

        def climbed():
            for k, (first, count) in enumerate(pieces):
                desk.wait(("climb", k), part(window, near_below + first, count))

        guarded(first_side & has_down, climbed)
        share_before(has_before)
        yield

        def dropped():
            for k, (first, count) in enumerate(pieces):
                desk.wait(("drop", k), part(window, left + tok + first, count))
            for k, (first, count) in enumerate(parts_of(head)):
                desk.wait(("fall", k), part(window, left + 2 * tok + first, count))

        guarded(last_side & has_up & high_core, dropped)
        desk.send(
            "last", part(window, left + tok, head), part(window, left + 2 * tok, head), partner,
            last_side & has_up & high_core,
        )
        yield
        desk.wait("pair", part(window, pl.multiple_of(left + (1 - 2 * core) * tok, 16), tok))
        for when, slot, first, count in (
            (low_core & has_down, "tail", far_below, tail[1]),
            (first_side & high_core, "share", left + tok, tok),
            (has_before & low_core, "wide", left - tok, tok),
            (has_before & high_core, "thin", far_below, tail[1]),
            (last_side & has_up & low_core, "last", left + 2 * tok, head),
        ):
            guarded(when, functools.partial(desk.wait, slot, part(window, first, count)))
        guarded(first_side, stay.wait)

    def steps(desk, ins, outs, scratch, common):
        (own,), (window,) = ins, outs
        keep = desk.local(0, own, window.at[pl.ds(left, tok)])
        keep.start()
        yield from by_way(desk, own, window, *scratch) if routed else direct(desk, own, window)
        keep.wait()

    outs = [(jax.ShapeDtypeStruct((reach.window, width), key_value.dtype), anywhere())]
    scratch = [pltpu.VMEM((tok, width), key_value.dtype)] if routed else []
    return Work(steps, [(key_value, in_vmem())], outs, scratch, slots, 2)


def owned_work(layout, reach, grad_window):
    width = grad_window.shape[1]
    tok, left, lines = reach.tok, reach.left, layout.lines
    places = layout.lines * layout.members
    routed = layout.sides == 2
    pieces, depth = parts_of(tok), 2
    near_below, far_below = reach.spot(2), reach.spot(3)
    tail = (reach.first(3), max(reach.rows(3), 0))
    head = max(reach.rows(-2), 0)
    every = pl.ds(0, width)
    low = grad_window.dtype
    if routed:
        slots = ["pair", "tail", "share", "wide", "thin", "last", "rise"]
        slots += [(name, k) for name in ("right", "left", "fall", "lift") for k in range(len(pieces))]
    else:
        slots = [("reach", delta) for delta in reach.deltas]

    def direct(desk, grad, out, landing):
        seat = desk.line * layout.members + desk.member
        for delta in reach.deltas:
            count = reach.rows(delta)
            desk.send(
                ("reach", delta),
                grad.at[pl.ds(reach.spot(delta), count)],
                landing[delta],
                (desk.group, seat - delta),
                (seat - delta >= 0) & (seat - delta < places),
            )
        load = desk.local(0, grad.at[pl.ds(left, tok)], out)
        load.start()
        load.wait()
        yield
        for delta in reach.deltas:

            @pl.when((seat + delta >= 0) & (seat + delta < places))
            def _():
                desk.wait(("reach", delta), landing[delta])
                first, count = reach.first(delta), reach.rows(delta)
                add_rows(out, first, every, landing[delta], every, count)

    def by_way(desk, grad, out, scratch):
        near, middle, l_wide, l_far, l_climb, l_y, l_pair, l_tail = scratch
        line, core = desk.line, desk.core
        first_side, last_side = desk.side == 0, desk.side == 1
        low_core, high_core = core == 0, core == 1
        has_up, has_down = line < lines - 1, line > 0
        has_before = last_side | has_down
        gate = last_side & has_up & high_core
        partner = desk.at(core=1 - core)

        def part(ref, first, count):
            return ref.at[pl.ds(first, count)]

        def receive(when, slot, target, first, buffer, at, count):
            @pl.when(when)
            def _():
                desk.wait(slot, part(buffer, at, count))
                add_rows(target, first, every, buffer, every, count, at)

        desk.send(
            "last", part(grad, left + 2 * tok, head), part(l_climb, 0, head), partner,
            last_side & has_up & low_core,
        )
        desk.send(
            "wide", part(grad, left - tok, tok), l_wide, partner, has_before & low_core
        )
        desk.send(
            "thin", part(grad, far_below, tail[1]), part(l_wide, 0, tail[1]), partner,
            has_before & high_core,
        )
        desk.send(
            "share", part(grad, left + tok, tok), l_far, partner, first_side & high_core
        )
        desk.send(
            "tail", part(grad, far_below, tail[1]), l_tail,
            desk.at(line=line - 1, core=1), low_core & has_down,
        )
        desk.send("rise", part(grad, left + 2 * tok, head), part(l_far, 0, head),
            desk.at(line=line + 1), gate,
        )
        loads = [
            (desk.local(0, part(grad, near_below, tok), near), None),
            (desk.local(1, part(grad, left + tok, tok), middle), last_side),
            (desk.local(2, part(grad, left + 2 * tok, head), part(middle, 0, head)), first_side),
            (desk.local(3, part(grad, left, tok), out), None),
        ]
        for load, when in loads:
            guarded(when, load.start)

        @pl.when(first_side)
        def _():
            middle[head:, :] = jnp.zeros((tok - head, width), low)

        yield
        for load, when in loads:
            guarded(when, load.wait)
        receive(gate, "last", middle, 0, l_climb, 0, head)
        receive(has_before & high_core, "wide", near, 0, l_wide, 0, tok)
        receive(has_before & low_core, "thin", near, tail[0], l_wide, 0, tail[1])

        def post(k):
            if k >= len(pieces):
                return
            if k >= depth:
                desk.settle(("fall", k - depth))
                desk.settle(("lift", k - depth))
            first, count = pieces[k]
            desk.send(
                ("fall", k), part(middle, first, count), part(l_far, first, count),
                desk.at(line=line + 1, core=0), gate,
            )
            desk.send(
                ("lift", k), part(near, first, count), part(l_climb, first, count),
                desk.at(line=line - 1), first_side & has_down,
            )

        for k in range(depth):
            post(k)
        mirrored = pl.multiple_of(left + (1 - 2 * core) * tok, 16)
        desk.send("pair", part(grad, mirrored, tok), l_pair, partner)
        yield
        receive(first_side & low_core, "share", middle, 0, l_far, 0, tok)
        receive(last_side & has_down & high_core, "rise", near, 0, l_far, 0, head)
        for k, (first, count) in enumerate(pieces):
            receive(first_side & has_up, ("lift", k), middle, first, l_climb, first, count)
            desk.send(
                ("left", k), part(middle, first, count), part(l_y, first, count),
                desk.at(side=1), first_side,
            )
            receive(
                last_side & has_down & low_core, ("fall", k), near, first, l_far, first, count
            )
            desk.send(
                ("right", k), part(near, first, count), part(l_y, first, count),
                desk.at(side=0), last_side,
            )
            post(k + depth)
            yield
        receive(has_up & high_core, "tail", out, tail[0], l_tail, 0, tail[1])
        desk.wait("pair", l_pair)
        for k, (first, count) in enumerate(pieces):
            where = part(l_y, first, count)
            guarded(first_side, functools.partial(desk.wait, ("right", k), where))
            guarded(last_side, functools.partial(desk.wait, ("left", k), where))

            def one(index, carry):
                rows = pl.ds(pl.multiple_of(first + index * 16, 16), 16)
                total = out[rows, :].astype(jnp.float32) + l_pair[rows, :].astype(jnp.float32)
                out[rows, :] = (total + l_y[rows, :].astype(jnp.float32)).astype(out.dtype)
                return carry

            lax.fori_loop(0, count // 16, one, 0)
            yield

    def steps(desk, ins, outs, scratch, common):
        if routed:
            yield from by_way(desk, ins[0], outs[0], scratch)
        else:
            yield from direct(desk, ins[0], outs[0], dict(zip(reach.deltas, scratch)))

    if routed:
        counts = [tok] * 7 + [tail[1]]
    else:
        counts = [reach.rows(delta) for delta in reach.deltas]
    return Work(
        steps,
        [(grad_window, anywhere())],
        [(jax.ShapeDtypeStruct((tok, width), low), in_vmem())],
        [pltpu.VMEM((count, width), low) for count in counts],
        slots,
        4,
    )


def sum_work(layout, block):
    sizes = (2, layout.sides, layout.model_width // layout.near, layout.lines)
    slots = [(stage, j) for stage, size in enumerate(sizes) for j in range(1, size)]

    def steps(desk, ins, outs, scratch, common):
        (block,), (out,) = ins, outs
        yield
        out[...] = block[...]
        for stage, (landing, size) in enumerate(zip(scratch, sizes)):
            mine = (desk.core, desk.side, desk.group, desk.line)[stage]
            landing[mine] = out[...]
            for j in range(1, size):
                other = (mine + j) % size
                to = desk.at(**{("core", "side", "group", "line")[stage]: other})
                desk.send((stage, j), landing.at[mine], landing.at[mine], to)
            yield
            for j in range(1, size):
                desk.wait((stage, j), landing.at[(mine + size - j) % size])
            total = landing[0]
            for j in range(1, size):
                total = total + landing[j]
            out[...] = total

    return Work(
        steps,
        [(block, in_vmem())],
        [(jax.ShapeDtypeStruct(block.shape, block.dtype), in_vmem())],
        [pltpu.VMEM((size, *block.shape), block.dtype) for size in sizes],
        slots,
        1,
    )


def column_sum(source):
    return jnp.sum(source.astype(jnp.float32), axis=0)


def norm_forward(source, gain_row, shift_row):
    row_mean = jnp.mean(source, axis=-1, keepdims=True)
    centred = source - row_mean
    variance = jnp.mean(centred * centred, axis=-1, keepdims=True)
    inv_scale = lax.rsqrt(variance + eps_norm)
    unit_rows = centred * inv_scale
    return (unit_rows * gain_row + shift_row, unit_rows, inv_scale)


def norm_backward(gradient, unit_rows, inv_scale, gain_row):
    scaled = gradient * gain_row
    grad_in = inv_scale * (
        scaled
        - jnp.mean(scaled, axis=-1, keepdims=True)
        - unit_rows * jnp.mean(scaled * unit_rows, axis=-1, keepdims=True)
    )
    return (grad_in, jnp.sum(gradient * unit_rows, axis=0), jnp.sum(gradient, axis=0))


def gelu_tanh(source):
    return jax.nn.gelu(source, approximate=True)


def adam_step(weight_now, gradient, first_old, second_old):
    first_new = beta_first * first_old + (1.0 - beta_first) * gradient
    second_new = beta_second * second_old + (1.0 - beta_second) * gradient * gradient
    first_hat = first_new / (1.0 - beta_first**STEP)
    second_hat = second_new / (1.0 - beta_second**STEP)
    update = -learn_rate * (
        first_hat / (jnp.sqrt(second_hat) + eps_adam)
        + weight_decay * weight_now.astype(jnp.float32)
    )
    return (first_new, second_new, update)


def round_up(count, unit):
    return -(-count // unit) * unit


def per_device(
    inputs, image_ids, token_mask, cotangent,
    w_qkv, w_out, w_up, w_down, norm_gains, bias_rows, up_bias,
    first_qkv, first_out, first_up, first_down, first_gains, first_bias, first_upbias,
    second_qkv, second_out, second_up, second_down, second_gains, second_bias, second_upbias,
):
    tok, width = inputs.shape
    layers, _, hidden_width = w_up.shape
    places = lax.axis_size("seq")
    place = lax.axis_index("seq")
    layout = Layout(lax.axis_size("dp"), places, width)
    group_tok = tok * places
    spare_count = group_tok - group_tok // IMG * IMG
    left = round_up(IMG - 1 + spare_count, 16)
    right = round_up(IMG - 1, 16)
    tile = tok // 2

    reach = Reach(tok, left, right)

    half = hidden_width // 2
    half_pad = round_up(half + 8 * layers, 128)
    wide_columns = 2 * half_pad

    def spread(array):
        pad = [(0, 0)] * (array.ndim - 1) + [(0, half_pad - half)]
        return jnp.concatenate([jnp.pad(array[..., :half], pad), jnp.pad(array[..., half:], pad)], -1)

    def unspread(array):
        return jnp.concatenate(
            [array[..., :half], array[..., half_pad : half_pad + half]], axis=-1
        )

    def filled(array, rows, columns):
        return jnp.pad(array, ((0, rows - array.shape[0]), (0, columns - array.shape[1])))

    attn_columns = layout.columns(4 * width, False)
    up_columns = layout.columns(wide_columns, True)
    down_columns = layout.columns(wide_columns, False)
    rows_of = jnp.concatenate([norm_gains.reshape(-1, layout.rows), bias_rows.reshape(-1, layout.rows)])
    row_count = rows_of.shape[0]
    shards = []
    for layer in range(layers):
        attn_shard = jnp.concatenate([w_qkv[layer], w_out[layer]], axis=1)
        up_shard = spread(w_up[layer])
        if layer == 0:
            up_shard = up_shard.at[:, half : half + row_count].set(rows_of.T)
        down_shard = spread(w_down[layer].T)
        shards += [
            filled(attn_shard, layout.padded, attn_columns),
            filled(up_shard, layout.padded, up_columns),
            filled(down_shard, layout.padded, down_columns if layer else up_columns),
        ]
    word = image_ids * 2 + (token_mask > 0).astype(jnp.int32)
    word = jnp.broadcast_to(word[:, None], (tok, 128))
    def gather(layer, which):
        return gather_work(layout, shards[3 * layer + which], which == 1 or (which == 2 and layer == 0))

    gathered = [[None] * 3 for _ in range(layers)]
    begun = [(layer, which) for layer in range(layers) for which in range(3)]
    *results, (window_word, *_) = exchange(
        "gather_parameters",
        layout,
        [gather(*spot) for spot in begun] + [window_work(layout, reach, word)],
        [[index] for index in range(len(begun))] + [[1]],
        40,
    )
    for (layer, which), (matrix,) in zip(begun, results):
        gathered[layer][which] = matrix
    window_word = window_word[:, 0]
    all_rows = gathered[0][1][:, half : half + row_count].T.astype(jnp.float32)
    gains = all_rows[: 2 * layers].reshape(layers, 2, width)
    shifts = all_rows[2 * layers :].reshape(layers, 6, width)
    up_shift = spread(up_bias.astype(jnp.float32))

    plan, own_code, span_code = attention_plan(
        tile, left, right, image_ids, token_mask, window_word // 2, window_word % 2, place, places
    )

    residual = inputs.astype(jnp.float32)
    kept_layers = []
    for layer in range(layers):
        attn_weight, up_weight, down_weight = gathered[layer]
        down_weight = down_weight[:, :wide_columns]
        normed, unit_one, inv_one = norm_forward(residual, gains[layer, 0], shifts[layer, 0])
        normed_low = normed.astype(jnp.bfloat16)
        projected = dot_nn(normed_low, attn_weight[:, : 3 * width])
        queries = (projected[:, :width] + shifts[layer, 2]).astype(jnp.bfloat16)
        value_shift = jnp.concatenate([jnp.zeros_like(shifts[layer, 3]), shifts[layer, 3]])
        key_value = (projected[:, width:] + value_shift).astype(jnp.bfloat16)
        ((window, *_),) = exchange(
            "fetch_window", layout, [window_work(layout, reach, key_value)], [[0]], 20
        )
        attended, lse = attention_forward(tile, left, plan, queries, window, own_code, span_code)
        middle = (
            residual
            + dot_nn(attended, attn_weight[:, 3 * width : 4 * width])
            + shifts[layer, 4]
        )
        hidden, unit_two, inv_two = norm_forward(middle, gains[layer, 1], shifts[layer, 1])
        hidden_low = hidden.astype(jnp.bfloat16)
        pre_act = dot_nn(hidden_low, up_weight[:, :wide_columns]) + up_shift[layer]
        active = gelu_tanh(pre_act).astype(jnp.bfloat16)
        residual = middle + dot_nt(active, down_weight) + shifts[layer, 5]
        active = filled(active, tok, down_columns)
        kept_layers.append(
            (window, unit_one, inv_one, normed_low, queries, lse, attended,
             unit_two, inv_two, hidden_low, pre_act, active)
        )

    def packed(rows):
        flat = jnp.concatenate([row.reshape(-1) for row in rows])
        return jnp.pad(flat, (0, -flat.size % 1024)).reshape(-1, 128)

    grad_res = cotangent.astype(jnp.float32)
    owned = [[None] * 3 for _ in range(layers)]
    row_grads = [None] * layers
    upbias_grads = [None] * layers
    for layer in reversed(range(layers)):
        (window, unit_one, inv_one, normed_low, queries, lse, attended,
         unit_two, inv_two, hidden_low, pre_act, active) = kept_layers[layer]
        attn_weight, up_weight, down_weight = gathered[layer]
        down_weight = down_weight[:, :wide_columns]
        grad_branch = grad_res.astype(jnp.bfloat16)
        grad_active = dot_nn(grad_branch, down_weight)
        _, gelu_pull = jax.vjp(gelu_tanh, pre_act)
        grad_pre = gelu_pull(grad_active)[0].astype(jnp.bfloat16)
        upbias_grads[layer] = unspread(column_sum(grad_pre))
        grad_hidden = dot_nt(grad_pre, up_weight[:, :wide_columns])
        back_two, gain_two, shift_two = norm_backward(
            grad_hidden, unit_two, inv_two, gains[layer, 1]
        )
        grad_mid = grad_res + back_two
        grad_attn = grad_mid.astype(jnp.bfloat16)
        grad_attended = dot_nt(grad_attn, attn_weight[:, 3 * width : 4 * width]).astype(
            jnp.bfloat16
        )
        grad_query, grad_window = attention_backward(
            tile, left, plan, queries, window, grad_attended, lse, own_code, span_code
        )
        works = [owned_work(layout, reach, grad_window)]
        if layer == 0:
            works.append(sum_work(layout, packed([*upbias_grads, *row_grads[1:]])))
        (grad_key_value,), *small_sum = exchange(
            "return_window", layout, works, [[0], [2, 4, 6, 7, 8]][: len(works)], 40
        )
        grad_proj = jnp.concatenate([grad_query, grad_key_value], axis=1)
        grad_normed = dot_nt(grad_proj, attn_weight[:, : 3 * width])
        back_one, gain_one, shift_one = norm_backward(
            grad_normed, unit_one, inv_one, gains[layer, 0]
        )
        grad_res = grad_mid + back_one
        row_grads[layer] = jnp.stack(
            [
                gain_one,
                gain_two,
                shift_one,
                shift_two,
                column_sum(grad_query),
                column_sum(grad_key_value[:, width:]),
                column_sum(grad_attn),
                column_sum(grad_branch),
            ]
        )
        grad_side = filled(jnp.concatenate([grad_proj, grad_attn], axis=1), tok, attn_columns)
        works = [
            reduce_work(layout, [normed_low.T, attended.T], grad_side, False, 3 * width),
            reduce_work(layout, [hidden_low.T], grad_pre, True),
            reduce_work(layout, [grad_branch.T], active, False),
        ]
        turns = [[0], [1], [2]]
        if layer == 0:
            works.append(sum_work(layout, packed(row_grads[:1])))
            turns.append([2, 4, 6, 8, 10])
        left_operands = pltpu.VMEM((2, 2, width, tok), jnp.bfloat16)
        right_operands = pltpu.VMEM((2, tok, max(attn_columns, down_columns) // 2), jnp.bfloat16)
        results = exchange(
            "reduce_gradients", layout, works, turns, 63, [left_operands, right_operands]
        )
        owned[layer], row_sum = [result[0] for result in results[:3]], results[3:]

    flat = small_sum[0][0].reshape(-1)
    upbias_grads = flat[: layers * hidden_width].reshape(layers, hidden_width)
    later = flat[layers * hidden_width :][: (layers - 1) * 8 * width].reshape(-1, 8, width)
    row_sums = jnp.concatenate([row_sum[0][0].reshape(-1)[: 8 * width].reshape(1, 8, width), later])
    seat = lax.axis_index("dp") * places + place
    row_sums = lax.dynamic_slice_in_dim(row_sums, seat * layout.rows, layout.rows, axis=2)

    def stacked(part):
        return jnp.stack([part(*owned[layer]) for layer in range(layers)])

    rows = layout.rows

    grads = (
        stacked(lambda attn, up, down: attn[:rows, : 3 * width]),
        stacked(lambda attn, up, down: attn[:rows, 3 * width : 4 * width]),
        stacked(lambda attn, up, down: unspread(up[:rows])),
        stacked(lambda attn, up, down: unspread(down[:rows]).T),
        row_sums[:, :2],
        row_sums[:, 2:],
        upbias_grads,
    )
    params = (w_qkv, w_out, w_up, w_down, norm_gains, bias_rows, up_bias)
    firsts = (first_qkv, first_out, first_up, first_down, first_gains, first_bias, first_upbias)
    seconds = (
        second_qkv, second_out, second_up, second_down, second_gains, second_bias, second_upbias,
    )
    results = [adam_step(*packed) for packed in zip(params, grads, firsts, seconds)]
    return (
        (residual, grad_res)
        + grads
        + tuple(result[0] for result in results)
        + tuple(result[1] for result in results)
        + tuple(result[2] for result in results)
    )


def solution(mesh):
    in_specs = (
        P(("dp", "seq"), None),
        P(("dp", "seq")),
        P(("dp", "seq")),
        P(("dp", "seq"), None),
        P(None, ("dp", "seq"), None),
        P(None, ("dp", "seq"), None),
        P(None, ("dp", "seq"), None),
        P(None, None, ("dp", "seq")),
        P(None, None, ("dp", "seq")),
        P(None, None, ("dp", "seq")),
        P(),
        P(None, ("dp", "seq"), None),
        P(None, ("dp", "seq"), None),
        P(None, ("dp", "seq"), None),
        P(None, None, ("dp", "seq")),
        P(None, None, ("dp", "seq")),
        P(None, None, ("dp", "seq")),
        P(),
        P(None, ("dp", "seq"), None),
        P(None, ("dp", "seq"), None),
        P(None, ("dp", "seq"), None),
        P(None, None, ("dp", "seq")),
        P(None, None, ("dp", "seq")),
        P(None, None, ("dp", "seq")),
        P(),
    )
    out_specs = (
        P(("dp", "seq"), None),
        P(("dp", "seq"), None),
        P(None, ("dp", "seq"), None),
        P(None, ("dp", "seq"), None),
        P(None, ("dp", "seq"), None),
        P(None, None, ("dp", "seq")),
        P(None, None, ("dp", "seq")),
        P(None, None, ("dp", "seq")),
        P(),
        P(None, ("dp", "seq"), None),
        P(None, ("dp", "seq"), None),
        P(None, ("dp", "seq"), None),
        P(None, None, ("dp", "seq")),
        P(None, None, ("dp", "seq")),
        P(None, None, ("dp", "seq")),
        P(),
        P(None, ("dp", "seq"), None),
        P(None, ("dp", "seq"), None),
        P(None, ("dp", "seq"), None),
        P(None, None, ("dp", "seq")),
        P(None, None, ("dp", "seq")),
        P(None, None, ("dp", "seq")),
        P(),
        P(None, ("dp", "seq"), None),
        P(None, ("dp", "seq"), None),
        P(None, ("dp", "seq"), None),
        P(None, None, ("dp", "seq")),
        P(None, None, ("dp", "seq")),
        P(None, None, ("dp", "seq")),
        P(),
    )
    return jax.shard_map(
        per_device, mesh=mesh, in_specs=in_specs, out_specs=out_specs, check_vma=False
    )
```

time: 1810 us -> 1510 us (0.83)
  Pallas kernels: 903 us -> 1180 us
  waiting for transfers between devices: 224 us -> 0 us
  starting transfers between devices: 182 us -> 0 us
  matrix products: 225 us -> 156 us
  local copies, waits for them, and re-layouts: 141 us -> 91.9 us
  blocking collectives: 38.7 us -> 0 us
    pallas_call x3 -> x7, Pallas kernels: 742 us -> 1020 us  [exchange(): pl.pallas_call(kernel, name=name, out_shape=[shape for shape, _ in outs],...]
    ppermute x25 -> x0, waiting for transfers between devices: 224 us -> none  [shifted(): return lax.ppermute(array, 'seq', pairs)]
    ppermute x25 -> x0, starting transfers between devices: 182 us -> none  [shifted(): return lax.ppermute(array, 'seq', pairs)]
    dot_general x8 -> x0, matrix products: 65.6 us -> none  [dot_tn(): lax.dot_general(left, right, (((0,), (0,)), ((), ())), preferred_element_...]
    psum x1 -> x0, blocking collectives: 38.7 us -> none  [per_device(): lax.psum(unspread(column_sum(grad_pre)), ('dp', 'seq'))]
    slice x13 -> x7, local copies, waits for them, and re-layouts: 27.6 us -> 1.15 us  [the longest x1 0.66 us: per_device(): residual = middle + dot_nt(active, down_weight) + shifts[layer, 5]]
    unnamed x253 -> x243, local copies, waits for them, and re-layouts: 50.2 us -> 57.7 us
  transfers between devices with their start and end apart: 25 -> 0, of which waited for: 8 -> 0; matrix products, arithmetic and copies ran while one was open for 7% -> 0% of each run, Pallas kernels for 15% -> 0%
where the time goes in v2:
time: 1510 us; the launch traced here: 1500 us
  Pallas kernels  1180 us (78%)
  matrix products  156 us (10%)
  local copies, waits for them, and re-layouts  91.9 us (6%)
  other arithmetic  59.3 us (4%)
  between operations  15.8 us (1%)
    pallas_call x7, Pallas kernels, exchange(): pl.pallas_call(kernel, name=name, out_shape=[shape for shape, _ in outs],...  1020 us
    pallas_call x2, Pallas kernels, attention_backward(): pl.pallas_call(functools.partial(attention_backward_kernel, tile, left, e...  100 us
    dot_general x8, matrix products, dot_nn(): lax.dot_general(left, right, (((1,), (0,)), ((), ())), preferred_element_...  83.2 us
    dot_general x8, matrix products, dot_nt(): lax.dot_general(left, right, (((1,), (1,)), ((), ())), preferred_element_...  72.6 us
    unnamed x243, local copies, waits for them, and re-layouts  57.7 us
    pallas_call x2, Pallas kernels, attention_forward(): pl.pallas_call(functools.partial(attention_forward_kernel, tile, left, ex...  53.9 us

profile of v2, /device:TPU:9, one launch (start us, length us, event | category | flops | bytes accessed | tf_op | source)
XLA Modules:
  0.0 1497.9 jit_solution(9063166255040712742)
XLA Ops:
  6.7 295.5 %gather_parameters.1 = (bf16[1152,4608]{1,0:T(8,128)(2,1)}, bf16[1152,4352]{1,0:T(8,128)(2,1)S(1)}, bf16[1152,4352]{1,0:T(8,128)(2,1)}, bf16[1152,4608]{1,0:T(8,...) custom-call(bf16[48,4608]{1,0:T(8,128)(2,1)S(1)} %get-tuple-element.312.refs_0_, ...), custom_call_target="tpu_custom_call" | custom-call | tf_op jit(solution)/shard_map/gather_parameters/pallas_call | solution.py:411
  325.6 7.4 fusion.29
  333.4 66.2 %fetch_window.2.window = bf16[2336,2304]{1,0:T(8,128)(2,1)S(1)} custom-call(bf16[480,2304]{1,0:T(8,128)(2,1)S(1)} %fusion.32.refs_0_), custom_call_target="tpu_custom_call" | custom-call | tf_op jit(solution)/shard_map/fetch_window/pallas_call | solution.py:411
  399.6 4.0 copy-done
  408.9 26.9 %attention_forward.2 = (bf16[480,1152]{1,0:T(8,128)(2,1)}, f32[480,128]{1,0:T(8,128)}) custom-call(s32[8]{0:T(128)} %stack.140.plan, bf16[480,1152]{1,0:T(8,128)(2,1)} %fusion.67.query, bf16[2336,2304]{1,0:T(8,128)(2,1)} %copy-done, s32[480,1]{1,0:T(8,128)} %copy.203.own_code, s32[4,1,768]{2,1,0:T(1,128)} %broadcast_in_dim.12.span_code), custom_call_target="tpu_custom_call" | custom-call | tf_op jit(solution)/shard_map/attention_forward/pallas_call | solution.py:187
  440.7 14.9 multiply_convert_fusion.1
  455.7 10.0 fusion.137
  466.2 4.8 fusion.25
  471.3 78.2 %fetch_window.3.window = bf16[2336,2304]{1,0:T(8,128)(2,1)S(1)} custom-call(bf16[480,2304]{1,0:T(8,128)(2,1)S(1)} %fusion.31.refs_0_), custom_call_target="tpu_custom_call" | custom-call | tf_op jit(solution)/shard_map/fetch_window/pallas_call | solution.py:411
  554.6 27.1 %attention_forward.3 = (bf16[480,1152]{1,0:T(8,128)(2,1)}, f32[480,128]{1,0:T(8,128)}) custom-call(s32[8]{0:T(128)} %stack.140.plan, bf16[480,1152]{1,0:T(8,128)(2,1)} %fusion.66.query, bf16[2336,2304]{1,0:T(8,128)(2,1)} %copy-done.1, s32[480,1]{1,0:T(8,128)} %copy.203.own_code, s32[4,1,768]{2,1,0:T(1,128)} %broadcast_in_dim.12.span_code), custom_call_target="tpu_custom_call" | custom-call | tf_op jit(solution)/shard_map/attention_forward/pallas_call | solution.py:187
  581.6 4.7 fusion.138
  586.8 17.2 %multiply_convert_fusion = (bf16[480,4352]{1,0:T(8,128)(2,1)}, f32[480,4352]{1,0:T(8,128)}) fusion(f32[4352]{0:T(1024)S(1)} %get-tuple-element.204, bf16[1152,4352]{1,0:T(8,128)(2,1)} %get-tuple-element.73, f32[480,1152]{0,1:T(8,128)S(1)} %get-tuple-element.297, f32[1152]{0:T(1024)S(1)} %get-tuple-element.193, f32[1152]{0:T(1024)S(1)} %get-tuple-element.206, ...), kind=kOutput, calls=%fused_computation.29 | convolution fusion | flops 4836618240 | bytes 24803072 | tf_op jit(solution)/shard_map/dot_general | solution.py:38
  604.0 13.2 convert_reduce_fusion
  617.2 12.2 fusion.140
  642.2 4.9 convolution_convert_fusion.1.grad
  647.1 49.9 %attention_backward.2 = (bf16[480,1152]{1,0:T(8,128)(2,1)}, bf16[2336,2304]{1,0:T(8,128)(2,1)}) custom-call(s32[8]{0:T(128)} %stack.140.plan, bf16[480,1152]{1,0:T(8,128)(2,1)} %fusion.66.query, bf16[2336,2304]{1,0:T(8,128)(2,1)} %copy-done.1, bf16[480,1152]{1,0:T(8,128)(2,1)} %convolution_convert_fusion.1.grad, f32[480,128]{1,0:T(8,128)} %get-tuple-element.75.lse_in, ...), custom_call_target="tpu_custom_call" | custom-call | tf_op jit(solution)/shard_map/attention_backward/pallas_call | solution.py:207
  697.0 4.1 copy-done.4
  701.1 97.9 %return_window.2 = bf16[480,2304]{1,0:T(8,128)(2,1)S(1)} custom-call(bf16[2336,2304]{1,0:T(8,128)(2,1)S(1)} %copy-done.4), custom_call_target="tpu_custom_call" | custom-call | tf_op jit(solution)/shard_map/return_window/pallas_call | solution.py:411
  799.0 10.1 fusion.139
  816.1 6.4 convert_reduce_fusion.4
  823.2 17.0 %convert_reduce_fusion.1 = (f32[4352]{0:T(1024)S(1)}, bf16[480,4352]{1,0:T(8,128)(2,1)}) fusion(f32[480,4352]{1,0:T(8,128)} %get-tuple-element.293, bf16[1152,4352]{1,0:T(8,128)(2,1)} %get-tuple-element.70, f32[480,1152]{0,1:T(8,128)} %get-tuple-element.238), kind=kOutput, calls=%fused_computation.28 | convolution fusion | flops 4859469824 | bytes 24790016 | tf_op jit(solution)/shard_map/dot_general | solution.py:38
  840.3 10.8 fusion.142
  853.3 4.2 multiply_reduce_fusion
  857.4 5.1 convert_reduce_fusion.5
  862.5 5.0 convolution_convert_fusion.grad
  867.5 50.3 %attention_backward.3 = (bf16[480,1152]{1,0:T(8,128)(2,1)}, bf16[2336,2304]{1,0:T(8,128)(2,1)}) custom-call(s32[8]{0:T(128)} %stack.140.plan, bf16[480,1152]{1,0:T(8,128)(2,1)} %fusion.67.query, bf16[2336,2304]{1,0:T(8,128)(2,1)} %copy-done, bf16[480,1152]{1,0:T(8,128)(2,1)} %convolution_convert_fusion.grad, f32[480,128]{1,0:T(8,128)} %get-tuple-element.78.lse_in, ...), custom_call_target="tpu_custom_call" | custom-call | tf_op jit(solution)/shard_map/attention_backward/pallas_call | solution.py:207
  917.7 4.1 copy-done.5
  921.8 92.7 %return_window.3 = (bf16[480,2304]{1,0:T(8,128)(2,1)S(1)}, f32[144,128]{1,0:T(8,128)S(1)}) custom-call(bf16[2336,2304]{1,0:T(8,128)(2,1)S(1)} %copy-done.5, f32[144,128]{1,0:T(8,128)S(1)} %pad_bitcast_fusion.refs_1_), custom_call_target="tpu_custom_call" | custom-call | tf_op jit(solution)/shard_map/return_window/pallas_call | solution.py:411
  1014.5 9.3 fusion.141
  1042.0 204.3 %reduce_gradients.2 = (f32[48,4608]{1,0:T(8,128)}, bf16[1152,480]{1,0:T(8,128)(2,1)}, bf16[1152,480]{1,0:T(8,128)(2,1)}, bf16[480,2304]{1,0:T(8,128)(2,1)}, f32[...) custom-call(bf16[1152,480]{1,0:T(8,128)(2,1)} %get-tuple-element.252, ...), custom_call_target="tpu_custom_call" | custom-call | tf_op jit(solution)/shard_map/reduce_gradients/pallas_call | solution.py:411
  1260.1 186.2 %reduce_gradients.3 = (f32[48,4608]{1,0:T(8,128)}, bf16[1152,480]{1,0:T(8,128)(2,1)}, bf16[1152,480]{1,0:T(8,128)(2,1)}, bf16[480,2304]{1,0:T(8,128)(2,1)}, f32[...) custom-call(bf16[1152,480]{1,0:T(8,128)(2,1)} %get-tuple-element.248, ...), custom_call_target="tpu_custom_call" | custom-call | tf_op jit(solution)/shard_map/reduce_gradients/pallas_call | solution.py:411
  1484.2 10.4 fusion.36
  (390 shorter events, 127.4 us)
Async XLA Ops:
  306.4 17.7 %copy-start.38 = (bf16[480,1152]{1,0:T(8,128)(2,1)S(1)}, bf16[480,1152]{1,0:T(8,128)(2,1)}, u32[]{:S(2)}) copy-start(bf16[480,1152]{1,0:T(8,128)(2,1)} %param.27) | copy-start | bytes 3317764
  323.8 117.0 %copy-start.67 = (f32[1152]{0:T(1024)}, f32[1152]{0:T(1024)S(1)}, u32[]{:S(2)}) copy-start(f32[1152]{0:T(1024)S(1)} %get-tuple-element.199) | copy-start | bytes 13828
  323.8 142.3 %copy-start.71 = (f32[1152]{0:T(1024)}, f32[1152]{0:T(1024)S(1)}, u32[]{:S(2)}) copy-start(f32[1152]{0:T(1024)S(1)} %get-tuple-element.197) | copy-start | bytes 13828
  323.8 263.0 %copy-start.69 = (f32[1152]{0:T(1024)}, f32[1152]{0:T(1024)S(1)}, u32[]{:S(2)}) copy-start(f32[1152]{0:T(1024)S(1)} %get-tuple-element.193) | copy-start | bytes 13828
  324.1 116.6 %copy-start.55 = (f32[1152]{0:T(1024)}, f32[1152]{0:T(1024)S(1)}, u32[]{:S(2)}) copy-start(f32[1152]{0:T(1024)S(1)} %get-tuple-element.208) | copy-start | bytes 13828
  325.0 110.8 %copy-start.11 = (bf16[480,1152]{0,1:T(8,128)(2,1)}, bf16[480,1152]{0,1:T(8,128)(2,1)S(1)}, u32[]{:S(2)}) copy-start(bf16[480,1152]{0,1:T(8,128)(2,1)S(1)} %copy.190) | copy-start | bytes 3317764
  439.7 16.0 %copy-start.13 = (f32[480,1152]{0,1:T(8,128)}, f32[480,1152]{0,1:T(8,128)S(1)}, u32[]{:S(2)}) copy-start(f32[480,1152]{0,1:T(8,128)S(1)} %get-tuple-element.291) | copy-start | bytes 6635524
  439.7 15.9 %copy-start.63 = (f32[480]{0:T(512)}, f32[480]{0:T(512)S(1)}, u32[]{:S(2)}) copy-start(f32[480]{0:T(512)S(1)} %broadcast_multiply_fusion.10) | copy-start | bytes 5764
  440.1 15.6 %copy-start.82 = (f32[480]{0:T(512)}, f32[480]{0:T(512)S(1)}, u32[]{:S(2)}) copy-start(f32[480]{0:T(512)S(1)} %add_rsqrt_fusion.2) | copy-start | bytes 5764
  455.7 10.5 slice-start.3
  455.7 10.4 slice-start.4
  455.7 10.4 slice-start.5
  581.6 22.4 %slice-start = ((s8[10616832]{0:T(1024)(128)(4,1)}), s8[4194304]{0:T(1024)(128)(4,1)S(1)}, s32[]{:S(2)}) async-start(s8[10616832]{0:T(1024)(128)(4,1)} %bitcast.115), calls=%async_computation | async-start | bytes 8388608
  586.4 52.0 %copy-start.7 = (f32[480,1152]{0,1:T(8,128)}, f32[480,1152]{0,1:T(8,128)S(1)}, u32[]{:S(2)}) copy-start(f32[480,1152]{0,1:T(8,128)S(1)} %get-tuple-element.297) | copy-start | bytes 6635524
  586.4 46.1 %copy-start.59 = (f32[480]{0:T(512)}, f32[480]{0:T(512)S(1)}, u32[]{:S(2)}) copy-start(f32[480]{0:T(512)S(1)} %broadcast_multiply_fusion.8) | copy-start | bytes 5764
  586.4 17.6 %slice-start.1 = ((s8[10616832]{0:T(1024)(128)(4,1)}), s8[4194304]{0:T(1024)(128)(4,1)S(1)}, s32[]{:S(2)}) async-start(s8[10616832]{0:T(1024)(128)(4,1)} %bitcast.115), calls=%async_computation.1 | async-start | bytes 8388608
  586.8 45.8 %copy-start.79 = (f32[480]{0:T(512)}, f32[480]{0:T(512)S(1)}, u32[]{:S(2)}) copy-start(f32[480]{0:T(512)S(1)} %add_rsqrt_fusion) | copy-start | bytes 5764
  586.8 17.2 %copy-start.39 = (bf16[480,1152]{1,0:T(8,128)(2,1)S(1)}, bf16[480,1152]{1,0:T(8,128)(2,1)}, u32[]{:S(2)}) copy-start(bf16[480,1152]{1,0:T(8,128)(2,1)} %param.30) | copy-start | bytes 3317764
  586.8 17.2 %slice-start.2 = ((s8[10616832]{0:T(1024)(128)(4,1)}), s8[2228224]{0:T(1024)(128)(4,1)S(1)}, s32[]{:S(2)}) async-start(s8[10616832]{0:T(1024)(128)(4,1)} %bitcast.115), calls=%async_computation.2 | async-start | bytes 4456448
  617.2 12.2 copy-start.26
  638.4 177.3 %copy-start.18 = (bf16[480,1152]{0,1:T(8,128)(2,1)}, bf16[480,1152]{0,1:T(8,128)(2,1)S(1)}, u32[]{:S(2)}) copy-start(bf16[480,1152]{0,1:T(8,128)(2,1)S(1)} %copy.209) | copy-start | bytes 3317764
  701.1 98.0 %copy-start.22 = (bf16[480,1152]{1,0:T(8,128)(2,1)S(1)}, bf16[480,1152]{1,0:T(8,128)(2,1)}, u32[]{:S(2)}) copy-start(bf16[480,1152]{1,0:T(8,128)(2,1)} %get-tuple-element.76) | copy-start | bytes 3317764
  799.0 23.6 %copy-start.2 = (bf16[480,2304]{1,0:T(8,128)(2,1)}, bf16[480,2304]{1,0:T(8,128)(2,1)S(1)}, u32[]{:S(2)}) copy-start(bf16[480,2304]{1,0:T(8,128)(2,1)S(1)} %return_window.2) | copy-start | bytes 6635524
  823.2 17.0 %copy-start.81 = (f32[4352]{0:T(1024)S(1)}, f32[4352]{0:T(1024)}, u32[]{:S(2)}) copy-start(f32[4352]{0:T(1024)} %get-tuple-element.300) | copy-start | bytes 52228
  921.8 92.7 %copy-start.24 = (bf16[480,1152]{1,0:T(8,128)(2,1)S(1)}, bf16[480,1152]{1,0:T(8,128)(2,1)}, u32[]{:S(2)}) copy-start(bf16[480,1152]{1,0:T(8,128)(2,1)} %get-tuple-element.79) | copy-start | bytes 3317764
  1042.0 205.2 %copy-start.93 = (bf16[2,6,36]{2,0,1:T(2,128)(2,1)S(1)}, bf16[2,6,36]{2,0,1:T(2,128)(2,1)}, u32[]{:S(2)}) copy-start(bf16[2,6,36]{2,0,1:T(2,128)(2,1)} %param.36) | copy-start | bytes 2596
  1042.0 205.2 %copy-start.96 = (f32[2,6,36]{2,0,1:T(2,128)S(1)}, f32[2,6,36]{2,0,1:T(2,128)}, u32[]{:S(2)}) copy-start(f32[2,6,36]{2,0,1:T(2,128)} %param.50) | copy-start | bytes 5188
  1042.0 205.2 %copy-start.97 = (f32[2,6,36]{2,0,1:T(2,128)S(1)}, f32[2,6,36]{2,0,1:T(2,128)}, u32[]{:S(2)}) copy-start(f32[2,6,36]{2,0,1:T(2,128)} %param.43) | copy-start | bytes 5188
  1042.0 205.8 %copy-start.99 = (bf16[2,2,36]{2,1,0:T(2,128)(2,1)S(1)}, bf16[2,2,36]{2,1,0:T(2,128)(2,1)}, u32[]{:S(2)}) copy-start(bf16[2,2,36]{2,1,0:T(2,128)(2,1)} %param.35) | copy-start | bytes 868
  1042.0 205.8 %copy-start.100 = (f32[2,2,36]{2,1,0:T(2,128)S(1)}, f32[2,2,36]{2,1,0:T(2,128)}, u32[]{:S(2)}) copy-start(f32[2,2,36]{2,1,0:T(2,128)} %param.49) | copy-start | bytes 1732
  1042.0 205.8 %copy-start.101 = (f32[2,2,36]{2,1,0:T(2,128)S(1)}, f32[2,2,36]{2,1,0:T(2,128)}, u32[]{:S(2)}) copy-start(f32[2,2,36]{2,1,0:T(2,128)} %param.42) | copy-start | bytes 1732
  1483.4 11.1 copy-start.54
  (77 other events, 271.8 us)

commit v3 on v2

--- a/solution.py
+++ b/solution.py
@@ -18,6 +18,8 @@
 learn_rate = 0.025
 weight_decay = 0.1
 eps_adam = 1e-08
+gelu_rate = math.sqrt(2.0 / math.pi)
+gelu_cube = 0.044715
 span_len = 768
 lane_pair = 256
 masked_score = -1e30
@@ -34,6 +36,11 @@
     return keys, values, inside
 
 
+def valid_lanes(start):
+    lanes = lax.broadcasted_iota(jnp.int32, (1, span_len), 1)
+    return (lanes >= start) & (lanes < start + IMG)
+
+
 def dot_nn(left, right):
     return lax.dot_general(left, right, (((1,), (0,)), ((), ())), preferred_element_type=jnp.float32)
 
@@ -47,21 +54,22 @@
 
 
 def attention_forward_kernel(
-    tile, left, exp_scale, plan, query, window, own_code, span_code, out, lse_out, bias, mix
+    tile, left, exp_scale, plan, query, window, own_code, out, lse_out, bias, mix
 ):
     tok, width = query.shape
     head_size = width // HEADS
 
     def one_span(tile_index, which):
-        offset = pl.multiple_of(plan[4 * tile_index + which], 16)
-        image = plan[4 * tile_index + 2 + which]
+        spot = 2 * tile_index + which
+        offset, image = pl.multiple_of(plan[0, spot], 16), plan[1, spot]
+        valid = valid_lanes(plan[2, spot])
         rows = pl.ds(pl.multiple_of(tile_index * tile, 16), tile)
         own_rows = pl.ds(pl.multiple_of(left + tile_index * tile, 16), tile)
         span = pl.ds(offset, span_len)
         code = own_code[rows, :]
         row_image = jnp.maximum(code, -code)
         mine = row_image == image
-        bias[...] = jnp.where(row_image == span_code[2 * tile_index + which], 0.0, masked_score)
+        bias[...] = jnp.where(mine & valid, 0.0, masked_score)
         self_bias = jnp.where(code < 0, 0.0, masked_score)
         lse_lane = lax.broadcasted_iota(jnp.int32, (tile, lse_out.shape[1]), 1)
 
@@ -92,7 +100,7 @@
     def one_tile(tile_index, carry):
         one_span(tile_index, 0)
 
-        @pl.when(plan[4 * tile_index + 2] != plan[4 * tile_index + 3])
+        @pl.when(plan[1, 2 * tile_index] != plan[1, 2 * tile_index + 1])
         def _():
             one_span(tile_index, 1)
 
@@ -103,7 +111,7 @@
 
 
 def attention_backward_kernel(
-    tile, left, exp_scale, plan, query, window, grad, lse_in, own_code, span_code,
+    tile, left, exp_scale, plan, query, window, grad, lse_in, own_code,
     grad_query, grad_window, bias, acc_query, acc_window,
 ):
     tok, width = query.shape
@@ -113,17 +121,16 @@
     acc_window[...] = jnp.zeros_like(acc_window)
 
     def one_span(tile_index, which):
-        offset = pl.multiple_of(plan[4 * tile_index + which], 16)
-        image = plan[4 * tile_index + 2 + which]
+        spot = 2 * tile_index + which
+        offset, image = pl.multiple_of(plan[0, spot], 16), plan[1, spot]
+        valid = valid_lanes(plan[2, spot])
         rows = pl.ds(pl.multiple_of(tile_index * tile, 16), tile)
         own_rows = pl.ds(pl.multiple_of(left + tile_index * tile, 16), tile)
         span = pl.ds(offset, span_len)
         code = own_code[rows, :]
         row_image = jnp.maximum(code, -code)
         mine = row_image == image
-        bias[...] = jnp.where(
-            mine & (span_code[2 * tile_index + which] == image), 0.0, masked_score
-        )
+        bias[...] = jnp.where(mine & valid, 0.0, masked_score)
         self_bias = jnp.where((code < 0) & mine, 0.0, masked_score)
         lse_lane = lax.broadcasted_iota(jnp.int32, (tile, lse_in.shape[1]), 1)
 
@@ -158,7 +165,7 @@
     def one_tile(tile_index, carry):
         one_span(tile_index, 0)
 
-        @pl.when(plan[4 * tile_index + 2] != plan[4 * tile_index + 3])
+        @pl.when(plan[1, 2 * tile_index] != plan[1, 2 * tile_index + 1])
         def _():
             one_span(tile_index, 1)
 
@@ -181,7 +188,7 @@
     return pl.BlockSpec(memory_space=pltpu.VMEM)
 
 
-def attention_forward(tile, left, plan, query, window, own_code, span_code):
+def attention_forward(tile, left, plan, query, window, own_code):
     tok, width = query.shape
     exp_scale = math.log2(math.e) / math.sqrt(width // HEADS)
     return pl.pallas_call(
@@ -191,17 +198,17 @@
             jax.ShapeDtypeStruct((tok, width), jnp.bfloat16),
             jax.ShapeDtypeStruct((tok, 128), jnp.float32),
         ],
-        in_specs=[pl.BlockSpec(memory_space=pltpu.SMEM)] + [in_vmem()] * 4,
+        in_specs=[pl.BlockSpec(memory_space=pltpu.SMEM)] + [in_vmem()] * 3,
         out_specs=[in_vmem()] * 2,
         scratch_shapes=[
             pltpu.VMEM((tile, span_len), jnp.float32),
             pltpu.VMEM((tok, width), jnp.float32),
         ],
         compiler_params=pltpu.CompilerParams(vmem_limit_bytes=60 * mib),
-    )(plan, query, window, own_code, span_code)
-
-
-def attention_backward(tile, left, plan, query, window, grad, lse, own_code, span_code):
+    )(plan, query, window, own_code)
+
+
+def attention_backward(tile, left, plan, query, window, grad, lse, own_code):
     tok, width = query.shape
     exp_scale = math.log2(math.e) / math.sqrt(width // HEADS)
     return pl.pallas_call(
@@ -211,7 +218,7 @@
             jax.ShapeDtypeStruct((tok, width), jnp.bfloat16),
             jax.ShapeDtypeStruct(window.shape, jnp.bfloat16),
         ],
-        in_specs=[pl.BlockSpec(memory_space=pltpu.SMEM)] + [in_vmem()] * 6,
+        in_specs=[pl.BlockSpec(memory_space=pltpu.SMEM)] + [in_vmem()] * 5,
         out_specs=[in_vmem()] * 2,
         scratch_shapes=[
             pltpu.VMEM((tile, span_len), jnp.float32),
@@ -219,31 +226,22 @@
             pltpu.VMEM(window.shape, jnp.float32),
         ],
         compiler_params=pltpu.CompilerParams(vmem_limit_bytes=62 * mib),
-    )(plan, query, window, grad, lse, own_code, span_code)
-
-
-def attention_plan(tile, left, right, own_ids, own_mask, window_ids, window_mask, place, places):
+    )(plan, query, window, grad, lse, own_code)
+
+
+def attention_plan(tile, left, right, own_ids, own_mask, window_ids, place, places):
     tok = own_ids.shape[0]
     window_len = left + tok + right
     room = jnp.minimum(window_len, left + (places - place) * tok) - span_len
     position = jnp.arange(window_len)
-    present = (position >= left - place * tok) & (position < left + (places - place) * tok)
-    floor_ids = jnp.where(position < left, -1, window_ids + 0)
-    ids = jnp.where(present, window_ids, floor_ids)
-    codes = jnp.where((window_mask > 0) & present, window_ids + 1, 0)
-    plans, spans = [], []
-    for index in range(tok // tile):
-        images = (own_ids[index * tile], own_ids[(index + 1) * tile - 1])
-        offsets = []
-        for image in images:
-            start = jnp.sum((ids < image) & (position < left + tok)).astype(jnp.int32)
-            offset = jnp.minimum(start // 16 * 16, room)
-            offsets.append(offset)
-            spans.append(lax.dynamic_slice(codes, (offset,), (span_len,)))
-        plans += offsets + [image + 1 for image in images]
-    plan = jnp.stack(plans).astype(jnp.int32)
+    ids = jnp.where(position < left - place * tok, -1, window_ids)
+    images = own_ids.reshape(tok // tile, tile)[:, :: tile - 1].reshape(-1)
+    before = (ids[None, :] < images[:, None]) & (position < left + tok)[None, :]
+    starts = jnp.sum(before.astype(jnp.int32), axis=1)
+    offsets = jnp.minimum(starts // 16 * 16, room)
+    plan = jnp.stack([offsets, images + 1, starts - offsets]).astype(jnp.int32)
     own_code = jnp.where(own_mask > 0, own_ids + 1, -(own_ids + 1)).astype(jnp.int32)[:, None]
-    return plan, own_code, jnp.stack(spans)[:, None, :].astype(jnp.int32)
+    return plan, own_code
 
 
 class Layout:
@@ -1211,31 +1209,339 @@
     )
 
 
-def column_sum(source):
-    return jnp.sum(source.astype(jnp.float32), axis=0)
-
-
-def norm_forward(source, gain_row, shift_row):
-    row_mean = jnp.mean(source, axis=-1, keepdims=True)
-    centred = source - row_mean
-    variance = jnp.mean(centred * centred, axis=-1, keepdims=True)
-    inv_scale = lax.rsqrt(variance + eps_norm)
-    unit_rows = centred * inv_scale
-    return (unit_rows * gain_row + shift_row, unit_rows, inv_scale)
-
-
-def norm_backward(gradient, unit_rows, inv_scale, gain_row):
+def lane_mean(source):
+    return jnp.mean(source, axis=1, keepdims=True)
+
+
+def unit_of(source):
+    centred = source - lane_mean(source)
+    inv_scale = lax.rsqrt(lane_mean(centred * centred) + eps_norm)
+    return centred * inv_scale, inv_scale
+
+
+def norm_input_gradient(gradient, unit_rows, inv_scale, gain_row):
     scaled = gradient * gain_row
-    grad_in = inv_scale * (
-        scaled
-        - jnp.mean(scaled, axis=-1, keepdims=True)
-        - unit_rows * jnp.mean(scaled * unit_rows, axis=-1, keepdims=True)
+    return inv_scale * (scaled - lane_mean(scaled) - unit_rows * lane_mean(scaled * unit_rows))
+
+
+def rows_sum(source):
+    return jnp.sum(source.astype(jnp.float32), axis=0, keepdims=True)
+
+
+def gelu_and_slope(source):
+    square = source * source
+    curve = jnp.tanh(gelu_rate * source * (1.0 + gelu_cube * square))
+    rise = gelu_rate * (1.0 + 3.0 * gelu_cube * square)
+    half_sum = 0.5 * (1.0 + curve)
+    return source * half_sum, half_sum + 0.5 * source * (1.0 - curve * curve) * rise
+
+
+def chunks_of(columns, lanes=768):
+    return [(first, min(lanes, columns - first)) for first in range(0, columns, lanes)]
+
+
+def moves(sources, targets, sems):
+    return [
+        pltpu.make_async_copy(source, target, sems.at[index])
+        for index, (source, target) in enumerate(zip(sources, targets))
+    ]
+
+
+def projection_forward_kernel(
+    residual, rows, weight, normed_out, inv_out, query_out, pair_out, unit_out, held, sems
+):
+    width = rows.shape[1]
+    sources = [weight.at[:, pl.ds(j * width, width)] for j in range(3)]
+    loads = moves(sources, [held.at[j] for j in range(3)], sems)
+    for load in loads:
+        load.start()
+    unit_rows, inv_scale = unit_of(residual[...].astype(jnp.float32))
+    unit_out[...] = unit_rows
+    inv_out[...] = jnp.broadcast_to(inv_scale, inv_out.shape)
+    normed = (unit_rows * rows[0:1, :] + rows[1:2, :]).astype(normed_out.dtype)
+    normed_out[...] = normed
+    loads[0].wait()
+    query_out[...] = (dot_nn(normed_out[...], held[0]) + rows[2:3, :]).astype(query_out.dtype)
+    loads[1].wait()
+    pair_out[:, :width] = dot_nn(normed_out[...], held[1]).astype(pair_out.dtype)
+    loads[2].wait()
+    values = dot_nn(normed_out[...], held[2]) + rows[3:4, :]
+    pair_out[:, width:] = values.astype(pair_out.dtype)
+
+
+def dense_call(kernel, name, ins, outs, scratch, *arrays):
+    return pl.pallas_call(
+        kernel,
+        name=name,
+        in_specs=ins,
+        out_specs=[spec for _, spec in outs],
+        out_shape=[shape for shape, _ in outs],
+        scratch_shapes=scratch,
+        compiler_params=pltpu.CompilerParams(vmem_limit_bytes=60 * mib),
+    )(*arrays)
+
+
+def kept(shape, kind=jnp.bfloat16):
+    return (jax.ShapeDtypeStruct(shape, kind), in_vmem())
+
+
+def projection_forward(residual, rows, attn_weight):
+    tok, width = residual.shape
+    return dense_call(
+        projection_forward_kernel,
+        "projection_forward",
+        [in_vmem(), in_vmem(), anywhere()],
+        [
+            kept((tok, width)),
+            kept((tok, 128), jnp.float32),
+            kept((tok, width)),
+            kept((tok, 2 * width)),
+            kept((tok, width), jnp.float32),
+        ],
+        [pltpu.VMEM((3, width, width), jnp.bfloat16), pltpu.SemaphoreType.DMA((3,))],
+        residual,
+        rows,
+        attn_weight,
     )
-    return (grad_in, jnp.sum(gradient * unit_rows, axis=0), jnp.sum(gradient, axis=0))
-
-
-def gelu_tanh(source):
-    return jax.nn.gelu(source, approximate=True)
+
+
+def whole(shape):
+    return pl.BlockSpec(shape, lambda step: (0,) * len(shape))
+
+
+def projection_backward_kernel(
+    grad_query, grad_pair, weight, unit, inv, rows, grad_mid, grad_res, sums, acc
+):
+    step = pl.program_id(0)
+    width = grad_query.shape[1]
+
+    @pl.when(step == 0)
+    def _():
+        acc[...] = dot_nt(grad_query[...], weight[...])
+
+    @pl.when(step == 1)
+    def _():
+        acc[...] += dot_nt(grad_pair[:, :width], weight[...])
+
+    @pl.when(step == 2)
+    def _():
+        gradient = acc[...] + dot_nt(grad_pair[:, width:], weight[...])
+        unit_rows = unit[...]
+        grad_res[...] = grad_mid[...] + norm_input_gradient(
+            gradient, unit_rows, inv[:, 0:1], rows[0:1, :]
+        )
+        sums[...] = jnp.zeros_like(sums)
+        sums[0:1, :] = rows_sum(gradient * unit_rows)
+        sums[1:2, :] = rows_sum(gradient)
+        sums[2:3, :] = rows_sum(grad_query[...])
+        sums[3:4, :] = rows_sum(grad_pair[:, width:])
+
+
+def projection_backward(grad_query, grad_pair, attn_weight, unit, inv, rows, grad_mid):
+    tok, width = grad_query.shape
+    return pl.pallas_call(
+        projection_backward_kernel,
+        name="projection_backward",
+        grid=(3,),
+        in_specs=[
+            whole((tok, width)),
+            whole((tok, 2 * width)),
+            pl.BlockSpec((width, width), lambda step: (0, step)),
+            whole((tok, width)),
+            whole((tok, 128)),
+            whole(rows.shape),
+            whole((tok, width)),
+        ],
+        out_specs=[whole((tok, width)), whole((8, width))],
+        out_shape=[
+            jax.ShapeDtypeStruct((tok, width), jnp.float32),
+            jax.ShapeDtypeStruct((8, width), jnp.float32),
+        ],
+        scratch_shapes=[pltpu.VMEM((tok, width), jnp.float32)],
+        compiler_params=pltpu.CompilerParams(vmem_limit_bytes=58 * mib),
+    )(grad_query, grad_pair, attn_weight, unit, inv, rows, grad_mid)
+
+
+class Stream:
+    def __init__(self, source, held, sems, chunks):
+        self.held, self.chunks = held, chunks
+        self.copies = [
+            pltpu.make_async_copy(
+                source.at[:, pl.ds(first, count)], held.at[k % 2, :, pl.ds(0, count)], sems.at[k]
+            )
+            for k, (first, count) in enumerate(chunks)
+        ]
+
+    def start(self, k):
+        if k < len(self.chunks):
+            self.copies[k].start()
+
+    def take(self, k):
+        self.copies[k].wait()
+        return self.held[k % 2, :, : self.chunks[k][1]]
+
+
+def mlp_forward_kernel(
+    chunks, attended, residual, attn_weight, rows, up_weight, up_shift, down_weight,
+    residual_out, hidden_out, inv_out, unit_out, active_out, slope_out,
+    out_held, up_held, down_held, active_held, slope_held, sems,
+):
+    width, count = rows.shape[1], len(chunks)
+    load = pltpu.make_async_copy(attn_weight.at[:, pl.ds(3 * width, width)], out_held, sems.at[4, 0])
+    load.start()
+    up = Stream(up_weight, up_held, sems.at[0], chunks)
+    down = Stream(down_weight, down_held, sems.at[1], chunks)
+    up.start(0)
+    down.start(0)
+    up.start(1)
+    load.wait()
+    middle = residual[...].astype(jnp.float32) + rows[4:5, :] + dot_nn(attended[...], out_held[...])
+    residual_out[...] = middle + rows[5:6, :]
+    unit_rows, inv_scale = unit_of(middle)
+    unit_out[...] = unit_rows
+    inv_out[...] = jnp.broadcast_to(inv_scale, inv_out.shape)
+    hidden_out[...] = (unit_rows * rows[6:7, :] + rows[7:8, :]).astype(hidden_out.dtype)
+    ahead = dot_nn(hidden_out[...], up.take(0))
+    stores = []
+    for k, (first, lanes) in enumerate(chunks):
+        now = ahead
+        columns = pl.ds(first, lanes)
+        up.start(k + 2)
+        down.start(k + 1)
+        if k + 1 < count:
+            ahead = dot_nn(hidden_out[...], up.take(k + 1))
+        value, slope = gelu_and_slope(now + up_shift[:, columns])
+        active_held[:, columns] = value.astype(active_held.dtype)
+        slope_held[:, columns] = slope.astype(slope_held.dtype)
+        for row, held, target in ((2, active_held, active_out), (3, slope_held, slope_out)):
+            store = pltpu.make_async_copy(
+                held.at[:, columns], target.at[:, columns], sems.at[row, k]
+            )
+            store.start()
+            stores.append(store)
+        residual_out[...] += dot_nt(active_held[:, columns], down.take(k))
+    for store in stores:
+        store.wait()
+
+
+def mlp_forward(attended, residual, attn_weight, rows, up_weight, up_shift, down_weight):
+    tok, width = attended.shape
+    columns = up_shift.shape[1]
+    chunks = chunks_of(columns)
+    hidden = (jax.ShapeDtypeStruct((tok, columns), jnp.bfloat16), anywhere())
+    weight_chunk = pltpu.VMEM((2, width, chunks[0][1]), jnp.bfloat16)
+    hidden_held = pltpu.VMEM((tok, columns), jnp.bfloat16)
+    return dense_call(
+        functools.partial(mlp_forward_kernel, chunks),
+        "mlp_forward",
+        [in_vmem(), in_vmem(), anywhere(), in_vmem(), anywhere(), in_vmem(), anywhere()],
+        [
+            kept((tok, width), jnp.float32),
+            kept((tok, width)),
+            kept((tok, 128), jnp.float32),
+            kept((tok, width), jnp.float32),
+            hidden,
+            hidden,
+        ],
+        [pltpu.VMEM((width, width), jnp.bfloat16)]
+        + [weight_chunk] * 2
+        + [hidden_held] * 2
+        + [pltpu.SemaphoreType.DMA((5, len(chunks)))],
+        attended,
+        residual,
+        attn_weight,
+        rows,
+        up_weight,
+        up_shift,
+        down_weight,
+    )
+
+
+def mlp_backward_kernel(
+    chunks, grad_res, down_weight, slope, up_weight, unit, inv, rows, attn_weight,
+    grad_pre, up_sum, grad_branch, grad_mid, grad_attn, grad_attended, sums,
+    out_held, up_held, down_held, pre_held, acc, sems,
+):
+    width, count = rows.shape[1], len(chunks)
+    down = Stream(down_weight, down_held, sems.at[1], chunks)
+    up = Stream(up_weight, up_held, sems.at[0], chunks)
+    down.start(0)
+    up.start(0)
+    down.start(1)
+    load = pltpu.make_async_copy(attn_weight.at[:, pl.ds(3 * width, width)], out_held, sems.at[3, 0])
+    load.start()
+    grad_branch[...] = grad_res[...].astype(grad_branch.dtype)
+    acc[...] = jnp.zeros_like(acc)
+    ahead = dot_nn(grad_branch[...], down.take(0))
+    stores = []
+    for k, (first, lanes) in enumerate(chunks):
+        now = ahead
+        columns = pl.ds(first, lanes)
+        down.start(k + 2)
+        up.start(k + 1)
+        if k + 1 < count:
+            ahead = dot_nn(grad_branch[...], down.take(k + 1))
+        low = (now * slope[:, columns].astype(jnp.float32)).astype(jnp.bfloat16)
+        pre_held[:, columns] = low
+        up_sum[:, columns] = rows_sum(low)
+        store = pltpu.make_async_copy(
+            pre_held.at[:, columns], grad_pre.at[:, columns], sems.at[2, k]
+        )
+        store.start()
+        stores.append(store)
+        acc[...] += dot_nt(pre_held[:, columns], up.take(k))
+    gradient = acc[...]
+    unit_rows = unit[...]
+    middle = grad_res[...].astype(jnp.float32) + norm_input_gradient(
+        gradient, unit_rows, inv[:, 0:1], rows[6:7, :]
+    )
+    grad_mid[...] = middle
+    grad_attn[...] = middle.astype(grad_attn.dtype)
+    load.wait()
+    grad_attended[...] = dot_nt(grad_attn[...], out_held[...]).astype(grad_attended.dtype)
+    sums[...] = jnp.zeros_like(sums)
+    sums[0:1, :] = rows_sum(gradient * unit_rows)
+    sums[1:2, :] = rows_sum(gradient)
+    sums[2:3, :] = rows_sum(grad_attn[...])
+    sums[3:4, :] = rows_sum(grad_branch[...])
+    for store in stores:
+        store.wait()
+
+
+def mlp_backward(grad_res, down_weight, slope, up_weight, unit, inv, rows, attn_weight):
+    tok, width = grad_res.shape
+    columns = slope.shape[1]
+    chunks = chunks_of(columns)
+    weight_chunk = pltpu.VMEM((2, width, chunks[0][1]), jnp.bfloat16)
+    return dense_call(
+        functools.partial(mlp_backward_kernel, chunks),
+        "mlp_backward",
+        [in_vmem(), anywhere(), in_vmem(), anywhere(), in_vmem(), in_vmem(), in_vmem(), anywhere()],
+        [
+            (jax.ShapeDtypeStruct((tok, columns), jnp.bfloat16), anywhere()),
+            kept((1, columns), jnp.float32),
+            kept((tok, width)),
+            kept((tok, width), jnp.float32),
+            kept((tok, width)),
+            kept((tok, width)),
+            kept((8, width), jnp.float32),
+        ],
+        [pltpu.VMEM((width, width), jnp.bfloat16)]
+        + [weight_chunk] * 2
+        + [
+            pltpu.VMEM((tok, columns), jnp.bfloat16),
+            pltpu.VMEM((tok, width), jnp.float32),
+            pltpu.SemaphoreType.DMA((4, len(chunks))),
+        ],
+        grad_res,
+        down_weight,
+        slope,
+        up_weight,
+        unit,
+        inv,
+        rows,
+        attn_weight,
+    )
 
 
 def adam_step(weight_now, gradient, first_old, second_old):
@@ -1306,8 +1612,7 @@
             filled(up_shard, layout.padded, up_columns),
             filled(down_shard, layout.padded, down_columns if layer else up_columns),
         ]
-    word = image_ids * 2 + (token_mask > 0).astype(jnp.int32)
-    word = jnp.broadcast_to(word[:, None], (tok, 128))
+    word = jnp.broadcast_to(image_ids[:, None], (tok, 128))
     def gather(layer, which):
         return gather_work(layout, shards[3 * layer + which], which == 1 or (which == 2 and layer == 0))
 
@@ -1326,147 +1631,137 @@
     all_rows = gathered[0][1][:, half : half + row_count].T.astype(jnp.float32)
     gains = all_rows[: 2 * layers].reshape(layers, 2, width)
     shifts = all_rows[2 * layers :].reshape(layers, 6, width)
-    up_shift = spread(up_bias.astype(jnp.float32))
-
-    plan, own_code, span_code = attention_plan(
-        tile, left, right, image_ids, token_mask, window_word // 2, window_word % 2, place, places
+    vectors = jnp.concatenate(
+        [gains[:, :1], shifts[:, :1], shifts[:, 2:], gains[:, 1:], shifts[:, 1:2]], axis=1
     )
-
-    residual = inputs.astype(jnp.float32)
+    up_shift = spread(up_bias.astype(jnp.float32))[:, None, :]
+
+    plan, own_code = attention_plan(
+        tile, left, right, image_ids, token_mask, window_word, place, places
+    )
+
+    residual = inputs
     kept_layers = []
     for layer in range(layers):
         attn_weight, up_weight, down_weight = gathered[layer]
-        down_weight = down_weight[:, :wide_columns]
-        normed, unit_one, inv_one = norm_forward(residual, gains[layer, 0], shifts[layer, 0])
-        normed_low = normed.astype(jnp.bfloat16)
-        projected = dot_nn(normed_low, attn_weight[:, : 3 * width])
-        queries = (projected[:, :width] + shifts[layer, 2]).astype(jnp.bfloat16)
-        value_shift = jnp.concatenate([jnp.zeros_like(shifts[layer, 3]), shifts[layer, 3]])
-        key_value = (projected[:, width:] + value_shift).astype(jnp.bfloat16)
+        rows = vectors[layer]
+        normed_low, inv_one, queries, key_value, unit_one = projection_forward(
+            residual, rows, attn_weight
+        )
         ((window, *_),) = exchange(
             "fetch_window", layout, [window_work(layout, reach, key_value)], [[0]], 20
         )
-        attended, lse = attention_forward(tile, left, plan, queries, window, own_code, span_code)
-        middle = (
-            residual
-            + dot_nn(attended, attn_weight[:, 3 * width : 4 * width])
-            + shifts[layer, 4]
-        )
-        hidden, unit_two, inv_two = norm_forward(middle, gains[layer, 1], shifts[layer, 1])
-        hidden_low = hidden.astype(jnp.bfloat16)
-        pre_act = dot_nn(hidden_low, up_weight[:, :wide_columns]) + up_shift[layer]
-        active = gelu_tanh(pre_act).astype(jnp.bfloat16)
-        residual = middle + dot_nt(active, down_weight) + shifts[layer, 5]
-        active = filled(active, tok, down_columns)
+        attended, lse = attention_forward(tile, left, plan, queries, window, own_code)
+        residual, hidden_low, inv_two, unit_two, active, slope = mlp_forward(
+            attended, residual, attn_weight, rows, up_weight, up_shift[layer], down_weight
+        )
         kept_layers.append(
             (window, unit_one, inv_one, normed_low, queries, lse, attended,
-             unit_two, inv_two, hidden_low, pre_act, active)
-        )
+             unit_two, inv_two, hidden_low, slope, active)
+        )
+
+    def reduce(works, turns):
+        left_operands = pltpu.VMEM((2, 2, width, tok), jnp.bfloat16)
+        right_operands = pltpu.VMEM((2, tok, max(attn_columns, up_columns) // 2), jnp.bfloat16)
+        operands = [left_operands, right_operands]
+        results = exchange("reduce_gradients", layout, works, turns, 63, operands)
+        return [result[0] for result in results]
 
     def packed(rows):
         flat = jnp.concatenate([row.reshape(-1) for row in rows])
         return jnp.pad(flat, (0, -flat.size % 1024)).reshape(-1, 128)
 
-    grad_res = cotangent.astype(jnp.float32)
+    grad_res = cotangent
     owned = [[None] * 3 for _ in range(layers)]
     row_grads = [None] * layers
     upbias_grads = [None] * layers
     for layer in reversed(range(layers)):
         (window, unit_one, inv_one, normed_low, queries, lse, attended,
-         unit_two, inv_two, hidden_low, pre_act, active) = kept_layers[layer]
+         unit_two, inv_two, hidden_low, slope, active) = kept_layers[layer]
         attn_weight, up_weight, down_weight = gathered[layer]
-        down_weight = down_weight[:, :wide_columns]
-        grad_branch = grad_res.astype(jnp.bfloat16)
-        grad_active = dot_nn(grad_branch, down_weight)
-        _, gelu_pull = jax.vjp(gelu_tanh, pre_act)
-        grad_pre = gelu_pull(grad_active)[0].astype(jnp.bfloat16)
-        upbias_grads[layer] = unspread(column_sum(grad_pre))
-        grad_hidden = dot_nt(grad_pre, up_weight[:, :wide_columns])
-        back_two, gain_two, shift_two = norm_backward(
-            grad_hidden, unit_two, inv_two, gains[layer, 1]
-        )
-        grad_mid = grad_res + back_two
-        grad_attn = grad_mid.astype(jnp.bfloat16)
-        grad_attended = dot_nt(grad_attn, attn_weight[:, 3 * width : 4 * width]).astype(
-            jnp.bfloat16
-        )
+        rows = vectors[layer]
+        grad_pre, up_sum, grad_branch, grad_mid, grad_attn, grad_attended, second_sums = (
+            mlp_backward(
+                grad_res, down_weight, slope, up_weight, unit_two, inv_two, rows, attn_weight
+            )
+        )
+        upbias_grads[layer] = unspread(up_sum[0])
         grad_query, grad_window = attention_backward(
-            tile, left, plan, queries, window, grad_attended, lse, own_code, span_code
+            tile, left, plan, queries, window, grad_attended, lse, own_code
         )
         works = [owned_work(layout, reach, grad_window)]
-        if layer == 0:
-            works.append(sum_work(layout, packed([*upbias_grads, *row_grads[1:]])))
-        (grad_key_value,), *small_sum = exchange(
-            "return_window", layout, works, [[0], [2, 4, 6, 7, 8]][: len(works)], 40
-        )
-        grad_proj = jnp.concatenate([grad_query, grad_key_value], axis=1)
-        grad_normed = dot_nt(grad_proj, attn_weight[:, : 3 * width])
-        back_one, gain_one, shift_one = norm_backward(
-            grad_normed, unit_one, inv_one, gains[layer, 0]
-        )
-        grad_res = grad_mid + back_one
+        reduce_up = reduce_work(layout, [hidden_low.T], grad_pre, True)
+        reduce_down = reduce_work(layout, [grad_branch.T], active, True)
+        if layer > 0:
+            works += [reduce_up, reduce_down]
+            results = reduce(works, [[0], [0], [1]])
+            grad_key_value, owned[layer][1], owned[layer][2] = results
+        else:
+            small = packed([*upbias_grads, *row_grads[1:]])
+            works += [waiting, reduce_up, sum_work(layout, small)]
+            results = reduce(works, [[0], [0], [1], [3, 5, 7, 8, 9]])
+            grad_key_value, owned[1][0], owned[0][1], small_sum = results
+        grad_res, first_sums = projection_backward(
+            grad_query, grad_key_value, attn_weight, unit_one, inv_one, rows, grad_mid
+        )
         row_grads[layer] = jnp.stack(
             [
-                gain_one,
-                gain_two,
-                shift_one,
-                shift_two,
-                column_sum(grad_query),
-                column_sum(grad_key_value[:, width:]),
-                column_sum(grad_attn),
-                column_sum(grad_branch),
+                first_sums[0], second_sums[0], first_sums[1], second_sums[1],
+                first_sums[2], first_sums[3], second_sums[2], second_sums[3],
             ]
         )
+        grad_proj = jnp.concatenate([grad_query, grad_key_value], axis=1)
         grad_side = filled(jnp.concatenate([grad_proj, grad_attn], axis=1), tok, attn_columns)
-        works = [
-            reduce_work(layout, [normed_low.T, attended.T], grad_side, False, 3 * width),
-            reduce_work(layout, [hidden_low.T], grad_pre, True),
-            reduce_work(layout, [grad_branch.T], active, False),
-        ]
-        turns = [[0], [1], [2]]
+        waiting = reduce_work(
+            layout, [normed_low.T, attended.T], grad_side, False, 3 * width
+        )
         if layer == 0:
-            works.append(sum_work(layout, packed(row_grads[:1])))
-            turns.append([2, 4, 6, 8, 10])
-        left_operands = pltpu.VMEM((2, 2, width, tok), jnp.bfloat16)
-        right_operands = pltpu.VMEM((2, tok, max(attn_columns, down_columns) // 2), jnp.bfloat16)
-        results = exchange(
-            "reduce_gradients", layout, works, turns, 63, [left_operands, right_operands]
-        )
-        owned[layer], row_sum = [result[0] for result in results[:3]], results[3:]
-
-    flat = small_sum[0][0].reshape(-1)
+            works = [reduce_down, waiting, sum_work(layout, packed(row_grads[:1]))]
+            owned[0][2], owned[0][0], row_sum = reduce(works, [[0], [1], [2, 4, 6, 8, 10]])
+
+    flat = small_sum.reshape(-1)
     upbias_grads = flat[: layers * hidden_width].reshape(layers, hidden_width)
     later = flat[layers * hidden_width :][: (layers - 1) * 8 * width].reshape(-1, 8, width)
-    row_sums = jnp.concatenate([row_sum[0][0].reshape(-1)[: 8 * width].reshape(1, 8, width), later])
+    row_sums = jnp.concatenate([row_sum.reshape(-1)[: 8 * width].reshape(1, 8, width), later])
     seat = lax.axis_index("dp") * places + place
     row_sums = lax.dynamic_slice_in_dim(row_sums, seat * layout.rows, layout.rows, axis=2)
 
     def stacked(part):
-        return jnp.stack([part(*owned[layer]) for layer in range(layers)])
+        return jnp.stack([part(*owned[layer]) for layer in range(layers)], axis=1)
 
     rows = layout.rows
-
     grads = (
         stacked(lambda attn, up, down: attn[:rows, : 3 * width]),
         stacked(lambda attn, up, down: attn[:rows, 3 * width : 4 * width]),
         stacked(lambda attn, up, down: unspread(up[:rows])),
-        stacked(lambda attn, up, down: unspread(down[:rows]).T),
+        stacked(lambda attn, up, down: unspread(down[:rows])),
         row_sums[:, :2],
         row_sums[:, 2:],
         upbias_grads,
     )
+    there = ((1, 0, 2), (1, 0, 2), (1, 0, 2), (2, 0, 1)) + ((0, 1, 2),) * 2 + ((0, 1),)
+    back = ((1, 0, 2), (1, 0, 2), (1, 0, 2), (1, 2, 0)) + ((0, 1, 2),) * 2 + ((0, 1),)
+
+    def turned(arrays, orders):
+        return tuple(jnp.transpose(array, order) for array, order in zip(arrays, orders))
+
     params = (w_qkv, w_out, w_up, w_down, norm_gains, bias_rows, up_bias)
     firsts = (first_qkv, first_out, first_up, first_down, first_gains, first_bias, first_upbias)
     seconds = (
         second_qkv, second_out, second_up, second_down, second_gains, second_bias, second_upbias,
     )
-    results = [adam_step(*packed) for packed in zip(params, grads, firsts, seconds)]
+    states = [turned(arrays, there) for arrays in (params, firsts, seconds)]
+    results = [
+        adam_step(param, gradient, first, second)
+        for param, gradient, first, second in zip(states[0], grads, states[1], states[2])
+    ]
+    grads = turned(grads, back)
     return (
         (residual, grad_res)
         + grads
-        + tuple(result[0] for result in results)
-        + tuple(result[1] for result in results)
-        + tuple(result[2] for result in results)
+        + turned([result[0] for result in results], back)
+        + turned([result[1] for result in results], back)
+        + turned([result[2] for result in results], back)
     )
 
 

time: 1510 us -> 1420 us (0.940)
  matrix products: 156 us -> 0 us
  Pallas kernels: 1180 us -> 1320 us
  other arithmetic: 59.3 us -> 16 us
    pallas_call x0 -> x8, Pallas kernels: none -> 162 us  [the longest x6 138 us: dense_call(): pl.pallas_call(kernel, name=name, in_specs=ins, out_specs=[spec for _, sp...]
    dot_general x16 -> x0, matrix products: 156 us -> none  [the longest x8 83.2 us: dot_nn(): lax.dot_general(left, right, (((1,), (0,)), ((), ())), preferred_element_...]
    reduce_sum x17 -> x1, other arithmetic: 35.2 us -> 0.2 us  [attention_plan(): starts = jnp.sum(before.astype(jnp.int32), axis=1)]
    pallas_call x7 -> x6, Pallas kernels: 1020 us -> 998 us  [exchange(): pl.pallas_call(kernel, name=name, out_shape=[shape for shape, _ in outs],...]
    unnamed x243 -> x127, local copies, waits for them, and re-layouts: 57.7 us -> 46.3 us
where the time goes in v3:
time: 1420 us; the launch traced here: 1410 us
  Pallas kernels  1320 us (93%)
  local copies, waits for them, and re-layouts  79.2 us (6%)
  other arithmetic  16 us (1%)
    pallas_call x6, Pallas kernels, exchange(): pl.pallas_call(kernel, name=name, out_shape=[shape for shape, _ in outs],...  998 us
    pallas_call x6, Pallas kernels, dense_call(): pl.pallas_call(kernel, name=name, in_specs=ins, out_specs=[spec for _, sp...  138 us
    pallas_call x2, Pallas kernels, attention_backward(): pl.pallas_call(functools.partial(attention_backward_kernel, tile, left, e...  99.9 us
    pallas_call x2, Pallas kernels, attention_forward(): pl.pallas_call(functools.partial(attention_forward_kernel, tile, left, ex...  56.2 us
    unnamed x127, local copies, waits for them, and re-layouts  46.3 us

profile of v3, /device:TPU:9, one launch (start us, length us, event | category | flops | bytes accessed | tf_op | source)
XLA Modules:
  0.0 1413.2 jit_solution(7221790851535785400)
XLA Ops:
  7.5 295.5 %gather_parameters.1 = (bf16[1152,4608]{1,0:T(8,128)(2,1)}, bf16[1152,4352]{1,0:T(8,128)(2,1)S(1)}, bf16[1152,4352]{1,0:T(8,128)(2,1)}, bf16[1152,4608]{1,0:T(8,...) custom-call(bf16[48,4608]{1,0:T(8,128)(2,1)S(1)} %get-tuple-element.361.refs_0_, ...), custom_call_target="tpu_custom_call" | custom-call | tf_op jit(solution)/shard_map/gather_parameters/pallas_call | solution.py:409
  303.0 3.7 copy-done.2
  308.4 10.7 projection_forward.2
  320.7 70.8 %fetch_window.2.window = bf16[2336,2304]{1,0:T(8,128)(2,1)S(1)} custom-call(bf16[480,2304]{1,0:T(8,128)(2,1)S(1)} %copy-done.3), custom_call_target="tpu_custom_call" | custom-call | tf_op jit(solution)/shard_map/fetch_window/pallas_call | solution.py:409
  391.6 4.1 copy-done
  398.1 28.1 %attention_forward.2 = (bf16[480,1152]{1,0:T(8,128)(2,1)}, f32[480,128]{1,0:T(8,128)}) custom-call(s32[3,4]{1,0:T(4,128)} %pad_add_fusion.plan, bf16[480,1152]{1,0:T(8,128)(2,1)} %get-tuple-element.110.query, bf16[2336,2304]{1,0:T(8,128)(2,1)} %copy-done, s32[480,1]{1,0:T(8,128)} %copy.235.own_code), custom_call_target="tpu_custom_call" | custom-call | tf_op jit(solution)/shard_map/attention_forward/pallas_call | solution.py:194
  427.0 28.8 %mlp_forward.2 = (f32[480,1152]{1,0:T(8,128)}, bf16[480,1152]{1,0:T(8,128)(2,1)}, f32[480,128]{1,0:T(8,128)}, f32[480,1152]{1,0:T(8,128)}, bf16[480,4352]{1,0:T(8,128)(2,1)}, /*index=5*/bf16[480,4352]{1,0:T(8,128)(2,1)}) custom-call(bf16[480,1152]{1,0:T(8,128)(2,1)} %get-tuple-element.112.attended, bf16[480,1152]{1,0:T(8,128)(2,1)} %residual.3, ...), custom_call_target="tpu_custom_call" | custom-call | tf_op jit(solution)/shard_map/mlp_forward/pallas_call | solution.py:1273
  455.8 11.1 projection_forward.3
  468.5 78.5 %fetch_window.3.window = bf16[2336,2304]{1,0:T(8,128)(2,1)S(1)} custom-call(bf16[480,2304]{1,0:T(8,128)(2,1)S(1)} %copy-done.4), custom_call_target="tpu_custom_call" | custom-call | tf_op jit(solution)/shard_map/fetch_window/pallas_call | solution.py:409
  547.0 4.0 copy-done.1
  551.0 28.2 %attention_forward.3 = (bf16[480,1152]{1,0:T(8,128)(2,1)}, f32[480,128]{1,0:T(8,128)}) custom-call(s32[3,4]{1,0:T(4,128)} %pad_add_fusion.plan, bf16[480,1152]{1,0:T(8,128)(2,1)} %get-tuple-element.116.query, bf16[2336,2304]{1,0:T(8,128)(2,1)} %copy-done.1, s32[480,1]{1,0:T(8,128)} %copy.235.own_code), custom_call_target="tpu_custom_call" | custom-call | tf_op jit(solution)/shard_map/attention_forward/pallas_call | solution.py:194
  579.1 29.0 %mlp_forward.3 = (f32[480,1152]{1,0:T(8,128)}, bf16[480,1152]{1,0:T(8,128)(2,1)}, f32[480,128]{1,0:T(8,128)}, f32[480,1152]{1,0:T(8,128)}, bf16[480,4352]{1,0:T(8,128)(2,1)}, /*index=5*/bf16[480,4352]{1,0:T(8,128)(2,1)}) custom-call(bf16[480,1152]{1,0:T(8,128)(2,1)} %get-tuple-element.118.attended, f32[480,1152]{1,0:T(8,128)} %get-tuple-element.114.residual, ...), custom_call_target="tpu_custom_call" | custom-call | tf_op jit(solution)/shard_map/mlp_forward/pallas_call | solution.py:1273
  608.2 29.2 %mlp_backward.2 = (bf16[480,4352]{1,0:T(8,128)(2,1)}, f32[1,4352]{1,0:T(1,128)}, bf16[480,1152]{1,0:T(8,128)(2,1)}, f32[480,1152]{1,0:T(8,128)}, bf16[480,1152]{...) custom-call(bf16[480,1152]{1,0:T(8,128)(2,1)} %grad_res.1, ...), custom_call_target="tpu_custom_call" | custom-call | tf_op jit(solution)/shard_map/mlp_backward/pallas_call | solution.py:1273
  637.3 50.0 %attention_backward.2 = (bf16[480,1152]{1,0:T(8,128)(2,1)}, bf16[2336,2304]{1,0:T(8,128)(2,1)}) custom-call(s32[3,4]{1,0:T(4,128)} %pad_add_fusion.plan, bf16[480,1152]{1,0:T(8,128)(2,1)} %get-tuple-element.116.query, bf16[2336,2304]{1,0:T(8,128)(2,1)} %copy-done.1, bf16[480,1152]{1,0:T(8,128)(2,1)} %get-tuple-element.125.grad, ...), custom_call_target="tpu_custom_call" | custom-call | tf_op jit(solution)/shard_map/attention_backward/pallas_call | solution.py:214
  690.6 198.9 %reduce_gradients.3 = (bf16[480,2304]{1,0:T(8,128)(2,1)}, f32[48,4352]{1,0:T(8,128)}, bf16[1152,480]{1,0:T(8,128)(2,1)}, bf16[480,2176]{1,0:T(8,128)(2,1)}, f32[...) custom-call(bf16[2336,2304]{1,0:T(8,128)(2,1)} %get-tuple-element.128.refs_0_, ...), custom_call_target="tpu_custom_call" | custom-call | tf_op jit(solution)/shard_map/reduce_gradients/pallas_call | solution.py:409
  889.6 12.3 projection_backward.2
  903.6 29.2 %mlp_backward.3 = (bf16[480,4352]{1,0:T(8,128)(2,1)}, f32[1,4352]{1,0:T(1,128)}, bf16[480,1152]{1,0:T(8,128)(2,1)}, f32[480,1152]{1,0:T(8,128)}, bf16[480,1152]{...) custom-call(f32[480,1152]{1,0:T(8,128)} %get-tuple-element.137.grad_res, ...), custom_call_target="tpu_custom_call" | custom-call | tf_op jit(solution)/shard_map/mlp_backward/pallas_call | solution.py:1273
  937.8 3.3 pad_maximum_fusion.refs_3_
  941.1 49.9 %attention_backward.3 = (bf16[480,1152]{1,0:T(8,128)(2,1)}, bf16[2336,2304]{1,0:T(8,128)(2,1)}) custom-call(s32[3,4]{1,0:T(4,128)} %pad_add_fusion.plan, bf16[480,1152]{1,0:T(8,128)(2,1)} %get-tuple-element.110.query, bf16[2336,2304]{1,0:T(8,128)(2,1)} %copy-done, bf16[480,1152]{1,0:T(8,128)(2,1)} %get-tuple-element.141.grad, ...), custom_call_target="tpu_custom_call" | custom-call | tf_op jit(solution)/shard_map/attention_backward/pallas_call | solution.py:214
  992.7 2.5 copy.241
  996.8 196.9 %reduce_gradients.4 = (bf16[480,2304]{1,0:T(8,128)(2,1)}, f32[48,4608]{1,0:T(8,128)}, bf16[1152,480]{1,0:T(8,128)(2,1)}, bf16[1152,480]{1,0:T(8,128)(2,1)}, bf16...) custom-call(bf16[2336,2304]{1,0:T(8,128)(2,1)} %get-tuple-element.14, ...), custom_call_target="tpu_custom_call" | custom-call | tf_op jit(solution)/shard_map/reduce_gradients/pallas_call | solution.py:409
  1193.7 12.0 projection_backward.3
  1210.6 3.3 pad_maximum_fusion.1.refs_4_
  1213.9 2.5 copy.244
  1219.7 157.2 %reduce_gradients.5 = (f32[48,4352]{1,0:T(8,128)}, bf16[1152,480]{1,0:T(8,128)(2,1)}, bf16[480,2176]{1,0:T(8,128)(2,1)}, f32[48,4608]{1,0:T(8,128)}, bf16[1152,4...) custom-call(bf16[1152,480]{1,0:T(8,128)(2,1)} %bitcast.180, ...), custom_call_target="tpu_custom_call" | custom-call | tf_op jit(solution)/shard_map/reduce_gradients/pallas_call | solution.py:409
  1383.3 1.7 copy.266
  1385.0 1.7 copy.271
  1386.7 1.7 copy.275
  1388.4 1.7 copy.279
  1393.9 1.7 copy.265
  1395.5 1.7 copy.270
  1398.9 1.7 copy.278
  (215 shorter events, 60.2 us)
Async XLA Ops:
  303.0 3.7 copy-start.2
  320.7 76.5 %copy-start.50 = (s32[480]{0:T(512)S(1)}, s32[480]{0:T(512)}, u32[]{:S(2)}) copy-start(s32[480]{0:T(512)} %param.29) | copy-start | bytes 5764
  391.5 4.1 copy-start
  398.1 28.1 %copy-start.34 = (bf16[2,4304]{1,0:T(2,128)(2,1)S(1)}, bf16[2,4304]{1,0:T(2,128)(2,1)}, u32[]{:S(2)}) copy-start(bf16[2,4304]{1,0:T(2,128)(2,1)} %param.37) | copy-start | bytes 51652
  547.0 4.0 copy-start.1
  637.3 50.0 %copy-start.23 = (bf16[480,1152]{1,0:T(8,128)(2,1)S(1)}, bf16[480,1152]{1,0:T(8,128)(2,1)}, u32[]{:S(2)}) copy-start(bf16[480,1152]{1,0:T(8,128)(2,1)} %get-tuple-element.131) | copy-start | bytes 3317764
  687.4 1.7 copy-start.22
  889.6 13.9 copy-start.45
  903.6 30.6 %copy-start.40 = (f32[1,4352]{1,0:T(1,128)S(1)}, f32[1,4352]{1,0:T(1,128)}, u32[]{:S(2)}) copy-start(f32[1,4352]{1,0:T(1,128)} %get-tuple-element.150) | copy-start | bytes 52228
  903.6 34.2 %copy-start.5 = (bf16[480,2304]{1,0:T(8,128)(2,1)S(1)}, bf16[480,2304]{1,0:T(8,128)(2,1)}, u32[]{:S(2)}) copy-start(bf16[480,2304]{1,0:T(8,128)(2,1)} %get-tuple-element.133.grad_pair) | copy-start | bytes 6635524
  903.6 34.2 %copy-start.9 = (bf16[480,1152]{1,0:T(8,128)(2,1)S(1)}, bf16[480,1152]{1,0:T(8,128)(2,1)}, u32[]{:S(2)}) copy-start(bf16[480,1152]{1,0:T(8,128)(2,1)} %get-tuple-element.127.grad_query) | copy-start | bytes 3317764
  941.1 49.9 %copy-start.8 = (bf16[480,1152]{1,0:T(8,128)(2,1)S(1)}, bf16[480,1152]{1,0:T(8,128)(2,1)}, u32[]{:S(2)}) copy-start(bf16[480,1152]{1,0:T(8,128)(2,1)} %get-tuple-element.118.attended) | copy-start | bytes 3317764
  992.7 2.5 copy-start.21
  1193.7 14.3 %copy-start.44 = (f32[8,1152]{1,0:T(8,128)S(1)}, f32[8,1152]{1,0:T(8,128)}, u32[]{:S(2)}) copy-start(f32[8,1152]{1,0:T(8,128)} %get-tuple-element.163) | copy-start | bytes 110596
  1193.7 16.9 %copy-start.6 = (bf16[480,2304]{1,0:T(8,128)(2,1)S(1)}, bf16[480,2304]{1,0:T(8,128)(2,1)}, u32[]{:S(2)}) copy-start(bf16[480,2304]{1,0:T(8,128)(2,1)} %get-tuple-element.153.grad_pair) | copy-start | bytes 6635524
  1193.7 16.9 %copy-start.10 = (bf16[480,1152]{1,0:T(8,128)(2,1)S(1)}, bf16[480,1152]{1,0:T(8,128)(2,1)}, u32[]{:S(2)}) copy-start(bf16[480,1152]{1,0:T(8,128)(2,1)} %get-tuple-element.143.grad_query) | copy-start | bytes 3317764
  1213.9 2.5 copy-start.7
  1216.4 1.6 copy-start.20
  1219.7 157.3 %copy-start.36 = (f32[144,128]{1,0:T(8,128)S(1)}, f32[144,128]{1,0:T(8,128)}, u32[]{:S(2)}) copy-start(f32[144,128]{1,0:T(8,128)} %get-tuple-element.171) | copy-start | bytes 221188
  1219.7 158.2 %copy-start.43 = (bf16[2,6,36]{2,0,1:T(2,128)(2,1)S(1)}, bf16[2,6,36]{2,0,1:T(2,128)(2,1)}, u32[]{:S(2)}) copy-start(bf16[2,6,36]{2,0,1:T(2,128)(2,1)} %param.36) | copy-start | bytes 2596
  1219.7 158.2 %copy-start.46 = (f32[2,6,36]{2,0,1:T(2,128)S(1)}, f32[2,6,36]{2,0,1:T(2,128)}, u32[]{:S(2)}) copy-start(f32[2,6,36]{2,0,1:T(2,128)} %param.50) | copy-start | bytes 5188
  1219.7 158.2 %copy-start.47 = (f32[2,6,36]{2,0,1:T(2,128)S(1)}, f32[2,6,36]{2,0,1:T(2,128)}, u32[]{:S(2)}) copy-start(f32[2,6,36]{2,0,1:T(2,128)} %param.43) | copy-start | bytes 5188
  1219.7 158.8 %copy-start.49 = (bf16[2,2,36]{2,1,0:T(2,128)(2,1)S(1)}, bf16[2,2,36]{2,1,0:T(2,128)(2,1)}, u32[]{:S(2)}) copy-start(bf16[2,2,36]{2,1,0:T(2,128)(2,1)} %param.35) | copy-start | bytes 868
  1219.7 158.8 %copy-start.51 = (f32[2,2,36]{2,1,0:T(2,128)S(1)}, f32[2,2,36]{2,1,0:T(2,128)}, u32[]{:S(2)}) copy-start(f32[2,2,36]{2,1,0:T(2,128)} %param.49) | copy-start | bytes 1732
  1219.7 158.8 %copy-start.52 = (f32[2,2,36]{2,1,0:T(2,128)S(1)}, f32[2,2,36]{2,1,0:T(2,128)}, u32[]{:S(2)}) copy-start(f32[2,2,36]{2,1,0:T(2,128)} %param.42) | copy-start | bytes 1732
  1380.5 1.7 copy-start.16
  1388.4 1.7 copy-start.31
  1398.9 1.7 copy-start.28
  1398.9 1.7 copy-start.27
  1398.9 1.7 copy-start.32
  1398.9 1.8 copy-start.33
  1403.7 1.8 copy-start.25
  (21 other events, 25.3 us)

commit v4 on v3

--- a/solution.py
+++ b/solution.py
@@ -4,6 +4,7 @@
 import jax
 import jax.numpy as jnp
 from jax import lax
+from jax.experimental import layout as array_layout
 from jax.experimental import pallas as pl
 from jax.experimental.pallas import tpu as pltpu
 from jax.sharding import PartitionSpec as P
@@ -95,7 +96,7 @@
             )
             return carry
 
-        lax.fori_loop(0, HEADS, one_head, 0, unroll=2)
+        lax.fori_loop(0, HEADS, one_head, 0, unroll=8)
 
     def one_tile(tile_index, carry):
         one_span(tile_index, 0)
@@ -110,67 +111,89 @@
     out[...] = mix[...].astype(out.dtype)
 
 
+def dot_fine(left, right, contract):
+    high = left.astype(jnp.bfloat16)
+    low = (left - high.astype(jnp.float32)).astype(jnp.bfloat16)
+    numbers = (contract, ((), ()))
+    product = lax.dot_general(high, right, numbers, preferred_element_type=jnp.float32)
+    return product + lax.dot_general(low, right, numbers, preferred_element_type=jnp.float32)
+
+
 def attention_backward_kernel(
-    tile, left, exp_scale, plan, query, window, grad, lse_in, own_code,
-    grad_query, grad_window, bias, acc_query, acc_window,
+    tile, left, exp_scale, plan, query, window, grad, lse_in, own_code, row_code,
+    grad_query, grad_window, bias, acc_query, acc_window, self_rows, lse_rows, inner_rows, square,
 ):
     tok, width = query.shape
     head_size = width // HEADS
     scale = 1.0 / math.sqrt(head_size)
     acc_query[...] = jnp.zeros_like(acc_query)
     acc_window[...] = jnp.zeros_like(acc_window)
+    square[...] = jnp.zeros_like(square)
+    head_of = lax.broadcasted_iota(jnp.int32, (128, width), 1) // head_size
+    spread = (head_of == lax.broadcasted_iota(jnp.int32, (128, width), 0)).astype(jnp.bfloat16)
+
+    def turned(columns):
+        square[:tile, :] = columns
+        return square[...].T[:, :tile]
 
     def one_span(tile_index, which):
         spot = 2 * tile_index + which
         offset, image = pl.multiple_of(plan[0, spot], 16), plan[1, spot]
-        valid = valid_lanes(plan[2, spot])
         rows = pl.ds(pl.multiple_of(tile_index * tile, 16), tile)
-        own_rows = pl.ds(pl.multiple_of(left + tile_index * tile, 16), tile)
         span = pl.ds(offset, span_len)
-        code = own_code[rows, :]
-        row_image = jnp.maximum(code, -code)
-        mine = row_image == image
+        code = row_code[tile_index]
+        mine = jnp.maximum(code, -code) == image
+        place = lax.broadcasted_iota(jnp.int32, (span_len, 1), 0)
+        valid = (place >= plan[2, spot]) & (place < plan[2, spot] + IMG)
         bias[...] = jnp.where(mine & valid, 0.0, masked_score)
-        self_bias = jnp.where((code < 0) & mine, 0.0, masked_score)
-        lse_lane = lax.broadcasted_iota(jnp.int32, (tile, lse_in.shape[1]), 1)
 
         def one_head(head, carry):
             lanes, value_lanes, inside = head_lanes(head, head_size, width)
             queries = jnp.where(inside, query[rows, lanes], 0)
             grads = jnp.where(inside, grad[rows, lanes], 0)
-            lse = jnp.sum(jnp.where(lse_lane == head, lse_in[rows, :], 0.0), axis=1, keepdims=True)
             keys = window[span, lanes]
-            own_key = window[own_rows, lanes].astype(jnp.float32)
-            own_value = window[own_rows, value_lanes].astype(jnp.float32)
-            queries_wide = queries.astype(jnp.float32)
-            grads_wide = grads.astype(jnp.float32)
-            prob = jnp.exp2(dot_nt(queries, keys) * exp_scale + bias[...] - lse)
-            self_score = jnp.sum(queries_wide * own_key, axis=1, keepdims=True) * exp_scale
-            self_prob = jnp.exp2(self_score + self_bias - lse)
-            grad_prob = dot_nt(grads, window[span, value_lanes])
-            self_grad = jnp.sum(grads_wide * own_value, axis=1, keepdims=True)
-            inner = jnp.sum(prob * grad_prob, axis=1, keepdims=True) + self_prob * self_grad
+            this = pl.ds(head, 1)
+            scores = dot_nt(keys, queries) * exp_scale + bias[...]
+            prob = jnp.exp2(scores - lse_rows[this, :])
+            grad_prob = dot_nt(window[span, value_lanes], grads)
+            inner = jnp.sum(prob * grad_prob, axis=0, keepdims=True) + self_rows[this, :]
+            inner_rows[this, :] = jnp.where(mine, inner, inner_rows[this, :])
             grad_scores = (prob * (grad_prob - inner)).astype(jnp.bfloat16)
-            self_grad_score = self_prob * (self_grad - inner)
-            part = dot_nn(grad_scores, keys) + self_grad_score * own_key
+            acc_window[span, lanes] += dot_nn(grad_scores, queries)
+            acc_window[span, value_lanes] += dot_nn(prob.astype(jnp.bfloat16), grads)
+            part = dot_tn(grad_scores, keys)
             acc_query[rows, lanes] += jnp.where(inside, part, 0.0)
-            acc_window[span, lanes] += dot_tn(grad_scores, queries)
-            acc_window[span, value_lanes] += dot_tn(prob.astype(jnp.bfloat16), grads)
-            acc_window[own_rows, lanes] += self_grad_score * queries_wide
-            acc_window[own_rows, value_lanes] += self_prob * grads_wide
             return carry
 
-        lax.fori_loop(0, HEADS, one_head, 0, unroll=2)
+        lax.fori_loop(0, HEADS, one_head, 0, unroll=8)
 
     def one_tile(tile_index, carry):
+        rows = pl.ds(pl.multiple_of(tile_index * tile, 16), tile)
+        own_rows = pl.ds(pl.multiple_of(left + tile_index * tile, 16), tile)
+        queries, grads = query[rows, :].astype(jnp.float32), grad[rows, :].astype(jnp.float32)
+        own_key = window[own_rows, :width].astype(jnp.float32)
+        own_value = window[own_rows, width:].astype(jnp.float32)
+        self_score = dot_fine(queries * own_key, spread, ((1,), (1,))) * exp_scale
+        self_grad = dot_fine(grads * own_value, spread, ((1,), (1,)))
+        lse = lse_in[rows, :]
+        self_prob = jnp.where(own_code[rows, :] < 0, jnp.exp2(self_score - lse), 0.0)
+        self_rows[...] = turned(self_prob * self_grad)
+        lse_rows[...] = turned(lse)
         one_span(tile_index, 0)
 
         @pl.when(plan[1, 2 * tile_index] != plan[1, 2 * tile_index + 1])
         def _():
             one_span(tile_index, 1)
 
+        inner = inner_rows[...].T
+        self_change = self_prob * (self_grad - inner[:tile, :])
+        change = dot_fine(self_change, spread, ((1,), (0,)))
+        acc_query[rows, :] += change * own_key
+        acc_window[own_rows, :width] += change * queries
+        acc_window[own_rows, width:] += dot_fine(self_prob, spread, ((1,), (0,))) * grads
         return carry
 
+    inner_rows[...] = jnp.zeros_like(inner_rows)
     lax.fori_loop(0, tok // tile, one_tile, 0)
     grad_query[...] = (acc_query[...] * scale).astype(grad_query.dtype)
     step = 16
@@ -218,15 +241,19 @@
             jax.ShapeDtypeStruct((tok, width), jnp.bfloat16),
             jax.ShapeDtypeStruct(window.shape, jnp.bfloat16),
         ],
-        in_specs=[pl.BlockSpec(memory_space=pltpu.SMEM)] + [in_vmem()] * 5,
+        in_specs=[pl.BlockSpec(memory_space=pltpu.SMEM)] + [in_vmem()] * 6,
         out_specs=[in_vmem()] * 2,
         scratch_shapes=[
-            pltpu.VMEM((tile, span_len), jnp.float32),
+            pltpu.VMEM((span_len, tile), jnp.float32),
             pltpu.VMEM((tok, width), jnp.float32),
             pltpu.VMEM(window.shape, jnp.float32),
+            pltpu.VMEM((128, tile), jnp.float32),
+            pltpu.VMEM((128, tile), jnp.float32),
+            pltpu.VMEM((128, tile), jnp.float32),
+            pltpu.VMEM((-(-tile // 128) * 128, 128), jnp.float32),
         ],
         compiler_params=pltpu.CompilerParams(vmem_limit_bytes=62 * mib),
-    )(plan, query, window, grad, lse, own_code)
+    )(plan, query, window, grad, lse, own_code, own_code.reshape(tok // tile, 1, tile))
 
 
 def attention_plan(tile, left, right, own_ids, own_mask, window_ids, place, places):
@@ -428,15 +455,16 @@
     return grouped
 
 
-def gather_work(layout, shard, one_block):
+def gather_work(layout, shard, one_block, line_last=False):
     lines, members, sides = layout.lines, layout.members, layout.sides
     width = shard.shape[1] // layout.blocks(one_block)
     spots = [("own", 0)]
     for t in range(1, lines):
         spots += [(f"below{t}", -t), (f"above{t}", t)]
     slots = [("mix", j) for j in range(1, members)]
-    slots += [(way, t) for way in ("up", "down") for t in range(lines)]
-    slots += [("cross", source) for source, _ in spots]
+    halves = (0, 1) if line_last else (0,)
+    slots += [(way, half, t) for way in ("up", "down") for half in halves for t in range(lines)]
+    slots += [("cross", source) for source, _ in (spots[:1] if line_last else spots)]
     slots += [("core", j) for j in range(1 if one_block else sides)]
     if not one_block:
         slots += [
@@ -464,6 +492,7 @@
         def present(step):
             return None if step == 0 else line >= -step if step < 0 else line < lines - step
 
+        yield
         for j in range(1, members):
             other = (member + j) % members
             desk.send(
@@ -486,33 +515,48 @@
         keep.start()
 
         def pass_on(source, what, half, where, when):
-            if half == 0:
+            if half == 0 and (source == "own" or not line_last):
                 desk.send(("cross", source), what, where, desk.at(group=1 - group), when)
             if not one_block:
                 for j in range(1, sides):
                     slot = ("side", half, source, j)
                     desk.send(slot, what, where, desk.at(side=(side + j) % sides), when)
 
+        def along(half, t, what, where, when):
+            for way, further, to in (("up", has_up, line + 1), ("down", has_down, line - 1)):
+                desk.send((way, half, t), what, where, desk.at(line=to), all_of(when, further))
+
         home = place(group, line)
-        desk.send(("up", 0), slab, home, desk.at(line=line + 1), has_up)
-        desk.send(("down", 0), slab, home, desk.at(line=line - 1), has_down)
+        along(0, 0, slab, home, None)
         pass_on("own", slab, 0, home, None)
         yield
-        for t in range(1, lines):
-            for way, name, step, further, to in (
-                ("up", "below", -t, has_up, line + 1),
-                ("down", "above", t, has_down, line - 1),
-            ):
-                when, where = present(step), place(group, line + step)
-                guarded(when, functools.partial(desk.wait, (way, t - 1), where))
-                desk.send((way, t), where, where, desk.at(line=to), all_of(when, further))
-                pass_on(f"{name}{t}", where, 0, where, when)
-            if t == 1:
-                where = place(1 - group, line)
-                desk.wait(("cross", "own"), where)
-                pass_on("own", where, 1, where, None)
+
+        def crossed():
+            where = place(1 - group, line)
+            desk.wait(("cross", "own"), where)
+            pass_on("own", where, 1, where, None)
+            if line_last:
+                along(1, 0, where, where, None)
+
+        if line_last:
+            crossed()
             yield
         for t in range(1, lines):
+            for half in halves:
+                for way, name, step, further, to in (
+                    ("up", "below", -t, has_up, line + 1),
+                    ("down", "above", t, has_down, line - 1),
+                ):
+                    when, where = present(step), place(1 - group if half else group, line + step)
+                    guarded(when, functools.partial(desk.wait, (way, half, t - 1), where))
+                    desk.send(
+                        (way, half, t), where, where, desk.at(line=to), all_of(when, further)
+                    )
+                    pass_on(f"{name}{t}", where, half, where, when)
+            if t == 1 and not line_last:
+                crossed()
+            yield
+        for t in range(1, 1 if line_last else lines):
             for name, step in ((f"below{t}", -t), (f"above{t}", t)):
                 when, where = present(step), place(1 - group, line + step)
                 guarded(when, functools.partial(desk.wait, ("cross", name), where))
@@ -612,6 +656,7 @@
         def first_of(tag, goal):
             return pl.multiple_of((group if tag else 1 - group) * near_rows + goal * slab_rows, 16)
 
+        yield
         for k, left in enumerate(left_in):
             desk.send(("left", k), left, left_land[k], partner)
         desk.send("right", right_in.at[:, away], right_land, partner)
@@ -1617,7 +1662,9 @@
         return gather_work(layout, shards[3 * layer + which], which == 1 or (which == 2 and layer == 0))
 
     gathered = [[None] * 3 for _ in range(layers)]
-    begun = [(layer, which) for layer in range(layers) for which in range(3)]
+    begun = [(0, 1), (0, 0), (0, 2)]
+    for layer in range(1, layers):
+        begun += [(layer, 0), (layer, 2), (layer, 1)]
     *results, (window_word, *_) = exchange(
         "gather_parameters",
         layout,
@@ -1745,6 +1792,16 @@
     def turned(arrays, orders):
         return tuple(jnp.transpose(array, order) for array, order in zip(arrays, orders))
 
+    def handed_out(arrays):
+        orders = ((1, 0, 2),) * 3 + ((2, 0, 1),)
+        large = [
+            array_layout.with_layout_constraint(
+                array, array_layout.Layout(major_to_minor=order)
+            )
+            for array, order in zip(arrays, orders)
+        ]
+        return tuple(large) + tuple(arrays[len(orders) :])
+
     params = (w_qkv, w_out, w_up, w_down, norm_gains, bias_rows, up_bias)
     firsts = (first_qkv, first_out, first_up, first_down, first_gains, first_bias, first_upbias)
     seconds = (
@@ -1755,13 +1812,13 @@
         adam_step(param, gradient, first, second)
         for param, gradient, first, second in zip(states[0], grads, states[1], states[2])
     ]
-    grads = turned(grads, back)
+    grads = handed_out(turned(grads, back))
     return (
         (residual, grad_res)
         + grads
-        + turned([result[0] for result in results], back)
-        + turned([result[1] for result in results], back)
-        + turned([result[2] for result in results], back)
+        + handed_out(turned([result[0] for result in results], back))
+        + handed_out(turned([result[1] for result in results], back))
+        + handed_out(turned([result[2] for result in results], back))
     )
 
 

time: 1420 us -> 1400 us (0.986)
  local copies, waits for them, and re-layouts: 79.2 us -> 58.3 us
  Pallas kernels: 1320 us -> 1300 us
  other arithmetic: 16 us -> 35.1 us
    unnamed x127 -> x97, local copies, waits for them, and re-layouts: 46.3 us -> 23.7 us
    transpose x4, other arithmetic: 3.32 us -> 22 us  [turned(): jnp.transpose(array, order)]
where the time goes in v4:
time: 1400 us; the launch traced here: 1390 us
  Pallas kernels  1300 us (93%)
  local copies, waits for them, and re-layouts  58.3 us (4%)
  other arithmetic  35.1 us (3%)
    pallas_call x6, Pallas kernels, exchange(): pl.pallas_call(kernel, name=name, out_shape=[shape for shape, _ in outs],...  987 us
    pallas_call x6, Pallas kernels, dense_call(): pl.pallas_call(kernel, name=name, in_specs=ins, out_specs=[spec for _, sp...  138 us
    pallas_call x2, Pallas kernels, attention_backward(): pl.pallas_call(functools.partial(attention_backward_kernel, tile, left, e...  94.3 us
    pallas_call x2, Pallas kernels, attention_forward(): pl.pallas_call(functools.partial(attention_forward_kernel, tile, left, ex...  53 us

profile of v4, /device:TPU:9, one launch (start us, length us, event | category | flops | bytes accessed | tf_op | source)
XLA Modules:
  0.0 1392.1 jit_solution(10579801330039484722)
XLA Ops:
  0.7 2.5 fusion.52
  11.7 288.8 %gather_parameters.1 = (bf16[1152,4352]{1,0:T(8,128)(2,1)S(1)}, bf16[1152,4608]{1,0:T(8,128)(2,1)}, bf16[1152,4352]{1,0:T(8,128)(2,1)}, bf16[1152,4608]{1,0:T(8,...) custom-call(bf16[48,4352]{1,0:T(8,128)(2,1)S(1)} %pad.61.refs_0_, ...), custom_call_target="tpu_custom_call" | custom-call | tf_op jit(solution)/shard_map/gather_parameters/pallas_call | solution.py:436
  300.5 3.8 copy-done.2
  305.9 10.7 projection_forward.2
  318.3 65.5 %fetch_window.2.window = bf16[2336,2304]{1,0:T(8,128)(2,1)S(1)} custom-call(bf16[480,2304]{1,0:T(8,128)(2,1)S(1)} %copy-done.3), custom_call_target="tpu_custom_call" | custom-call | tf_op jit(solution)/shard_map/fetch_window/pallas_call | solution.py:436
  383.8 4.1 copy-done
  390.4 26.3 %attention_forward.2 = (bf16[480,1152]{1,0:T(8,128)(2,1)}, f32[480,128]{1,0:T(8,128)}) custom-call(s32[3,4]{1,0:T(4,128)} %pad_add_fusion.plan, bf16[480,1152]{1,0:T(8,128)(2,1)} %get-tuple-element.110.query, bf16[2336,2304]{1,0:T(8,128)(2,1)} %copy-done, s32[480,1]{1,0:T(8,128)} %copy.151.own_code), custom_call_target="tpu_custom_call" | custom-call | tf_op jit(solution)/shard_map/attention_forward/pallas_call | solution.py:217
  417.5 28.7 %mlp_forward.2 = (f32[480,1152]{1,0:T(8,128)}, bf16[480,1152]{1,0:T(8,128)(2,1)}, f32[480,128]{1,0:T(8,128)}, f32[480,1152]{1,0:T(8,128)}, bf16[480,4352]{1,0:T(8,128)(2,1)}, /*index=5*/bf16[480,4352]{1,0:T(8,128)(2,1)}) custom-call(bf16[480,1152]{1,0:T(8,128)(2,1)} %get-tuple-element.112.attended, bf16[480,1152]{1,0:T(8,128)(2,1)} %residual.3, ...), custom_call_target="tpu_custom_call" | custom-call | tf_op jit(solution)/shard_map/mlp_forward/pallas_call | solution.py:1318
  446.2 11.1 projection_forward.3
  458.9 77.6 %fetch_window.3.window = bf16[2336,2304]{1,0:T(8,128)(2,1)S(1)} custom-call(bf16[480,2304]{1,0:T(8,128)(2,1)S(1)} %copy-done.4), custom_call_target="tpu_custom_call" | custom-call | tf_op jit(solution)/shard_map/fetch_window/pallas_call | solution.py:436
  536.5 3.9 copy-done.1
  540.5 26.6 %attention_forward.3 = (bf16[480,1152]{1,0:T(8,128)(2,1)}, f32[480,128]{1,0:T(8,128)}) custom-call(s32[3,4]{1,0:T(4,128)} %pad_add_fusion.plan, bf16[480,1152]{1,0:T(8,128)(2,1)} %get-tuple-element.116.query, bf16[2336,2304]{1,0:T(8,128)(2,1)} %copy-done.1, s32[480,1]{1,0:T(8,128)} %copy.151.own_code), custom_call_target="tpu_custom_call" | custom-call | tf_op jit(solution)/shard_map/attention_forward/pallas_call | solution.py:217
  567.1 29.0 %mlp_forward.3 = (f32[480,1152]{1,0:T(8,128)}, bf16[480,1152]{1,0:T(8,128)(2,1)}, f32[480,128]{1,0:T(8,128)}, f32[480,1152]{1,0:T(8,128)}, bf16[480,4352]{1,0:T(8,128)(2,1)}, /*index=5*/bf16[480,4352]{1,0:T(8,128)(2,1)}) custom-call(bf16[480,1152]{1,0:T(8,128)(2,1)} %get-tuple-element.118.attended, f32[480,1152]{1,0:T(8,128)} %get-tuple-element.114.residual, ...), custom_call_target="tpu_custom_call" | custom-call | tf_op jit(solution)/shard_map/mlp_forward/pallas_call | solution.py:1318
  596.1 29.2 %mlp_backward.2 = (bf16[480,4352]{1,0:T(8,128)(2,1)}, f32[1,4352]{1,0:T(1,128)}, bf16[480,1152]{1,0:T(8,128)(2,1)}, f32[480,1152]{1,0:T(8,128)}, bf16[480,1152]{...) custom-call(bf16[480,1152]{1,0:T(8,128)(2,1)} %grad_res.1, ...), custom_call_target="tpu_custom_call" | custom-call | tf_op jit(solution)/shard_map/mlp_backward/pallas_call | solution.py:1318
  626.0 47.3 %attention_backward.2 = (bf16[480,1152]{1,0:T(8,128)(2,1)}, bf16[2336,2304]{1,0:T(8,128)(2,1)}) custom-call(s32[3,4]{1,0:T(4,128)} %pad_add_fusion.plan, bf16[480,1152]{1,0:T(8,128)(2,1)} %get-tuple-element.116.query, bf16[2336,2304]{1,0:T(8,128)(2,1)} %copy-done.1, bf16[480,1152]{1,0:T(8,128)(2,1)} %get-tuple-element.125.grad, ...), custom_call_target="tpu_custom_call" | custom-call | tf_op jit(solution)/shard_map/attention_backward/pallas_call | solution.py:237
  673.3 1.6 copy.155
  674.9 1.6 copy.154
  676.6 205.4 %reduce_gradients.3 = (bf16[480,2304]{1,0:T(8,128)(2,1)}, f32[48,4352]{1,0:T(8,128)}, bf16[1152,480]{1,0:T(8,128)(2,1)}, bf16[480,2176]{1,0:T(8,128)(2,1)}, f32[...) custom-call(bf16[2336,2304]{1,0:T(8,128)(2,1)} %get-tuple-element.128.refs_0_, ...), custom_call_target="tpu_custom_call" | custom-call | tf_op jit(solution)/shard_map/reduce_gradients/pallas_call | solution.py:436
  881.9 12.0 projection_backward.2
  895.7 29.4 %mlp_backward.3 = (bf16[480,4352]{1,0:T(8,128)(2,1)}, f32[1,4352]{1,0:T(1,128)}, bf16[480,1152]{1,0:T(8,128)(2,1)}, f32[480,1152]{1,0:T(8,128)}, bf16[480,1152]{...) custom-call(f32[480,1152]{1,0:T(8,128)} %get-tuple-element.137.grad_res, ...), custom_call_target="tpu_custom_call" | custom-call | tf_op jit(solution)/shard_map/mlp_backward/pallas_call | solution.py:1318
  926.8 3.5 pad_maximum_fusion.refs_3_
  930.2 46.9 %attention_backward.3 = (bf16[480,1152]{1,0:T(8,128)(2,1)}, bf16[2336,2304]{1,0:T(8,128)(2,1)}) custom-call(s32[3,4]{1,0:T(4,128)} %pad_add_fusion.plan, bf16[480,1152]{1,0:T(8,128)(2,1)} %get-tuple-element.110.query, bf16[2336,2304]{1,0:T(8,128)(2,1)} %copy-done, bf16[480,1152]{1,0:T(8,128)(2,1)} %get-tuple-element.141.grad, ...), custom_call_target="tpu_custom_call" | custom-call | tf_op jit(solution)/shard_map/attention_backward/pallas_call | solution.py:237
  978.8 2.5 copy.157
  982.9 199.4 %reduce_gradients.4 = (bf16[480,2304]{1,0:T(8,128)(2,1)}, f32[48,4608]{1,0:T(8,128)}, bf16[1152,480]{1,0:T(8,128)(2,1)}, bf16[1152,480]{1,0:T(8,128)(2,1)}, bf16...) custom-call(bf16[2336,2304]{1,0:T(8,128)(2,1)} %get-tuple-element.14, ...), custom_call_target="tpu_custom_call" | custom-call | tf_op jit(solution)/shard_map/reduce_gradients/pallas_call | solution.py:436
  1182.3 12.2 projection_backward.3
  1196.9 3.5 pad_maximum_fusion.1.refs_4_
  1200.4 2.5 copy.160
  1206.1 150.4 %reduce_gradients.5 = (f32[48,4352]{1,0:T(8,128)}, bf16[1152,480]{1,0:T(8,128)(2,1)}, bf16[480,2176]{1,0:T(8,128)(2,1)}, f32[48,4608]{1,0:T(8,128)}, bf16[1152,4...) custom-call(bf16[1152,480]{1,0:T(8,128)(2,1)} %bitcast.164, ...), custom_call_target="tpu_custom_call" | custom-call | tf_op jit(solution)/shard_map/reduce_gradients/pallas_call | solution.py:436
  1362.8 6.9 fusion.3
  1372.7 7.0 fusion.5
  1380.7 2.3 fusion.25
  1384.9 5.8 fusion.8
  (201 shorter events, 42.0 us)
Async XLA Ops:
  300.5 3.8 copy-start.2
  316.7 1.6 copy-start.3
  383.8 4.1 copy-start
  387.9 1.6 copy-start.45
  390.4 26.3 %copy-start.31 = (bf16[2,4304]{1,0:T(2,128)(2,1)S(1)}, bf16[2,4304]{1,0:T(2,128)(2,1)}, u32[]{:S(2)}) copy-start(bf16[2,4304]{1,0:T(2,128)(2,1)} %param.37) | copy-start | bytes 51652
  457.3 1.6 copy-start.4
  536.5 4.0 copy-start.1
  626.0 47.3 %copy-start.21 = (bf16[480,1152]{1,0:T(8,128)(2,1)S(1)}, bf16[480,1152]{1,0:T(8,128)(2,1)}, u32[]{:S(2)}) copy-start(bf16[480,1152]{1,0:T(8,128)(2,1)} %get-tuple-element.131) | copy-start | bytes 3317764
  673.3 1.7 copy-start.20
  881.9 13.7 copy-start.41
  895.7 30.2 %copy-start.37 = (f32[1,4352]{1,0:T(1,128)S(1)}, f32[1,4352]{1,0:T(1,128)}, u32[]{:S(2)}) copy-start(f32[1,4352]{1,0:T(1,128)} %get-tuple-element.150) | copy-start | bytes 52228
  895.7 31.0 %copy-start.5 = (bf16[480,2304]{1,0:T(8,128)(2,1)S(1)}, bf16[480,2304]{1,0:T(8,128)(2,1)}, u32[]{:S(2)}) copy-start(bf16[480,2304]{1,0:T(8,128)(2,1)} %get-tuple-element.133.grad_pair) | copy-start | bytes 6635524
  930.2 46.9 %copy-start.12 = (bf16[480,1152]{1,0:T(8,128)(2,1)S(1)}, bf16[480,1152]{1,0:T(8,128)(2,1)}, u32[]{:S(2)}) copy-start(bf16[480,1152]{1,0:T(8,128)(2,1)} %get-tuple-element.118.attended) | copy-start | bytes 3317764
  978.8 2.5 copy-start.19
  1182.3 13.9 copy-start.40
  1182.3 14.6 %copy-start.6 = (bf16[480,2304]{1,0:T(8,128)(2,1)S(1)}, bf16[480,2304]{1,0:T(8,128)(2,1)}, u32[]{:S(2)}) copy-start(bf16[480,2304]{1,0:T(8,128)(2,1)} %get-tuple-element.153.grad_pair) | copy-start | bytes 6635524
  1200.4 2.5 copy-start.11
  1202.8 1.6 copy-start.18
  1206.1 150.4 %copy-start.33 = (f32[144,128]{1,0:T(8,128)S(1)}, f32[144,128]{1,0:T(8,128)}, u32[]{:S(2)}) copy-start(f32[144,128]{1,0:T(8,128)} %get-tuple-element.171) | copy-start | bytes 221188
  1206.1 151.3 %copy-start.42 = (f32[2,6,36]{2,0,1:T(2,128)S(1)}, f32[2,6,36]{2,0,1:T(2,128)}, u32[]{:S(2)}) copy-start(f32[2,6,36]{2,0,1:T(2,128)} %param.50) | copy-start | bytes 5188
  1206.1 151.3 %copy-start.43 = (f32[2,6,36]{2,0,1:T(2,128)S(1)}, f32[2,6,36]{2,0,1:T(2,128)}, u32[]{:S(2)}) copy-start(f32[2,6,36]{2,0,1:T(2,128)} %param.43) | copy-start | bytes 5188
  1206.1 151.9 %copy-start.46 = (f32[2,2,36]{2,1,0:T(2,128)S(1)}, f32[2,2,36]{2,1,0:T(2,128)}, u32[]{:S(2)}) copy-start(f32[2,2,36]{2,1,0:T(2,128)} %param.49) | copy-start | bytes 1732
  1206.1 151.9 %copy-start.47 = (f32[2,2,36]{2,1,0:T(2,128)S(1)}, f32[2,2,36]{2,1,0:T(2,128)}, u32[]{:S(2)}) copy-start(f32[2,2,36]{2,1,0:T(2,128)} %param.42) | copy-start | bytes 1732
  1361.0 1.4 copy-start.7
  1361.0 1.8 copy-start.14
  1362.8 6.9 copy-start.28
  1371.0 1.7 copy-start.17
  1372.7 7.0 copy-start.25
  1372.7 7.1 copy-start.24
  1383.5 1.4 copy-start.22
  1384.9 5.9 copy-start.34
  1384.9 5.9 copy-start.35
  (16 other events, 16.0 us)

commit v5 on v4

--- a/solution.py
+++ b/solution.py
@@ -55,10 +55,20 @@
 
 
 def attention_forward_kernel(
-    tile, left, exp_scale, plan, query, window, own_code, out, lse_out, bias, mix
+    tile, left, exp_scale, plan, query, source, own_code, out, lse_out, bias, mix, window, sems
 ):
     tok, width = query.shape
     head_size = width // HEADS
+    cut = min((HEADS // 2 - 1) * head_size // 128 * 128, width - lane_pair) + lane_pair
+    loads = []
+    for first, lanes in ((0, cut), (cut, width - cut)):
+        for shift in (0, width):
+            columns = pl.ds(first + shift, lanes)
+            load = pltpu.make_async_copy(
+                source.at[:, columns], window.at[:, columns], sems.at[len(loads)]
+            )
+            load.start()
+            loads.append(load)
 
     def one_span(tile_index, which):
         spot = 2 * tile_index + which
@@ -96,7 +106,19 @@
             )
             return carry
 
-        lax.fori_loop(0, HEADS, one_head, 0, unroll=8)
+        def one_half(half, carry):
+            for number in (0, 1):
+
+                @pl.when((tile_index == 0) & (which == 0) & (half == number))
+                def _():
+                    for load in loads[2 * number : 2 * number + 2]:
+                        load.wait()
+
+            for index in range(HEADS // 2):
+                one_head(half * (HEADS // 2) + index, 0)
+            return carry
+
+        lax.fori_loop(0, 2, one_half, 0)
 
     def one_tile(tile_index, carry):
         one_span(tile_index, 0)
@@ -120,12 +142,15 @@
 
 
 def attention_backward_kernel(
-    tile, left, exp_scale, plan, query, window, grad, lse_in, own_code, row_code,
-    grad_query, grad_window, bias, acc_query, acc_window, self_rows, lse_rows, inner_rows, square,
+    tile, left, exp_scale, plan, query, source, grad, lse_in, own_code, row_code,
+    grad_query, target, bias, acc_query, acc_window, self_rows, lse_rows, inner_rows, square,
+    window, grad_window, sems,
 ):
     tok, width = query.shape
     head_size = width // HEADS
     scale = 1.0 / math.sqrt(head_size)
+    load = pltpu.make_async_copy(source, window, sems.at[0])
+    load.start()
     acc_query[...] = jnp.zeros_like(acc_query)
     acc_window[...] = jnp.zeros_like(acc_window)
     square[...] = jnp.zeros_like(square)
@@ -194,6 +219,7 @@
         return carry
 
     inner_rows[...] = jnp.zeros_like(inner_rows)
+    load.wait()
     lax.fori_loop(0, tok // tile, one_tile, 0)
     grad_query[...] = (acc_query[...] * scale).astype(grad_query.dtype)
     step = 16
@@ -204,7 +230,16 @@
         grad_window[rows, width:] = acc_window[rows, width:].astype(grad_window.dtype)
         return carry
 
-    lax.fori_loop(0, acc_window.shape[0] // step, narrow, 0)
+    blocks, stores = acc_window.shape[0] // step, []
+    for part in range(4):
+        first, last = blocks * part // 4, blocks * (part + 1) // 4
+        lax.fori_loop(first, last, narrow, 0)
+        rows = pl.ds(first * step, (last - first) * step)
+        store = pltpu.make_async_copy(grad_window.at[rows], target.at[rows], sems.at[1 + part])
+        store.start()
+        stores.append(store)
+    for store in stores:
+        store.wait()
 
 
 def in_vmem():
@@ -221,11 +256,13 @@
             jax.ShapeDtypeStruct((tok, width), jnp.bfloat16),
             jax.ShapeDtypeStruct((tok, 128), jnp.float32),
         ],
-        in_specs=[pl.BlockSpec(memory_space=pltpu.SMEM)] + [in_vmem()] * 3,
+        in_specs=[pl.BlockSpec(memory_space=pltpu.SMEM), in_vmem(), anywhere(), in_vmem()],
         out_specs=[in_vmem()] * 2,
         scratch_shapes=[
             pltpu.VMEM((tile, span_len), jnp.float32),
             pltpu.VMEM((tok, width), jnp.float32),
+            pltpu.VMEM(window.shape, window.dtype),
+            pltpu.SemaphoreType.DMA((4,)),
         ],
         compiler_params=pltpu.CompilerParams(vmem_limit_bytes=60 * mib),
     )(plan, query, window, own_code)
@@ -241,8 +278,8 @@
             jax.ShapeDtypeStruct((tok, width), jnp.bfloat16),
             jax.ShapeDtypeStruct(window.shape, jnp.bfloat16),
         ],
-        in_specs=[pl.BlockSpec(memory_space=pltpu.SMEM)] + [in_vmem()] * 6,
-        out_specs=[in_vmem()] * 2,
+        in_specs=[pl.BlockSpec(memory_space=pltpu.SMEM), in_vmem(), anywhere()] + [in_vmem()] * 4,
+        out_specs=[in_vmem(), anywhere()],
         scratch_shapes=[
             pltpu.VMEM((span_len, tile), jnp.float32),
             pltpu.VMEM((tok, width), jnp.float32),
@@ -251,6 +288,9 @@
             pltpu.VMEM((128, tile), jnp.float32),
             pltpu.VMEM((128, tile), jnp.float32),
             pltpu.VMEM((-(-tile // 128) * 128, 128), jnp.float32),
+            pltpu.VMEM(window.shape, jnp.bfloat16),
+            pltpu.VMEM(window.shape, jnp.bfloat16),
+            pltpu.SemaphoreType.DMA((5,)),
         ],
         compiler_params=pltpu.CompilerParams(vmem_limit_bytes=62 * mib),
     )(plan, query, window, grad, lse, own_code, own_code.reshape(tok // tile, 1, tile))
@@ -1738,7 +1778,8 @@
         )
         works = [owned_work(layout, reach, grad_window)]
         reduce_up = reduce_work(layout, [hidden_low.T], grad_pre, True)
-        reduce_down = reduce_work(layout, [grad_branch.T], active, True)
+        split = 3 if layer else 6
+        reduce_down = reduce_work(layout, [grad_branch.T], active, True, split=split)
         if layer > 0:
             works += [reduce_up, reduce_down]
             results = reduce(works, [[0], [0], [1]])

time: 1400 us -> 1380 us (0.986)
  Pallas kernels: 1300 us -> 1280 us
where the time goes in v5:
time: 1380 us
  Pallas kernels  1280 us (93%)
  local copies, waits for them, and re-layouts  58.4 us (4%)
  other arithmetic  35.1 us (3%)
    pallas_call x6, Pallas kernels, exchange(): pl.pallas_call(kernel, name=name, out_shape=[shape for shape, _ in outs],...  976 us
    pallas_call x6, Pallas kernels, dense_call(): pl.pallas_call(kernel, name=name, in_specs=ins, out_specs=[spec for _, sp...  138 us
    pallas_call x2, Pallas kernels, attention_backward(): pl.pallas_call(functools.partial(attention_backward_kernel, tile, left, e...  91.4 us
    pallas_call x2, Pallas kernels, attention_forward(): pl.pallas_call(functools.partial(attention_forward_kernel, tile, left, ex...  51.9 us

profile of v5, /device:TPU:9, one launch (start us, length us, event | category | flops | bytes accessed | tf_op | source)
XLA Modules:
  0.0 1377.4 jit_solution(11406521679269630626)
XLA Ops:
  0.7 2.5 fusion.52
  11.7 288.8 %gather_parameters.1 = (bf16[1152,4352]{1,0:T(8,128)(2,1)S(1)}, bf16[1152,4608]{1,0:T(8,128)(2,1)}, bf16[1152,4352]{1,0:T(8,128)(2,1)}, bf16[1152,4608]{1,0:T(8,...) custom-call(bf16[48,4352]{1,0:T(8,128)(2,1)S(1)} %pad.61.refs_0_, ...), custom_call_target="tpu_custom_call" | custom-call | tf_op jit(solution)/shard_map/gather_parameters/pallas_call | solution.py:476
  300.5 3.8 copy-done.2
  305.9 10.7 projection_forward.2
  318.3 65.5 %fetch_window.2.source = bf16[2336,2304]{1,0:T(8,128)(2,1)S(1)} custom-call(bf16[480,2304]{1,0:T(8,128)(2,1)S(1)} %copy-done.3), custom_call_target="tpu_custom_call" | custom-call | tf_op jit(solution)/shard_map/fetch_window/pallas_call | solution.py:476
  383.8 4.1 copy-done
  390.4 26.0 %attention_forward.2 = (bf16[480,1152]{1,0:T(8,128)(2,1)}, f32[480,128]{1,0:T(8,128)}) custom-call(s32[3,4]{1,0:T(4,128)} %pad_add_fusion.plan, bf16[480,1152]{1,0:T(8,128)(2,1)} %get-tuple-element.110.query, bf16[2336,2304]{1,0:T(8,128)(2,1)} %copy-done, s32[480,1]{1,0:T(8,128)} %copy.151.own_code), custom_call_target="tpu_custom_call" | custom-call | tf_op jit(solution)/shard_map/attention_forward/pallas_call | solution.py:252
  417.1 28.7 %mlp_forward.2 = (f32[480,1152]{1,0:T(8,128)}, bf16[480,1152]{1,0:T(8,128)(2,1)}, f32[480,128]{1,0:T(8,128)}, f32[480,1152]{1,0:T(8,128)}, bf16[480,4352]{1,0:T(8,128)(2,1)}, /*index=5*/bf16[480,4352]{1,0:T(8,128)(2,1)}) custom-call(bf16[480,1152]{1,0:T(8,128)(2,1)} %get-tuple-element.112.attended, bf16[480,1152]{1,0:T(8,128)(2,1)} %residual.3, ...), custom_call_target="tpu_custom_call" | custom-call | tf_op jit(solution)/shard_map/mlp_forward/pallas_call | solution.py:1358
  445.8 11.1 projection_forward.3
  458.6 77.6 %fetch_window.3.source = bf16[2336,2304]{1,0:T(8,128)(2,1)S(1)} custom-call(bf16[480,2304]{1,0:T(8,128)(2,1)S(1)} %copy-done.4), custom_call_target="tpu_custom_call" | custom-call | tf_op jit(solution)/shard_map/fetch_window/pallas_call | solution.py:476
  536.2 3.9 copy-done.1
  540.2 26.0 %attention_forward.3 = (bf16[480,1152]{1,0:T(8,128)(2,1)}, f32[480,128]{1,0:T(8,128)}) custom-call(s32[3,4]{1,0:T(4,128)} %pad_add_fusion.plan, bf16[480,1152]{1,0:T(8,128)(2,1)} %get-tuple-element.116.query, bf16[2336,2304]{1,0:T(8,128)(2,1)} %copy-done.1, s32[480,1]{1,0:T(8,128)} %copy.151.own_code), custom_call_target="tpu_custom_call" | custom-call | tf_op jit(solution)/shard_map/attention_forward/pallas_call | solution.py:252
  566.1 29.0 %mlp_forward.3 = (f32[480,1152]{1,0:T(8,128)}, bf16[480,1152]{1,0:T(8,128)(2,1)}, f32[480,128]{1,0:T(8,128)}, f32[480,1152]{1,0:T(8,128)}, bf16[480,4352]{1,0:T(8,128)(2,1)}, /*index=5*/bf16[480,4352]{1,0:T(8,128)(2,1)}) custom-call(bf16[480,1152]{1,0:T(8,128)(2,1)} %get-tuple-element.118.attended, f32[480,1152]{1,0:T(8,128)} %get-tuple-element.114.residual, ...), custom_call_target="tpu_custom_call" | custom-call | tf_op jit(solution)/shard_map/mlp_forward/pallas_call | solution.py:1358
  595.1 29.2 %mlp_backward.2 = (bf16[480,4352]{1,0:T(8,128)(2,1)}, f32[1,4352]{1,0:T(1,128)}, bf16[480,1152]{1,0:T(8,128)(2,1)}, f32[480,1152]{1,0:T(8,128)}, bf16[480,1152]{...) custom-call(bf16[480,1152]{1,0:T(8,128)(2,1)} %grad_res.1, ...), custom_call_target="tpu_custom_call" | custom-call | tf_op jit(solution)/shard_map/mlp_backward/pallas_call | solution.py:1358
  625.0 45.9 %attention_backward.2 = (bf16[480,1152]{1,0:T(8,128)(2,1)}, bf16[2336,2304]{1,0:T(8,128)(2,1)}) custom-call(s32[3,4]{1,0:T(4,128)} %pad_add_fusion.plan, bf16[480,1152]{1,0:T(8,128)(2,1)} %get-tuple-element.116.query, bf16[2336,2304]{1,0:T(8,128)(2,1)} %copy-done.1, bf16[480,1152]{1,0:T(8,128)(2,1)} %get-tuple-element.125.grad, ...), custom_call_target="tpu_custom_call" | custom-call | tf_op jit(solution)/shard_map/attention_backward/pallas_call | solution.py:274
  670.9 1.7 copy.155
  674.2 205.5 %reduce_gradients.3 = (bf16[480,2304]{1,0:T(8,128)(2,1)}, f32[48,4352]{1,0:T(8,128)}, bf16[1152,480]{1,0:T(8,128)(2,1)}, bf16[480,2176]{1,0:T(8,128)(2,1)}, f32[...) custom-call(bf16[2336,2304]{1,0:T(8,128)(2,1)} %get-tuple-element.128.refs_0_, ...), custom_call_target="tpu_custom_call" | custom-call | tf_op jit(solution)/shard_map/reduce_gradients/pallas_call | solution.py:476
  879.7 12.0 projection_backward.2
  893.4 29.4 %mlp_backward.3 = (bf16[480,4352]{1,0:T(8,128)(2,1)}, f32[1,4352]{1,0:T(1,128)}, bf16[480,1152]{1,0:T(8,128)(2,1)}, f32[480,1152]{1,0:T(8,128)}, bf16[480,1152]{...) custom-call(f32[480,1152]{1,0:T(8,128)} %get-tuple-element.137.grad_res, ...), custom_call_target="tpu_custom_call" | custom-call | tf_op jit(solution)/shard_map/mlp_backward/pallas_call | solution.py:1358
  924.5 3.5 pad_maximum_fusion.refs_3_
  927.9 45.5 %attention_backward.3 = (bf16[480,1152]{1,0:T(8,128)(2,1)}, bf16[2336,2304]{1,0:T(8,128)(2,1)}) custom-call(s32[3,4]{1,0:T(4,128)} %pad_add_fusion.plan, bf16[480,1152]{1,0:T(8,128)(2,1)} %get-tuple-element.110.query, bf16[2336,2304]{1,0:T(8,128)(2,1)} %copy-done, bf16[480,1152]{1,0:T(8,128)(2,1)} %get-tuple-element.141.grad, ...), custom_call_target="tpu_custom_call" | custom-call | tf_op jit(solution)/shard_map/attention_backward/pallas_call | solution.py:274
  973.5 1.7 copy.158
  975.2 2.5 copy.157
  979.3 199.5 %reduce_gradients.4 = (bf16[480,2304]{1,0:T(8,128)(2,1)}, f32[48,4608]{1,0:T(8,128)}, bf16[1152,480]{1,0:T(8,128)(2,1)}, bf16[1152,480]{1,0:T(8,128)(2,1)}, bf16...) custom-call(bf16[2336,2304]{1,0:T(8,128)(2,1)} %get-tuple-element.14, ...), custom_call_target="tpu_custom_call" | custom-call | tf_op jit(solution)/shard_map/reduce_gradients/pallas_call | solution.py:476
  1178.8 12.2 projection_backward.3
  1193.3 3.5 pad_maximum_fusion.1.refs_4_
  1196.8 2.5 copy.160
  1202.6 139.2 %reduce_gradients.5 = (f32[48,4352]{1,0:T(8,128)}, bf16[1152,480]{1,0:T(8,128)(2,1)}, bf16[480,2176]{1,0:T(8,128)(2,1)}, f32[48,4608]{1,0:T(8,128)}, bf16[1152,4...) custom-call(bf16[1152,480]{1,0:T(8,128)(2,1)} %bitcast.164, ...), custom_call_target="tpu_custom_call" | custom-call | tf_op jit(solution)/shard_map/reduce_gradients/pallas_call | solution.py:476
  1348.2 6.9 fusion.3
  1358.0 7.0 fusion.5
  1366.1 2.3 fusion.25
  1370.2 5.8 fusion.8
  (201 shorter events, 42.0 us)
Async XLA Ops:
  300.5 3.8 copy-start.2
  316.7 1.6 copy-start.3
  383.8 4.1 copy-start
  387.9 1.6 copy-start.45
  390.4 26.0 %copy-start.31 = (bf16[2,4304]{1,0:T(2,128)(2,1)S(1)}, bf16[2,4304]{1,0:T(2,128)(2,1)}, u32[]{:S(2)}) copy-start(bf16[2,4304]{1,0:T(2,128)(2,1)} %param.37) | copy-start | bytes 51652
  457.0 1.6 copy-start.4
  536.2 4.0 copy-start.1
  625.0 45.9 %copy-start.21 = (bf16[480,1152]{1,0:T(8,128)(2,1)S(1)}, bf16[480,1152]{1,0:T(8,128)(2,1)}, u32[]{:S(2)}) copy-start(bf16[480,1152]{1,0:T(8,128)(2,1)} %get-tuple-element.131) | copy-start | bytes 3317764
  670.9 1.7 copy-start.20
  879.6 13.7 copy-start.41
  893.4 30.2 %copy-start.37 = (f32[1,4352]{1,0:T(1,128)S(1)}, f32[1,4352]{1,0:T(1,128)}, u32[]{:S(2)}) copy-start(f32[1,4352]{1,0:T(1,128)} %get-tuple-element.150) | copy-start | bytes 52228
  893.4 31.0 %copy-start.5 = (bf16[480,2304]{1,0:T(8,128)(2,1)S(1)}, bf16[480,2304]{1,0:T(8,128)(2,1)}, u32[]{:S(2)}) copy-start(bf16[480,2304]{1,0:T(8,128)(2,1)} %get-tuple-element.133.grad_pair) | copy-start | bytes 6635524
  927.9 45.6 %copy-start.12 = (bf16[480,1152]{1,0:T(8,128)(2,1)S(1)}, bf16[480,1152]{1,0:T(8,128)(2,1)}, u32[]{:S(2)}) copy-start(bf16[480,1152]{1,0:T(8,128)(2,1)} %get-tuple-element.118.attended) | copy-start | bytes 3317764
  975.2 2.5 copy-start.19
  1178.8 13.9 %copy-start.40 = (f32[8,1152]{1,0:T(8,128)S(1)}, f32[8,1152]{1,0:T(8,128)}, u32[]{:S(2)}) copy-start(f32[8,1152]{1,0:T(8,128)} %get-tuple-element.163) | copy-start | bytes 110596
  1178.8 14.6 %copy-start.6 = (bf16[480,2304]{1,0:T(8,128)(2,1)S(1)}, bf16[480,2304]{1,0:T(8,128)(2,1)}, u32[]{:S(2)}) copy-start(bf16[480,2304]{1,0:T(8,128)(2,1)} %get-tuple-element.153.grad_pair) | copy-start | bytes 6635524
  1196.8 2.5 copy-start.11
  1199.3 1.6 copy-start.18
  1202.6 139.3 %copy-start.33 = (f32[144,128]{1,0:T(8,128)S(1)}, f32[144,128]{1,0:T(8,128)}, u32[]{:S(2)}) copy-start(f32[144,128]{1,0:T(8,128)} %get-tuple-element.171) | copy-start | bytes 221188
  1202.6 140.2 %copy-start.42 = (f32[2,6,36]{2,0,1:T(2,128)S(1)}, f32[2,6,36]{2,0,1:T(2,128)}, u32[]{:S(2)}) copy-start(f32[2,6,36]{2,0,1:T(2,128)} %param.50) | copy-start | bytes 5188
  1202.6 140.2 %copy-start.43 = (f32[2,6,36]{2,0,1:T(2,128)S(1)}, f32[2,6,36]{2,0,1:T(2,128)}, u32[]{:S(2)}) copy-start(f32[2,6,36]{2,0,1:T(2,128)} %param.43) | copy-start | bytes 5188
  1202.6 140.8 %copy-start.46 = (f32[2,2,36]{2,1,0:T(2,128)S(1)}, f32[2,2,36]{2,1,0:T(2,128)}, u32[]{:S(2)}) copy-start(f32[2,2,36]{2,1,0:T(2,128)} %param.49) | copy-start | bytes 1732
  1202.6 140.8 %copy-start.47 = (f32[2,2,36]{2,1,0:T(2,128)S(1)}, f32[2,2,36]{2,1,0:T(2,128)}, u32[]{:S(2)}) copy-start(f32[2,2,36]{2,1,0:T(2,128)} %param.42) | copy-start | bytes 1732
  1346.3 1.4 copy-start.7
  1346.3 1.8 copy-start.14
  1348.2 6.9 copy-start.28
  1356.4 1.7 copy-start.17
  1358.0 7.0 copy-start.25
  1358.0 7.1 copy-start.24
  1368.8 1.4 copy-start.22
  1370.2 5.9 copy-start.34
  1370.2 5.9 copy-start.35
  (16 other events, 16.0 us)

commit v6 on v5

--- a/solution.py
+++ b/solution.py
@@ -934,7 +934,7 @@
         return self.first(delta) - self.tok * delta + self.left
 
 
-def parts_of(count, step=80):
+def parts_of(count, step=48):
     return [(first, min(step, count - first)) for first in range(0, count, step)]
 
 

time: 1380 us -> 1380 us (level)
  no operation moved by 1% of the time
where the time goes in v6:
time: 1380 us; the launch traced here: 1370 us
  Pallas kernels  1280 us (93%)
  local copies, waits for them, and re-layouts  58.4 us (4%)
  other arithmetic  34.9 us (3%)
    pallas_call x6, Pallas kernels, exchange(): pl.pallas_call(kernel, name=name, out_shape=[shape for shape, _ in outs],...  971 us
    pallas_call x6, Pallas kernels, dense_call(): pl.pallas_call(kernel, name=name, in_specs=ins, out_specs=[spec for _, sp...  138 us
    pallas_call x2, Pallas kernels, attention_backward(): pl.pallas_call(functools.partial(attention_backward_kernel, tile, left, e...  91.4 us
    pallas_call x2, Pallas kernels, attention_forward(): pl.pallas_call(functools.partial(attention_forward_kernel, tile, left, ex...  51.9 us

profile of v6, /device:TPU:9, one launch (start us, length us, event | category | flops | bytes accessed | tf_op | source)
XLA Modules:
  0.0 1371.9 jit_solution(8438415685043693874)
XLA Ops:
  0.7 2.5 fusion.52
  11.7 289.3 %gather_parameters.1 = (bf16[1152,4352]{1,0:T(8,128)(2,1)S(1)}, bf16[1152,4608]{1,0:T(8,128)(2,1)}, bf16[1152,4352]{1,0:T(8,128)(2,1)}, bf16[1152,4608]{1,0:T(8,...) custom-call(bf16[48,4352]{1,0:T(8,128)(2,1)S(1)} %pad.61.refs_0_, ...), custom_call_target="tpu_custom_call" | custom-call | tf_op jit(solution)/shard_map/gather_parameters/pallas_call | solution.py:476
  301.0 3.8 copy-done.2
  306.4 10.7 projection_forward.2
  318.8 64.5 %fetch_window.2.source = bf16[2336,2304]{1,0:T(8,128)(2,1)S(1)} custom-call(bf16[480,2304]{1,0:T(8,128)(2,1)S(1)} %copy-done.3), custom_call_target="tpu_custom_call" | custom-call | tf_op jit(solution)/shard_map/fetch_window/pallas_call | solution.py:476
  383.3 4.1 copy-done
  389.8 26.0 %attention_forward.2 = (bf16[480,1152]{1,0:T(8,128)(2,1)}, f32[480,128]{1,0:T(8,128)}) custom-call(s32[3,4]{1,0:T(4,128)} %pad_add_fusion.plan, bf16[480,1152]{1,0:T(8,128)(2,1)} %get-tuple-element.110.query, bf16[2336,2304]{1,0:T(8,128)(2,1)} %copy-done, s32[480,1]{1,0:T(8,128)} %copy.151.own_code), custom_call_target="tpu_custom_call" | custom-call | tf_op jit(solution)/shard_map/attention_forward/pallas_call | solution.py:252
  416.6 28.7 %mlp_forward.2 = (f32[480,1152]{1,0:T(8,128)}, bf16[480,1152]{1,0:T(8,128)(2,1)}, f32[480,128]{1,0:T(8,128)}, f32[480,1152]{1,0:T(8,128)}, bf16[480,4352]{1,0:T(8,128)(2,1)}, /*index=5*/bf16[480,4352]{1,0:T(8,128)(2,1)}) custom-call(bf16[480,1152]{1,0:T(8,128)(2,1)} %get-tuple-element.112.attended, bf16[480,1152]{1,0:T(8,128)(2,1)} %residual.3, ...), custom_call_target="tpu_custom_call" | custom-call | tf_op jit(solution)/shard_map/mlp_forward/pallas_call | solution.py:1358
  445.3 11.1 projection_forward.3
  458.0 76.6 %fetch_window.3.source = bf16[2336,2304]{1,0:T(8,128)(2,1)S(1)} custom-call(bf16[480,2304]{1,0:T(8,128)(2,1)S(1)} %copy-done.4), custom_call_target="tpu_custom_call" | custom-call | tf_op jit(solution)/shard_map/fetch_window/pallas_call | solution.py:476
  534.7 3.9 copy-done.1
  538.6 26.0 %attention_forward.3 = (bf16[480,1152]{1,0:T(8,128)(2,1)}, f32[480,128]{1,0:T(8,128)}) custom-call(s32[3,4]{1,0:T(4,128)} %pad_add_fusion.plan, bf16[480,1152]{1,0:T(8,128)(2,1)} %get-tuple-element.116.query, bf16[2336,2304]{1,0:T(8,128)(2,1)} %copy-done.1, s32[480,1]{1,0:T(8,128)} %copy.151.own_code), custom_call_target="tpu_custom_call" | custom-call | tf_op jit(solution)/shard_map/attention_forward/pallas_call | solution.py:252
  564.6 29.0 %mlp_forward.3 = (f32[480,1152]{1,0:T(8,128)}, bf16[480,1152]{1,0:T(8,128)(2,1)}, f32[480,128]{1,0:T(8,128)}, f32[480,1152]{1,0:T(8,128)}, bf16[480,4352]{1,0:T(8,128)(2,1)}, /*index=5*/bf16[480,4352]{1,0:T(8,128)(2,1)}) custom-call(bf16[480,1152]{1,0:T(8,128)(2,1)} %get-tuple-element.118.attended, f32[480,1152]{1,0:T(8,128)} %get-tuple-element.114.residual, ...), custom_call_target="tpu_custom_call" | custom-call | tf_op jit(solution)/shard_map/mlp_forward/pallas_call | solution.py:1358
  593.6 29.2 %mlp_backward.2 = (bf16[480,4352]{1,0:T(8,128)(2,1)}, f32[1,4352]{1,0:T(1,128)}, bf16[480,1152]{1,0:T(8,128)(2,1)}, f32[480,1152]{1,0:T(8,128)}, bf16[480,1152]{...) custom-call(bf16[480,1152]{1,0:T(8,128)(2,1)} %grad_res.1, ...), custom_call_target="tpu_custom_call" | custom-call | tf_op jit(solution)/shard_map/mlp_backward/pallas_call | solution.py:1358
  623.4 45.9 %attention_backward.2 = (bf16[480,1152]{1,0:T(8,128)(2,1)}, bf16[2336,2304]{1,0:T(8,128)(2,1)}) custom-call(s32[3,4]{1,0:T(4,128)} %pad_add_fusion.plan, bf16[480,1152]{1,0:T(8,128)(2,1)} %get-tuple-element.116.query, bf16[2336,2304]{1,0:T(8,128)(2,1)} %copy-done.1, bf16[480,1152]{1,0:T(8,128)(2,1)} %get-tuple-element.125.grad, ...), custom_call_target="tpu_custom_call" | custom-call | tf_op jit(solution)/shard_map/attention_backward/pallas_call | solution.py:274
  669.3 1.7 copy.155
  672.6 204.8 %reduce_gradients.3 = (bf16[480,2304]{1,0:T(8,128)(2,1)}, f32[48,4352]{1,0:T(8,128)}, bf16[1152,480]{1,0:T(8,128)(2,1)}, bf16[480,2176]{1,0:T(8,128)(2,1)}, f32[...) custom-call(bf16[2336,2304]{1,0:T(8,128)(2,1)} %get-tuple-element.128.refs_0_, ...), custom_call_target="tpu_custom_call" | custom-call | tf_op jit(solution)/shard_map/reduce_gradients/pallas_call | solution.py:476
  877.4 12.0 projection_backward.2
  891.2 29.4 %mlp_backward.3 = (bf16[480,4352]{1,0:T(8,128)(2,1)}, f32[1,4352]{1,0:T(1,128)}, bf16[480,1152]{1,0:T(8,128)(2,1)}, f32[480,1152]{1,0:T(8,128)}, bf16[480,1152]{...) custom-call(f32[480,1152]{1,0:T(8,128)} %get-tuple-element.137.grad_res, ...), custom_call_target="tpu_custom_call" | custom-call | tf_op jit(solution)/shard_map/mlp_backward/pallas_call | solution.py:1358
  922.2 3.5 pad_maximum_fusion.refs_3_
  925.7 45.5 %attention_backward.3 = (bf16[480,1152]{1,0:T(8,128)(2,1)}, bf16[2336,2304]{1,0:T(8,128)(2,1)}) custom-call(s32[3,4]{1,0:T(4,128)} %pad_add_fusion.plan, bf16[480,1152]{1,0:T(8,128)(2,1)} %get-tuple-element.110.query, bf16[2336,2304]{1,0:T(8,128)(2,1)} %copy-done, bf16[480,1152]{1,0:T(8,128)(2,1)} %get-tuple-element.141.grad, ...), custom_call_target="tpu_custom_call" | custom-call | tf_op jit(solution)/shard_map/attention_backward/pallas_call | solution.py:274
  971.2 1.7 copy.158
  972.9 2.5 copy.157
  977.0 196.2 %reduce_gradients.4 = (bf16[480,2304]{1,0:T(8,128)(2,1)}, f32[48,4608]{1,0:T(8,128)}, bf16[1152,480]{1,0:T(8,128)(2,1)}, bf16[1152,480]{1,0:T(8,128)(2,1)}, bf16...) custom-call(bf16[2336,2304]{1,0:T(8,128)(2,1)} %get-tuple-element.14, ...), custom_call_target="tpu_custom_call" | custom-call | tf_op jit(solution)/shard_map/reduce_gradients/pallas_call | solution.py:476
  1173.2 12.2 projection_backward.3
  1187.7 3.5 pad_maximum_fusion.1.refs_4_
  1191.2 2.5 copy.160
  1197.0 139.8 %reduce_gradients.5 = (f32[48,4352]{1,0:T(8,128)}, bf16[1152,480]{1,0:T(8,128)(2,1)}, bf16[480,2176]{1,0:T(8,128)(2,1)}, f32[48,4608]{1,0:T(8,128)}, bf16[1152,4...) custom-call(bf16[1152,480]{1,0:T(8,128)(2,1)} %bitcast.164, ...), custom_call_target="tpu_custom_call" | custom-call | tf_op jit(solution)/shard_map/reduce_gradients/pallas_call | solution.py:476
  1343.1 6.9 fusion.3
  1352.9 7.0 fusion.5
  1361.0 2.3 fusion.25
  1365.1 5.7 fusion.8
  (201 shorter events, 42.0 us)
Async XLA Ops:
  301.0 3.8 copy-start.2
  317.1 1.6 copy-start.3
  383.3 4.1 copy-start
  387.3 1.6 copy-start.45
  389.8 26.0 %copy-start.31 = (bf16[2,4304]{1,0:T(2,128)(2,1)S(1)}, bf16[2,4304]{1,0:T(2,128)(2,1)}, u32[]{:S(2)}) copy-start(bf16[2,4304]{1,0:T(2,128)(2,1)} %param.37) | copy-start | bytes 51652
  456.4 1.6 copy-start.4
  534.6 4.0 copy-start.1
  623.4 45.9 %copy-start.21 = (bf16[480,1152]{1,0:T(8,128)(2,1)S(1)}, bf16[480,1152]{1,0:T(8,128)(2,1)}, u32[]{:S(2)}) copy-start(bf16[480,1152]{1,0:T(8,128)(2,1)} %get-tuple-element.131) | copy-start | bytes 3317764
  669.3 1.7 copy-start.20
  877.4 13.7 copy-start.41
  891.2 30.2 %copy-start.37 = (f32[1,4352]{1,0:T(1,128)S(1)}, f32[1,4352]{1,0:T(1,128)}, u32[]{:S(2)}) copy-start(f32[1,4352]{1,0:T(1,128)} %get-tuple-element.150) | copy-start | bytes 52228
  891.2 31.0 %copy-start.5 = (bf16[480,2304]{1,0:T(8,128)(2,1)S(1)}, bf16[480,2304]{1,0:T(8,128)(2,1)}, u32[]{:S(2)}) copy-start(bf16[480,2304]{1,0:T(8,128)(2,1)} %get-tuple-element.133.grad_pair) | copy-start | bytes 6635524
  925.7 45.6 %copy-start.12 = (bf16[480,1152]{1,0:T(8,128)(2,1)S(1)}, bf16[480,1152]{1,0:T(8,128)(2,1)}, u32[]{:S(2)}) copy-start(bf16[480,1152]{1,0:T(8,128)(2,1)} %get-tuple-element.118.attended) | copy-start | bytes 3317764
  972.9 2.5 copy-start.19
  1173.2 13.9 %copy-start.40 = (f32[8,1152]{1,0:T(8,128)S(1)}, f32[8,1152]{1,0:T(8,128)}, u32[]{:S(2)}) copy-start(f32[8,1152]{1,0:T(8,128)} %get-tuple-element.163) | copy-start | bytes 110596
  1173.2 14.6 %copy-start.6 = (bf16[480,2304]{1,0:T(8,128)(2,1)S(1)}, bf16[480,2304]{1,0:T(8,128)(2,1)}, u32[]{:S(2)}) copy-start(bf16[480,2304]{1,0:T(8,128)(2,1)} %get-tuple-element.153.grad_pair) | copy-start | bytes 6635524
  1191.2 2.5 copy-start.11
  1193.7 1.6 copy-start.18
  1197.0 139.8 %copy-start.33 = (f32[144,128]{1,0:T(8,128)S(1)}, f32[144,128]{1,0:T(8,128)}, u32[]{:S(2)}) copy-start(f32[144,128]{1,0:T(8,128)} %get-tuple-element.171) | copy-start | bytes 221188
  1197.0 140.7 %copy-start.42 = (f32[2,6,36]{2,0,1:T(2,128)S(1)}, f32[2,6,36]{2,0,1:T(2,128)}, u32[]{:S(2)}) copy-start(f32[2,6,36]{2,0,1:T(2,128)} %param.50) | copy-start | bytes 5188
  1197.0 140.7 %copy-start.43 = (f32[2,6,36]{2,0,1:T(2,128)S(1)}, f32[2,6,36]{2,0,1:T(2,128)}, u32[]{:S(2)}) copy-start(f32[2,6,36]{2,0,1:T(2,128)} %param.43) | copy-start | bytes 5188
  1197.0 141.3 %copy-start.46 = (f32[2,2,36]{2,1,0:T(2,128)S(1)}, f32[2,2,36]{2,1,0:T(2,128)}, u32[]{:S(2)}) copy-start(f32[2,2,36]{2,1,0:T(2,128)} %param.49) | copy-start | bytes 1732
  1197.0 141.3 %copy-start.47 = (f32[2,2,36]{2,1,0:T(2,128)S(1)}, f32[2,2,36]{2,1,0:T(2,128)}, u32[]{:S(2)}) copy-start(f32[2,2,36]{2,1,0:T(2,128)} %param.42) | copy-start | bytes 1732
  1341.2 1.4 copy-start.7
  1341.2 1.8 copy-start.14
  1343.1 6.9 copy-start.28
  1351.3 1.7 copy-start.17
  1352.9 7.0 copy-start.25
  1352.9 7.1 copy-start.24
  1363.7 1.4 copy-start.22
  1365.1 5.8 copy-start.34
  1365.1 5.8 copy-start.35
  (16 other events, 16.0 us)
